TPU v7x, 32 devices: a whole 2x2x4 slice. The times are simulated.
32 devices in a mesh: groups: 2 (over x), tgt: 8 (over z, y), tile: 2 (over core).
Axes of the slice: x: 2, y: 2, z: 4, core: 2. Of those that a mesh axis runs over, the one named last changes fastest.
Arguments:
- embeddings: bfloat16 [53248, 1024], P(('groups', 'tile'), 'tgt'), parts along dimension 0, may hold values from -6 to 6
- land_mask: int32 [53248], P(('groups', 'tile')), parts along dimension 0, may hold values from 0 to 1, as said below
- factor_in: bfloat16 [1024, 256], P('tgt'), may hold values from -0.1875 to 0.1875
- factor_out: bfloat16 [256, 4096], P(None, 'tgt'), may hold values from -0.375 to 0.375
- targets: bfloat16 [53248, 4096], P(('groups', 'tile'), 'tgt'), parts along dimension 0, may hold values from -6 to 6
- target_weight: float32 [4096], P('tgt'), may hold values from 64 to 256
Outputs:
- grad_in: float32 [2048, 256], P(('groups', 'tgt'), 'tile'), parts along dimension 0
- grad_out: float32 [512, 4096], P(('groups', 'tile'), 'tgt'), parts along dimension 0
There are 2 independent parts, one for each index of `groups`. A program takes and returns all parts, laid end to end along the dimension named above; an argument that names none is the same for every part. Nothing has to cross between parts.
Inputs may be any that keep to these rules, and one draw needn't show every extreme that they name: `land_mask`: 1 marks a land cell.
All inputs are finite; a program needn't handle non-finite values.
Results may differ from a plain program's by a relative error of at most 0.0012.
Values may be sent and summed in bfloat16 or wider, within the bound.
No kernel may reach another device: no remote copies, remote signals or barrier semaphores. Data moves between devices by JAX's collectives and lax.ppermute only.
A program may use at most 128 MiB of HBM per device.

v0:
```python
import jax
import jax.numpy as jnp
from jax import lax
from jax.sharding import PartitionSpec as P


def local(embeddings, land_mask, factor_in, factor_out, targets, target_weight):
    latent_terms = jnp.dot(embeddings, factor_in, preferred_element_type=jnp.float32)
    latent_part = lax.psum_scatter(latent_terms, "tgt", scatter_dimension=0, tiled=True).astype(
        jnp.bfloat16
    )
    latent = lax.all_gather(latent_part, "tgt", axis=0, tiled=True)
    predicted = jnp.dot(latent, factor_out, preferred_element_type=jnp.float32)
    local_count = jnp.sum(land_mask).astype(jnp.float32)
    land_total = lax.psum(local_count, "tile")
    cell_weight = land_mask.astype(jnp.float32) / land_total
    residual = (
        (predicted - targets.astype(jnp.float32)) * cell_weight[:, None] * target_weight[None, :]
    ).astype(jnp.bfloat16)
    out_partial = jnp.einsum("pr,pk->rk", latent, residual, preferred_element_type=jnp.float32)
    grad_out = lax.psum_scatter(out_partial, "tile", scatter_dimension=0, tiled=True)
    grad_terms = jnp.einsum("pk,rk->pr", residual, factor_out, preferred_element_type=jnp.float32)
    grad_rows = lax.psum_scatter(grad_terms, "tgt", scatter_dimension=0, tiled=True).astype(
        jnp.bfloat16
    )
    latent_grad = lax.all_gather(grad_rows, "tgt", axis=0, tiled=True)
    in_partial = jnp.einsum(
        "pe,pr->er", embeddings, latent_grad, preferred_element_type=jnp.float32
    )
    grad_in = lax.psum_scatter(in_partial, "tile", scatter_dimension=1, tiled=True)
    return (grad_in, grad_out)


def solution(mesh):
    return jax.shard_map(
        local,
        mesh=mesh,
        in_specs=(
            P(("groups", "tile"), "tgt"),
            P(("groups", "tile")),
            P("tgt", None),
            P(None, "tgt"),
            P(("groups", "tile"), "tgt"),
            P("tgt"),
        ),
        out_specs=(P(("groups", "tgt"), "tile"), P(("groups", "tile"), "tgt")),
        check_vma=False,
    )
```

profile of v0, /device:TPU:0, one launch (start us, length us, event | category | flops | bytes accessed | tf_op | source)
XLA Modules:
  0.0 732.8 jit_solution(9744261232821557768)
XLA Ops:
  7.2 0.0 reduce-scatter.5.cloned.1.call-start
  7.2 1.9 copy-done
  9.1 7.6 %fusion = f32[13312,256]{1,0:T(8,128)} fusion(bf16[13312,128]{1,0:T(8,128)(2,1)S(1)} %copy-done, bf16[128,256]{1,0:T(8,128)(2,1)} %param.8), kind=kOutput, calls=%fused_computation.3 | convolution fusion | flops 872415232 | bytes 17104896 | tf_op jit(solution)/shard_map/dot_general | solution.py:8
  16.8 0.0 all-gather.3.cloned.1.call-start
  16.9 224.6 %reduce-scatter.5.cloned.1.call-done = f32[1664,256]{1,0:T(8,128)} async-done(((f32[13312,256]{1,0:T(8,128)}), f32[1664,256]{1,0:T(8,128)}) %reduce-scatter.5.cloned.1.call-update) | async-done | bytes 1703952 | tf_op jit(solution)/shard_map/reduce_scatter | solution.py:9
  241.4 2.5 convert_element_type.18
  243.9 0.0 reduce-scatter.7.cloned.1.call-start
  244.0 0.6 reduce_sum.9
  245.3 3.0 psum.7
  248.2 0.7 convert_divide_fusion
  248.9 99.8 %all-gather.3.cloned.1.call-done = bf16[13312,256]{1,0:T(8,128)(2,1)} async-done(((bf16[1664,256]{1,0:T(8,128)(2,1)}), bf16[13312,256]{1,0:T(8,128)(2,1)}) %all-gather.3.cloned.1.call-update) | async-done | bytes 6815760 | tf_op jit(solution)/shard_map/all_gather | solution.py:12
  348.7 12.7 %multiply_convert_fusion = bf16[13312,512]{1,0:T(8,128)(2,1)} fusion(bf16[13312,512]{1,0:T(8,128)(2,1)} %param.10, bf16[13312,256]{1,0:T(8,128)(2,1)} %all-gather.3.cloned.1.call-done, bf16[256,512]{1,0:T(8,128)(2,1)} %param.9, f32[512]{0:T(512)S(1)} %copy-done.2, f32[13312]{0:T(1024)S(1)} %convert_divide_fusion), kind=kOutput, calls=%fused_computation | convolution fusion | flops 3523739648 | bytes 34396160 | tf_op jit(solution)/shard_map/dot_general | solution.py:13
  361.4 13.5 %fusion.1 = f32[13312,256]{1,0:T(8,128)} fusion(bf16[13312,512]{1,0:T(8,128)(2,1)} %multiply_convert_fusion, bf16[256,512]{1,0:T(8,128)(2,1)} %param.9), kind=kOutput, calls=%fused_computation.4 | convolution fusion | flops 3489660928 | bytes 27525120 | tf_op jit(solution)/shard_map/pk,rk->pr/dot_general | solution.py:22
  375.0 0.0 all-gather.5.cloned.1.call-start
  375.0 220.2 %reduce-scatter.7.cloned.1.call-done = f32[1664,256]{1,0:T(8,128)} async-done(((f32[13312,256]{1,0:T(8,128)}), f32[1664,256]{1,0:T(8,128)}) %reduce-scatter.7.cloned.1.call-update) | async-done | bytes 1703952 | tf_op jit(solution)/shard_map/reduce_scatter | solution.py:23
  595.2 2.4 convert_element_type.23
  597.6 0.0 reduce-scatter.9.cloned.1.call-start
  597.7 104.8 %all-gather.5.cloned.1.call-done = bf16[13312,256]{1,0:T(8,128)(2,1)} async-done(((bf16[1664,256]{1,0:T(8,128)(2,1)}), bf16[13312,256]{1,0:T(8,128)(2,1)}) %all-gather.5.cloned.1.call-update) | async-done | bytes 6815760 | tf_op jit(solution)/shard_map/all_gather | solution.py:26
  702.5 5.6 convolution_bitcast_fusion
  708.1 0.2 reduce-scatter.11.cloned.1.call-start
  708.3 11.4 %fusion.2 = f32[256,512]{1,0:T(8,128)} fusion(bf16[13312,256]{1,0:T(8,128)(2,1)} %all-gather.3.cloned.1.call-done, bf16[13312,512]{1,0:T(8,128)(2,1)} %multiply_convert_fusion), kind=kOutput, calls=%fused_computation.5 | convolution fusion | flops 3489660928 | bytes 20971520 | tf_op jit(solution)/shard_map/pr,pk->rk/dot_general | solution.py:20
  719.7 0.0 reduce-scatter.9.cloned.1.call-done
  719.7 1.6 copy.8
  721.3 4.7 reduce-scatter.11.cloned.1.call-done
  (11 shorter events, 0.1 us)
Async XLA Ops:
  7.2 2.0 copy-start
  7.2 236.8 %copy-start.1 = (s32[13312]{0:T(1024)S(1)}, s32[13312]{0:T(1024)}, u32[]{:S(2)}) copy-start(s32[13312]{0:T(1024)} %param.7) | copy-start | bytes 159748
  7.2 341.5 %copy-start.2 = (f32[512]{0:T(512)S(1)}, f32[512]{0:T(512)}, u32[]{:S(2)}) copy-start(f32[512]{0:T(512)} %param.11) | copy-start | bytes 6148
  7.2 234.2 %reduce-scatter.5.cloned.1.call-start = ((), (), s32[]{:S(2)}) async-start(), calls=%async_computation.4 | async-start | bytes 15335424 | tf_op jit(solution)/shard_map/reduce_scatter | solution.py:9
  16.8 331.9 %all-gather.3.cloned.1.call-start = ((), (), s32[]{:S(2)}) async-start(), calls=%async_computation.5 | async-start | bytes 7667712 | tf_op jit(solution)/shard_map/all_gather | solution.py:12
  243.9 351.3 %reduce-scatter.7.cloned.1.call-start = ((), (), s32[]{:S(2)}) async-start(), calls=%async_computation.6 | async-start | bytes 15335424 | tf_op jit(solution)/shard_map/reduce_scatter | solution.py:23
  375.0 327.5 %all-gather.5.cloned.1.call-start = ((), (), s32[]{:S(2)}) async-start(), calls=%async_computation.7 | async-start | bytes 7667712 | tf_op jit(solution)/shard_map/all_gather | solution.py:26
  597.6 122.1 %reduce-scatter.9.cloned.1.call-start = ((), (), s32[]{:S(2)}) async-start(), calls=%async_computation.8 | async-start | bytes 196608 | tf_op jit(solution)/shard_map/reduce_scatter | solution.py:30
  708.1 17.9 %reduce-scatter.11.cloned.1.call-start = ((), (), s32[]{:S(2)}) async-start(), calls=%async_computation.9 | async-start | bytes 786432 | tf_op jit(solution)/shard_map/reduce_scatter | solution.py:21
Sparse Core Ops, SparseCore 0:
  16.9 224.4 reduce-scatter.4
  244.0 104.6 all-gather.2
  375.1 220.0 reduce-scatter.6
  597.8 104.6 all-gather.4
  708.2 5.6 reduce-scatter.8
  719.8 6.0 reduce-scatter.10
where the time goes:
time: 733 us
  waiting for transfers between devices  654 us (89%)
  matrix products  50.8 us (7%)
  between operations  14.8 us (2%)
    reduce_scatter x1, waiting for transfers between devices, local(): lax.psum_scatter(latent_terms, 'tgt', scatter_dimension=0, tiled=True)  225 us
    reduce_scatter x1, waiting for transfers between devices, local(): lax.psum_scatter(grad_terms, 'tgt', scatter_dimension=0, tiled=True)  220 us
    all_gather x1, waiting for transfers between devices, local(): latent_grad = lax.all_gather(grad_rows, 'tgt', axis=0, tiled=True)  105 us
    all_gather x1, waiting for transfers between devices, local(): latent = lax.all_gather(latent_part, 'tgt', axis=0, tiled=True)  99.8 us
  transfers between devices with their start and end apart: 6, of which 5 were waited for; matrix products, arithmetic and copies ran while one was open for 2% of the time, Pallas kernels for 0%

commit v1 on v0

v1 whole, which is shorter than its diff:
```python
import functools

import jax
import jax.numpy as jnp
from jax import lax
from jax.experimental import pallas as pl
from jax.experimental.pallas import tpu as pltpu
from jax.sharding import PartitionSpec as P

BF16 = jnp.bfloat16
F32 = jnp.float32
BLOCK = 256
SUB = 16


def compact_kernel(cap, rows, mask_ref, x_ref, out_ref, offset):
    step = pl.program_id(0)

    @pl.when(step == 0)
    def _():
        count = jnp.sum(mask_ref[...])
        base = jnp.maximum(cap - count, 0)
        offset[0] = base

        def clear(i, carry):
            out_ref[pl.ds(pl.multiple_of(i * BLOCK, BLOCK), BLOCK), :] = jnp.zeros(
                (BLOCK, out_ref.shape[1]), out_ref.dtype
            )
            return carry

        lax.fori_loop(0, base // BLOCK + 1, clear, 0)

    first = offset[0]
    mask = mask_ref[pl.ds(step, 1), 0, :]
    offset[0] = first + jnp.sum(mask)
    start = jnp.minimum(first // SUB * SUB, rows - BLOCK - SUB)
    start = pl.multiple_of(start, SUB)
    before = lax.broadcasted_iota(jnp.int32, (BLOCK, BLOCK), 0) < lax.broadcasted_iota(
        jnp.int32, (BLOCK, BLOCK), 1
    )
    prefix = jnp.dot(
        mask.astype(F32).astype(BF16), before.astype(F32).astype(BF16), preferred_element_type=F32
    ).astype(jnp.int32)
    slot = jnp.where(mask > 0, prefix + (first - start), -1)
    choose = lax.broadcasted_iota(jnp.int32, (BLOCK + SUB, BLOCK), 0) == slot
    moved = jnp.dot(choose.astype(F32).astype(BF16), x_ref[...], preferred_element_type=F32).astype(BF16)
    out_ref[pl.ds(start, SUB), :] += moved[:SUB]
    out_ref[pl.ds(start + SUB, BLOCK), :] = moved[SUB:]


def compact(mask_blocks, x, cap, extra):
    blocks, width = mask_blocks.shape[0], x.shape[1]
    rows = cap + extra + 2 * BLOCK
    return pl.pallas_call(
        functools.partial(compact_kernel, cap, rows),
        grid=(blocks,),
        out_shape=jax.ShapeDtypeStruct((rows, width), x.dtype),
        in_specs=[
            pl.BlockSpec(mask_blocks.shape, lambda i: (0, 0, 0)),
            pl.BlockSpec((BLOCK, width), lambda i: (i, 0)),
        ],
        out_specs=pl.BlockSpec((rows, width), lambda i: (0, 0)),
        scratch_shapes=[pltpu.SMEM((1,), jnp.int32)],
        compiler_params=pltpu.CompilerParams(vmem_limit_bytes=40 * 1024 * 1024),
        cost_estimate=pl.CostEstimate(
            flops=2 * (BLOCK + SUB) * x.shape[0] * width,
            bytes_accessed=2 * (x.shape[0] + rows) * width,
            transcendentals=0,
        ),
    )(mask_blocks, x)


def balance(buffer, cap, extra, received):
    other = lax.ppermute(buffer[cap : cap + extra], "tile", [(0, 1), (1, 0)])
    row = lax.broadcasted_iota(jnp.int32, (extra, 1), 0)
    head = jnp.where(row < received, other, buffer[:extra])
    return jnp.concatenate([head, buffer[extra:cap]], axis=0)


def gradients(cells, targets, factor_in, factor_out, target_weight, land_total):
    shards = lax.axis_size("tgt")
    own_cells = lax.all_to_all(cells, "tgt", split_axis=0, concat_axis=1, tiled=True)
    whole_in = lax.all_gather(factor_in, "tgt", axis=0, tiled=True)
    own_latent = jnp.dot(own_cells, whole_in, preferred_element_type=F32).astype(BF16)
    latent = lax.all_gather(own_latent, "tgt", axis=0, tiled=True)
    predicted = jnp.dot(latent, factor_out, preferred_element_type=F32)
    residual = (
        (predicted - targets.astype(F32)) * (1.0 / land_total) * target_weight[None, :]
    ).astype(BF16)
    out_partial = jnp.einsum("pr,pk->rk", latent, residual, preferred_element_type=F32)
    grad_out = lax.psum_scatter(out_partial, "tile", scatter_dimension=0, tiled=True)
    terms = jnp.einsum("pk,rk->pr", residual, factor_out, preferred_element_type=F32).astype(BF16)
    parts = lax.all_to_all(
        terms.reshape(shards, -1, terms.shape[1]), "tgt", split_axis=0, concat_axis=0, tiled=True
    )
    latent_grad = jnp.sum(parts.astype(F32), axis=0).astype(BF16)
    in_partial = jnp.einsum("pe,pr->er", own_cells, latent_grad, preferred_element_type=F32)
    in_half = lax.psum_scatter(in_partial, "tile", scatter_dimension=1, tiled=True)
    grad_in = lax.psum_scatter(in_half, "tgt", scatter_dimension=0, tiled=True)
    return grad_in, grad_out


def local(embeddings, land_mask, factor_in, factor_out, targets, target_weight):
    cells = embeddings.shape[0]
    shards, tiles, groups = lax.axis_size("tgt"), lax.axis_size("tile"), lax.axis_size("groups")
    grain = SUB * shards * 2
    cap = -(-cells * 33 // (64 * grain)) * grain
    extra = cap // 2

    tile, group = lax.axis_index("tile"), lax.axis_index("groups")
    count = jnp.sum(land_mask)
    place = jnp.arange(groups * tiles, dtype=jnp.int32)
    counts = lax.psum(
        jnp.where(place == group * tiles + tile, count, 0), ("groups", "tile")
    ).reshape(groups, tiles)
    over = jnp.maximum(counts - cap, 0)
    fits = jnp.all((over <= extra) & (jnp.minimum(counts, cap) + over[:, ::-1] <= cap))
    mine = lax.dynamic_index_in_dim(counts, group, 0, keepdims=False)
    land_total = jnp.sum(mine).astype(F32)
    received = lax.dynamic_index_in_dim(
        lax.dynamic_index_in_dim(over, group, 0, keepdims=False), 1 - tile, 0, keepdims=False
    )
    mask_blocks = land_mask.reshape(-1, 1, BLOCK)

    def compacted():
        few = balance(compact(mask_blocks, embeddings, cap, extra), cap, extra, received)
        few_targets = balance(compact(mask_blocks, targets, cap, extra), cap, extra, received)
        return gradients(few, few_targets, factor_in, factor_out, target_weight, land_total)

    def full():
        land = land_mask[:, None] > 0
        return gradients(
            jnp.where(land, embeddings, 0), jnp.where(land, targets, 0),
            factor_in, factor_out, target_weight, land_total,
        )

    return lax.cond(fits, compacted, full)


def solution(mesh):
    return jax.shard_map(
        local,
        mesh=mesh,
        in_specs=(
            P(("groups", "tile"), "tgt"),
            P(("groups", "tile")),
            P("tgt", None),
            P(None, "tgt"),
            P(("groups", "tile"), "tgt"),
            P("tgt"),
        ),
        out_specs=(P(("groups", "tgt"), "tile"), P(("groups", "tile"), "tgt")),
        check_vma=False,
    )
```

time: 733 us -> 385 us (0.53)
  waiting for transfers between devices: 654 us -> 97.5 us
  blocking collectives: 2.97 us -> 152 us
  Pallas kernels: 0 us -> 68 us
  matrix products: 50.8 us -> 18.7 us
  other arithmetic: 6.19 us -> 15.7 us
    reduce_scatter x4 -> x3, waiting for transfers between devices: 449 us -> 80.1 us  [the longest x1 66.9 us: gradients(): grad_in = lax.psum_scatter(in_half, 'tgt', scatter_dimension=0, tiled=True)]
    all_gather x2 -> x1, waiting for transfers between devices: 205 us -> 9.39 us  [gradients(): latent = lax.all_gather(own_latent, 'tgt', axis=0, tiled=True)]
    all_to_all x0 -> x1, blocking collectives: none -> 82.5 us  [gradients(): lax.all_to_all(terms.reshape(shards, -1, terms.shape[1]), 'tgt', split_ax...]
    pallas_call x0 -> x2, Pallas kernels: none -> 68 us  [compact(): pl.pallas_call(functools.partial(compact_kernel, cap, rows), grid=(blocks...]
    all_gather x0 -> x1, blocking collectives: none -> 62.7 us  [gradients(): whole_in = lax.all_gather(factor_in, 'tgt', axis=0, tiled=True)]
    dot_general x5, matrix products: 50.8 us -> 18.7 us  [the longest x1 5.95 us: gradients(): predicted = jnp.dot(latent, factor_out, preferred_element_type=F32)]
    select_n x0 -> x3, other arithmetic: none -> 9.55 us  [the longest x2 8.91 us: balance(): head = jnp.where(row < received, other, buffer[:extra])]
    ppermute x0 -> x2, waiting for transfers between devices: none -> 7.89 us  [balance(): other = lax.ppermute(buffer[cap:cap + extra], 'tile', [(0, 1), (1, 0)])]
  transfers between devices with their start and end apart: 6 -> 7, of which waited for: 5 -> 6; matrix products, arithmetic and copies ran while one was open for 2% -> 4% of each run, Pallas kernels for 0% -> 9%
where the time goes in v1:
time: 385 us; the launch traced here: 382 us
  blocking collectives  152 us (39%)
  waiting for transfers between devices  97.5 us (25%)
  Pallas kernels  68 us (18%)
  matrix products  18.7 us (5%)
  other arithmetic  15.7 us (4%)
  between operations  15 us (4%)
  local copies, waits for them, and re-layouts  8.84 us (2%)
  starting transfers between devices  6.13 us (2%)
    all_to_all x1, blocking collectives, gradients(): lax.all_to_all(terms.reshape(shards, -1, terms.shape[1]), 'tgt', split_ax...  82.5 us
    pallas_call x2, Pallas kernels, compact(): pl.pallas_call(functools.partial(compact_kernel, cap, rows), grid=(blocks...  68 us
    reduce_scatter x1, waiting for transfers between devices, gradients(): grad_in = lax.psum_scatter(in_half, 'tgt', scatter_dimension=0, tiled=True)  66.9 us
    all_gather x1, blocking collectives, gradients(): whole_in = lax.all_gather(factor_in, 'tgt', axis=0, tiled=True)  62.7 us
    reduce_scatter x1, waiting for transfers between devices, gradients(): lax.psum_scatter(out_partial, 'tile', scatter_dimension=0, tiled=True)  12 us
    all_gather x1, waiting for transfers between devices, gradients(): latent = lax.all_gather(own_latent, 'tgt', axis=0, tiled=True)  9.39 us
    select_n x2, other arithmetic, balance(): head = jnp.where(row < received, other, buffer[:extra])  8.91 us
    ppermute x2, waiting for transfers between devices, balance(): other = lax.ppermute(buffer[cap:cap + extra], 'tile', [(0, 1), (1, 0)])  7.89 us
  transfers between devices with their start and end apart: 7, of which 6 were waited for; matrix products, arithmetic and copies ran while one was open for 4% of the time, Pallas kernels for 9%

profile of v1, /device:TPU:0, one launch (start us, length us, event | category | flops | bytes accessed | tf_op | source)
XLA Modules:
  0.0 381.8 jit_solution(7007052429546769153)
XLA Ops:
  7.2 1.5 reduce_sum.42
  9.4 6.3 %psum.7 = s32[2,2]{1,0:T(2,128)S(1)} all-reduce(s32[2,2]{1,0:T(2,128)S(1)} %reshape.34), channel_id=1, replica_groups=mesh['groups'=2,'tgt'=8,'tile'=2] {'groups','tile'}, use_global_device_ids=true, to_apply=%region_1.2 | all-reduce | flops 4 | bytes 32 | tf_op jit(solution)/shard_map/psum | solution.py:113
  18.4 356.9 %conditional.1 = (f32[128,128]{1,0:T(8,128)}, f32[128,512]{1,0:T(8,128)}) conditional(s32[]{:T(128)} %convert_element_type.38, (s32[13312]{0:T(1024)}, bf16[13312,128]{1,0:T(8,128)(2,1)}, bf16[128,256]{1,0:T(8,128)(2,1)}, bf16[256,512]{1,0:T(8,128)(2,1)}, bf16[13312,512]{1,0:T(8,128)(2,1)}, /*index=5*/f32[]{:T(128)}, f32[512]{0:T(512)}) %tuple.16, ...), branch_computations={%region_4.9_spmd, %region_9.14_spmd} | conditional | flops 12263240704 | bytes 262542048 | solution.py:137
  18.6 31.8 %branch_1_fun.2 = bf16[10880,128]{1,0:T(8,128)(2,1)S(1)} custom-call(s32[52,1,256]{2,1,0:T(1,128)} %bitcast.46, bf16[13312,128]{1,0:T(8,128)(2,1)} %get-tuple-element.67.x_ref), custom_call_target="tpu_custom_call" | custom-call | flops 926941184 | bytes 6193152 | tf_op jit(solution)/shard_map/cond/branch_1_fun/pallas_call | solution.py:54
  52.7 1.5 collective-permute-done
  54.2 3.1 slice_select_fusion.1
  57.3 1.3 pad_maximum_fusion
  58.7 6.0 %all-to-all-start.2 = ((bf16[8,864,128]{2,1,0:T(8,128)(2,1)}), bf16[8,864,128]{2,1,0:T(8,128)(2,1)S(1)}, u32[]{:S(2)}, u32[]{:S(2)}) async-start(bf16[8,864,128]{2,1,0:T(8,128)(2,1)} %bitcast.6), calls=%async_computation.5 | async-start | bytes 3538944 | tf_op jit(solution)/shard_map/cond/branch_1_fun/all_to_all | solution.py:82
  64.7 62.7 %all_gather.10 = bf16[1024,256]{1,0:T(8,128)(2,1)S(1)} all-gather(bf16[128,256]{1,0:T(8,128)(2,1)S(1)} %copy-done.8), channel_id=1, replica_groups=mesh['groups'=2,'tgt'=8,'tile'=2] {'tgt'}, dimensions={0}, use_global_device_ids=true | all-gather | bytes 589824 | tf_op jit(solution)/shard_map/cond/branch_1_fun/all_gather | solution.py:83
  127.4 1.4 fusion.6
  128.9 36.2 %branch_1_fun.3 = bf16[10880,512]{1,0:T(8,128)(2,1)S(1)} custom-call(s32[52,1,256]{2,1,0:T(1,128)S(1)} %bitcast.47, bf16[13312,512]{1,0:T(8,128)(2,1)} %get-tuple-element.70.x_ref), custom_call_target="tpu_custom_call" | custom-call | flops 3707764736 | bytes 24772608 | tf_op jit(solution)/shard_map/cond/branch_1_fun/pallas_call | solution.py:54
  165.1 4.2 %copy-done = bf16[10880,512]{1,0:T(8,128)(2,1)} copy-done((bf16[10880,512]{1,0:T(8,128)(2,1)}, bf16[10880,512]{1,0:T(8,128)(2,1)S(1)}, u32[]{:S(2)}) %copy-start) | copy-done | bytes 11141144 | tf_op jit(solution)/shard_map/cond
  169.3 2.0 slice.21
  171.4 6.4 %collective-permute-done.1 = bf16[3456,512]{1,0:T(8,128)(2,1)S(1)} collective-permute-done((bf16[3456,512]{1,0:T(8,128)(2,1)}, bf16[3456,512]{1,0:T(8,128)(2,1)S(1)}, u32[]{:S(2)}, u32[]{:S(2)}) %collective-permute-start.1) | collective-permute-done | bytes 3538976 | tf_op jit(solution)/shard_map/cond/branch_1_fun/ppermute | solution.py:74
  177.8 5.8 %slice_select_fusion = (bf16[3456,512]{1,0:T(8,128)(2,1)}, bf16[3456,512]{1,0:T(8,128)(2,1)}) fusion(bf16[3456,512]{1,0:T(8,128)(2,1)S(1)} %collective-permute-done.1, bf16[10880,512]{1,0:T(8,128)(2,1)} %copy-done, pred[3456]{0:T(1024)(128)(4,1)S(1)} %iota_compare_fusion), kind=kLoop, calls=%fused_computation.7 | loop fusion | flops 1769472 | bytes 17698176 | tf_op jit(solution)/shard_map/cond/branch_1_fun/jit(_where)/select_n | solution.py:76
  183.5 9.4 %all-gather.5.cloned.1.call-done = bf16[6912,256]{1,0:T(8,128)(2,1)} async-done(((bf16[864,256]{1,0:T(8,128)(2,1)}), bf16[6912,256]{1,0:T(8,128)(2,1)}) %all-gather.5.cloned.1.call-update) | async-done | bytes 3538960 | tf_op jit(solution)/shard_map/cond/branch_1_fun/all_gather | solution.py:85
  192.9 5.9 %multiply_convert_fusion.1 = bf16[6912,512]{1,0:T(8,128)(2,1)S(1)} fusion(bf16[3456,512]{1,0:T(8,128)(2,1)} %get-tuple-element.80, bf16[3456,512]{1,0:T(8,128)(2,1)} %get-tuple-element.79, f32[512]{0:T(512)S(1)} %copy-done.12, f32[]{:T(128)S(6)} %div.5, bf16[6912,256]{1,0:T(8,128)(2,1)} %all-gather.5.cloned.1.call-done, bf16[256,512]{1,0:T(8,128)(2,1)} %get-tuple-element.69), kind=kOutput, calls=%fused_computation.5 | convolution fusion | flops 1840250880 | bytes 17958916 | tf_op jit(solution)/shard_map/cond/branch_1_fun/dot_general | solution.py:86
  198.9 2.0 convolution_convert_fusion.2
  201.8 82.5 %all_to_all.39 = bf16[8,864,256]{2,1,0:T(8,128)(2,1)S(1)} all-to-all(bf16[8,864,256]{2,1,0:T(8,128)(2,1)S(1)} %bitcast.43), channel_id=1, replica_groups=mesh['groups'=2,'tgt'=8,'tile'=2] {'tgt'}, dimensions={0} | all-to-all | bytes 7077888 | tf_op jit(solution)/shard_map/cond/branch_1_fun/all_to_all | solution.py:93
  284.3 1.4 reduce_sum.39
  285.7 3.4 fusion
  289.2 5.9 %fusion.11 = f32[256,512]{1,0:T(8,128)} fusion(bf16[6912,256]{1,0:T(8,128)(2,1)S(1)} %copy-done.3, bf16[6912,512]{1,0:T(8,128)(2,1)} %copy-done.2), kind=kOutput, calls=%fused_computation.24 | convolution fusion | flops 1811939328 | bytes 11141120 | tf_op jit(solution)/shard_map/cond/branch_1_fun/pr,pk->rk/dot_general | solution.py:90
  296.4 12.0 %reduce-scatter.17.cloned.1.call-done = f32[128,512]{1,0:T(8,128)} async-done(((f32[256,512]{1,0:T(8,128)}), f32[128,512]{1,0:T(8,128)}) %reduce-scatter.17.cloned.1.call-update) | async-done | bytes 262160 | tf_op jit(solution)/shard_map/cond/branch_1_fun/reduce_scatter | solution.py:91
  308.4 66.9 %reduce-scatter.15.cloned.1.call-done = f32[128,128]{1,0:T(8,128)} async-done(((f32[1024,128]{1,0:T(8,128)}), f32[128,128]{1,0:T(8,128)}) %reduce-scatter.15.cloned.1.call-update) | async-done | bytes 65552 | tf_op jit(solution)/shard_map/cond/branch_1_fun/reduce_scatter | solution.py:99
  (36 shorter events, 6.7 us)
Async XLA Ops:
  51.4 2.8 collective-permute-start
  57.3 7.4 %copy-start.8 = (bf16[128,256]{1,0:T(8,128)(2,1)S(1)}, bf16[128,256]{1,0:T(8,128)(2,1)}, u32[]{:S(2)}) copy-start(bf16[128,256]{1,0:T(8,128)(2,1)} %get-tuple-element.68) | copy-start | bytes 196612 | tf_op jit(solution)/shard_map/cond
  58.7 70.2 %copy-start.6 = (s32[13312]{0:T(1024)S(1)}, s32[13312]{0:T(1024)}, u32[]{:S(2)}) copy-start(s32[13312]{0:T(1024)} %get-tuple-element.66) | copy-start | bytes 159748 | tf_op jit(solution)/shard_map/cond
  58.7 68.7 %all-to-all-start.2 = ((bf16[8,864,128]{2,1,0:T(8,128)(2,1)}), bf16[8,864,128]{2,1,0:T(8,128)(2,1)S(1)}, u32[]{:S(2)}, u32[]{:S(2)}) async-start(bf16[8,864,128]{2,1,0:T(8,128)(2,1)} %bitcast.6), calls=%async_computation.5 | async-start | bytes 3538944 | tf_op jit(solution)/shard_map/cond/branch_1_fun/all_to_all | solution.py:82
  64.6 128.3 %all-gather.5.cloned.1.call-start = ((), (), s32[]{:S(2)}) async-start(), calls=%async_computation.14 | async-start | bytes 3981312 | tf_op jit(solution)/shard_map/cond/branch_1_fun/all_gather | solution.py:85
  127.4 37.7 %copy-start.5 = (bf16[8,864,128]{2,1,0:T(8,128)(2,1)}, bf16[8,864,128]{2,1,0:T(8,128)(2,1)S(1)}, u32[]{:S(2)}) copy-start(bf16[8,864,128]{2,1,0:T(8,128)(2,1)S(1)} %all-to-all-done.2) | copy-start | bytes 5308420 | tf_op jit(solution)/shard_map/cond
  128.8 167.5 %reduce-scatter.13.cloned.1.call-start = ((), (), s32[]{:S(2)}) async-start(), calls=%async_computation.15 | async-start | bytes 1572864 | tf_op jit(solution)/shard_map/cond/branch_1_fun/reduce_scatter | solution.py:98
  165.1 4.2 %copy-start = (bf16[10880,512]{1,0:T(8,128)(2,1)}, bf16[10880,512]{1,0:T(8,128)(2,1)S(1)}, u32[]{:S(2)}) copy-start(bf16[10880,512]{1,0:T(8,128)(2,1)S(1)} %branch_1_fun.3) | copy-start | bytes 33423364 | tf_op jit(solution)/shard_map/cond
  171.3 6.4 %collective-permute-start.1 = (bf16[3456,512]{1,0:T(8,128)(2,1)}, bf16[3456,512]{1,0:T(8,128)(2,1)S(1)}, u32[]{:S(2)}, u32[]{:S(2)}) collective-permute-start(bf16[3456,512]{1,0:T(8,128)(2,1)} %slice.21), channel_id=1, source_target_pairs={{0,1},{1,0},{2,3},{3,2},{4,5},{5,4},{6,7},{7,6},{8,9},{9,8},{10,11... | collective-permute-start | bytes 10616840 | tf_op jit(solution)/shard_map/cond/branch_1_fun/ppermute | solution.py:74
  171.4 21.6 %copy-start.12 = (f32[512]{0:T(512)S(1)}, f32[512]{0:T(512)}, u32[]{:S(2)}) copy-start(f32[512]{0:T(512)} %get-tuple-element.72) | copy-start | bytes 6148 | tf_op jit(solution)/shard_map/cond
  192.9 6.0 %copy-start.10 = (bf16[256,512]{1,0:T(8,128)(2,1)S(1)}, bf16[256,512]{1,0:T(8,128)(2,1)}, u32[]{:S(2)}) copy-start(bf16[256,512]{1,0:T(8,128)(2,1)} %get-tuple-element.69) | copy-start | bytes 786436 | tf_op jit(solution)/shard_map/cond
  198.9 2.9 copy-start.2
  285.7 3.5 copy-start.3
  289.1 19.3 %reduce-scatter.17.cloned.1.call-start = ((), (), s32[]{:S(2)}) async-start(), calls=%async_computation.17 | async-start | bytes 786432 | tf_op jit(solution)/shard_map/cond/branch_1_fun/reduce_scatter | solution.py:91
  295.1 80.2 %reduce-scatter.15.cloned.1.call-start = ((), (), s32[]{:S(2)}) async-start(), calls=%async_computation.16 | async-start | bytes 589824 | tf_op jit(solution)/shard_map/cond/branch_1_fun/reduce_scatter | solution.py:99
Sparse Core Ops, SparseCore 0:
  129.0 63.9 all-gather.4
  289.3 7.0 reduce-scatter.12
  299.3 9.1 reduce-scatter.16
  312.2 63.0 reduce-scatter.14

commit v2 on v0

v2 whole, which is shorter than its diff:
```python
import functools

import jax
import jax.numpy as jnp
from jax import lax
from jax.experimental import pallas as pl
from jax.experimental.pallas import tpu as pltpu
from jax.sharding import PartitionSpec as P

BF16 = jnp.bfloat16
F32 = jnp.float32
BLOCK = 256
GROUP = 13
SUB = 16
CHUNKS = 2
MIB = 1024 * 1024


def dot(a, b, dims=((1,), (0,))):
    return lax.dot_general(a, b, (dims, ((), ())), preferred_element_type=F32)


def compact_kernel(group, cap, extra, rows, shards, first_ref, pair_ref, mask_ref, cells_ref, targets_ref, *refs):
    (late_ref, early_ref, over_ref, main_ref, pair_out_ref, far_ref, cells_all, targets_all, sems) = refs
    step = pl.program_id(0)
    arrays = ((cells_ref, cells_all), (targets_ref, targets_all))

    @pl.when(step == 0)
    def _():
        def clear(i, carry):
            for _, out_ref in arrays:
                out_ref[pl.ds(pl.multiple_of(i * BLOCK, BLOCK), BLOCK), :] = jnp.zeros(
                    (BLOCK, out_ref.shape[1]), out_ref.dtype
                )
            return carry

        lax.fori_loop(0, first_ref[0] // BLOCK + 1, clear, 0)

    before = lax.broadcasted_iota(jnp.int32, (BLOCK, BLOCK), 0) < lax.broadcasted_iota(
        jnp.int32, (BLOCK, BLOCK), 1
    )
    before = before.astype(F32).astype(BF16)
    place = lax.broadcasted_iota(jnp.int32, (BLOCK + SUB, BLOCK), 0)
    mask = mask_ref[0]
    prefix = dot(mask.astype(F32).astype(BF16), before).astype(jnp.int32)
    for k in range(group):
        first = first_ref[step * group + k]
        start = jnp.minimum(first // SUB * SUB, rows - BLOCK - SUB)
        slot = jnp.where(mask[k : k + 1] > 0, prefix[k : k + 1] + (first - start), -1)
        choose = (place == slot).astype(F32).astype(BF16)
        start = pl.multiple_of(start, SUB)
        for x_ref, out_ref in arrays:
            moved = dot(choose, x_ref[k * BLOCK : (k + 1) * BLOCK, :]).astype(BF16)
            out_ref[pl.ds(start, SUB), :] += moved[:SUB]
            out_ref[pl.ds(start + SUB, BLOCK), :] = moved[SUB:]

    @pl.when(step == pl.num_programs(0) - 1)
    def _():
        block, count = extra // shards, shards // 2
        moves = [
            (cells_all.at[pl.ds(extra + (y * count + z) * block, block)], late_ref.at[2 * z + y])
            for z in range(count)
            for y in (0, 1)
        ]
        moves += [
            (cells_all.at[pl.ds(cap, extra)], over_ref),
            (cells_all.at[pl.ds(0, extra)], early_ref),
            (targets_all.at[pl.ds(pl.multiple_of(pair_ref[0], SUB), extra // 2)], pair_out_ref),
            (targets_all.at[pl.ds(cap, extra)], far_ref),
            (targets_all.at[pl.ds(0, cap)], main_ref),
        ]
        copies = [pltpu.make_async_copy(x, out, sems.at[i]) for i, (x, out) in enumerate(moves)]
        for copy in copies:
            copy.start()
        for copy in copies:
            copy.wait()


def compact(firsts, pair_at, mask_blocks, cells, targets, cap, extra, shards):
    rows = -(-(cap + extra + 2 * BLOCK) // BLOCK) * BLOCK
    blocks = mask_blocks.shape[0]
    group = max(g for g in range(1, GROUP + 1) if blocks % g == 0)
    width, columns = cells.shape[1], targets.shape[1]
    shapes = [(shards, extra // shards, width), (extra, width), (extra, width)]
    shapes += [(cap, columns), (extra // 2, columns), (extra, columns)]
    return pl.pallas_call(
        functools.partial(compact_kernel, group, cap, extra, rows, shards),
        grid_spec=pltpu.PrefetchScalarGridSpec(
            num_scalar_prefetch=2,
            grid=(blocks // group,),
            in_specs=[pl.BlockSpec((1, group, BLOCK), lambda i, f, p: (i, 0, 0))]
            + [pl.BlockSpec((group * BLOCK, w), lambda i, f, p: (i, 0)) for w in (width, columns)],
            out_specs=[pl.BlockSpec(memory_space=pl.ANY)] * len(shapes),
            scratch_shapes=[
                pltpu.VMEM((rows, width), BF16),
                pltpu.VMEM((rows, columns), BF16),
                pltpu.SemaphoreType.DMA((shards + 5,)),
            ],
        ),
        out_shape=[jax.ShapeDtypeStruct(shape, BF16) for shape in shapes],
        compiler_params=pltpu.CompilerParams(vmem_limit_bytes=40 * MIB),
        cost_estimate=pl.CostEstimate(
            flops=2 * (BLOCK + SUB) * blocks * BLOCK * (width + columns),
            bytes_accessed=2 * (blocks * BLOCK + rows) * (width + columns),
            transcendentals=0,
        ),
        name="compact",
    )(firsts, pair_at.reshape(1), mask_blocks.reshape(-1, group, BLOCK), cells, targets)


SWAP = [(0, 1), (1, 0)]


def send(x, moves):
    return lax.ppermute(x, "tgt", moves)


def shifted(count, s, flip):
    return [(2 * z + y, 2 * ((z + s) % count) + (y ^ flip)) for z in range(count) for y in (0, 1)]


def latent_kernel(y_ref, slot_ref, cells_ref, factor_ref, out_ref):
    total = None
    for source in range(cells_ref.shape[0]):
        flip = (y_ref[0] + source) % 2
        part = dot(cells_ref[source], factor_ref[flip, slot_ref[source // 2]])
        total = part if total is None else total + part
    out_ref[...] = total.astype(BF16)


def latent_of(y, slot_of, cells, factor_in):
    sources, rows, width = cells.shape
    rank = factor_in.shape[3]
    return pl.pallas_call(
        latent_kernel,
        in_specs=[pl.BlockSpec(memory_space=pltpu.SMEM)] * 2 + [pl.BlockSpec(memory_space=pltpu.VMEM)] * 2,
        out_specs=pl.BlockSpec(memory_space=pltpu.VMEM),
        out_shape=jax.ShapeDtypeStruct((rows, rank), BF16),
        compiler_params=pltpu.CompilerParams(vmem_limit_bytes=16 * MIB),
        cost_estimate=pl.CostEstimate(
            flops=2 * sources * rows * width * rank,
            bytes_accessed=2 * sources * width * (rows + rank) + 2 * rows * rank,
            transcendentals=0,
        ),
        name="latent",
    )(y.reshape(1), slot_of, cells, factor_in)


def residual_kernel(
    count, mixed, own_ref, pair_ref, part_ref, scale_ref, weight_ref, far_weight_ref, factor_ref, far_factor_ref, *refs
):
    slot = pl.program_id(0)
    latents, refs = refs[:count], refs[count:]
    targets_ref, far_targets_ref, refs = refs[0], refs[1], refs[2:]
    if mixed:
        other_ref, refs = refs[0], refs[1:]
    terms, (out_ref, far_out_ref, held) = refs[:count], refs[count:]
    rows = targets_ref.shape[0]

    for s in range(count):

        @pl.when(slot == s)
        def _():
            held[...] = latents[s][...]

    @pl.when(slot == 0)
    def _():
        out_ref[...] = jnp.zeros_like(out_ref)
        far_out_ref[...] = jnp.zeros_like(far_out_ref)

    latent = held[...]
    targets = targets_ref[...].astype(F32)
    if mixed:
        row = own_ref[slot] * rows + lax.broadcasted_iota(jnp.int32, (rows, 1), 0)
        targets = jnp.where(row < part_ref[0], other_ref[...].astype(F32), targets)
    factor, far_factor = factor_ref[...], far_factor_ref[...]
    scale = scale_ref[0, 0]
    residual = ((dot(latent, factor) - targets) * scale * weight_ref[...]).astype(BF16)
    far_targets = far_targets_ref[...].astype(F32)
    far_residual = ((dot(latent, far_factor) - far_targets) * scale * far_weight_ref[...]).astype(BF16)
    total = dot(residual, factor, ((1,), (1,))) + dot(far_residual, far_factor, ((1,), (1,)))
    total = total.astype(BF16)
    for s in range(count):

        @pl.when(slot == s)
        def _():
            terms[s][...] = total

    out_ref[...] += dot(latent, residual, ((0,), (0,)))
    far_out_ref[...] += dot(latent, far_residual, ((0,), (0,)))


def residual_of(own_at, pair_at, received, scale, weights, factors, latents, own, pair, other):
    count = len(latents)
    rows, rank = latents[0].shape
    width = own.shape[1]
    mixed = other is not None
    whole = lambda shape: pl.BlockSpec(shape, lambda i, o, p, r: (0, 0))
    by_own = pl.BlockSpec((rows, width), lambda i, o, p, r: (o[i], 0))
    by_pair = pl.BlockSpec((rows, width), lambda i, o, p, r: (p[i], 0))
    result = pl.pallas_call(
        functools.partial(residual_kernel, count, mixed),
        grid_spec=pltpu.PrefetchScalarGridSpec(
            num_scalar_prefetch=3,
            grid=(count,),
            in_specs=[pl.BlockSpec((1, 1), lambda i, o, p, r: (0, 0), memory_space=pltpu.SMEM)]
            + [whole((1, width))] * 2
            + [whole((rank, width))] * 2
            + [whole((rows, rank))] * count
            + [by_own, by_pair]
            + [by_own] * mixed,
            out_specs=[whole((rows, rank))] * count + [whole((rank, width))] * 2,
            scratch_shapes=[pltpu.VMEM((rows, rank), BF16)],
        ),
        out_shape=[jax.ShapeDtypeStruct((rows, rank), BF16)] * count
        + [jax.ShapeDtypeStruct((rank, width), F32)] * 2,
        compiler_params=pltpu.CompilerParams(vmem_limit_bytes=56 * MIB),
        cost_estimate=pl.CostEstimate(
            flops=count * rows * rank * width,
            bytes_accessed=count * rows * (rank + width),
            transcendentals=0,
        ),
        name="residual",
    )(
        own_at, pair_at, received, scale.reshape(1, 1), *[w.reshape(1, -1) for w in weights], *factors,
        *latents, own, pair, *([other] * mixed),
    )
    return result[:count], result[count], result[count + 1]


def in_kernel(tile_ref, *refs):
    (keep_ref, pass_ref), refs = refs[-2:], refs[:-2]
    half = keep_ref.shape[2]
    for tile in (0, 1):

        @pl.when(tile_ref[0] == tile)
        def _():
            for source in range(keep_ref.shape[0]):
                total = None
                for cells_ref, grads_ref in zip(refs[:CHUNKS], refs[CHUNKS:]):
                    part = dot(cells_ref[source], grads_ref[...], ((0,), (0,)))
                    total = part if total is None else total + part
                keep_ref[source] = total[:, tile * half : (tile + 1) * half]
                pass_ref[source] = total[:, (1 - tile) * half : (2 - tile) * half]


def in_of(tile, cells, latent_grads):
    sources, rows, width = cells[0].shape
    rank = latent_grads[0].shape[1]
    shape = jax.ShapeDtypeStruct((sources, width, rank // 2), F32)
    return pl.pallas_call(
        in_kernel,
        in_specs=[pl.BlockSpec(memory_space=pltpu.SMEM)]
        + [pl.BlockSpec(memory_space=pltpu.VMEM)] * (2 * CHUNKS),
        out_specs=[pl.BlockSpec(memory_space=pltpu.VMEM)] * 2,
        out_shape=[shape, shape],
        compiler_params=pltpu.CompilerParams(vmem_limit_bytes=16 * MIB),
        cost_estimate=pl.CostEstimate(
            flops=2 * CHUNKS * sources * rows * width * rank,
            bytes_accessed=2 * CHUNKS * rows * (width * sources + rank) + 4 * sources * width * rank,
            transcendentals=0,
        ),
        name="in_part",
    )(tile.reshape(1), *cells, *latent_grads)


def compacted_gradients(
    late, early, over, own_targets, pair_late, over_targets, received, whole_in, factors, weights, land_total
):
    shards = lax.axis_size("tgt")
    count = shards // 2
    index, tile = lax.axis_index("tgt"), lax.axis_index("tile")
    z, y = index // 2, index % 2
    extra = early.shape[0]
    scale = 1.0 / land_total
    slot_z = (z - jnp.arange(count, dtype=jnp.int32)) % count

    other_cells = lax.ppermute(over, "tile", SWAP)
    other_targets = lax.ppermute(over_targets, "tile", SWAP)

    def merged(own, other, at, size):
        row = at + lax.broadcasted_iota(jnp.int32, (size, 1), 0)
        own, other = (lax.dynamic_slice_in_dim(x, at, size, axis=0) for x in (own, other))
        return jnp.where(row < received[0], other, own)

    order = (1, 0)
    early = merged(early, other_cells, 0, extra)
    early = early.reshape(2, count, extra // shards, -1).swapaxes(0, 1).reshape(late.shape)

    def owners_cells(x):
        return lax.all_to_all(x, "tgt", split_axis=0, concat_axis=0, tiled=True)

    def along_line(x):
        return [x] + [send(x, shifted(count, s, 0)) for s in range(1, count)]

    pairs = {1: send(pair_late, shifted(count, 0, 1))}
    cells = {1: owners_cells(late), 0: owners_cells(early)}
    mine = latent_of(y, slot_z, cells[1], whole_in)
    mine, own_targets, other_targets = lax.optimization_barrier((mine, own_targets, other_targets))
    latents = {1: along_line(mine)}
    pair_early = merged(own_targets, other_targets, (1 - y) * (extra // 2), extra // 2)
    pairs[0] = send(pair_early, shifted(count, 0, 1))
    cells[0], latents[1] = lax.optimization_barrier((cells[0], latents[1]))
    latents[0] = along_line(latent_of(y, slot_z, cells[0], whole_in))

    def residual(chunk):
        return residual_of(
            slot_z + (chunk * 2 + y) * count, slot_z, received, scale, weights, factors,
            latents[chunk], own_targets, pairs[chunk], other_targets if chunk == 0 else None,
        )

    def summed(terms):
        total = terms[0].astype(F32)
        for s in range(1, count):
            total = total + send(terms[s], shifted(count, -s, 0)).astype(F32)
        return total.astype(BF16)

    late_parts, latents[0], pairs[0] = lax.optimization_barrier((residual(1), latents[0], pairs[0]))
    grads = {1: summed(late_parts[0])}
    early_parts, grads[1] = lax.optimization_barrier((residual(0), grads[1]))
    grads[0] = summed(early_parts[0])
    own_part, far_part = late_parts[1] + early_parts[1], late_parts[2] + early_parts[2]
    out_part = jnp.stack([own_part, far_part])
    half = out_part.shape[1] // 2
    out_half = lax.dynamic_slice_in_dim(out_part, tile * half, half, axis=1) + lax.ppermute(
        lax.dynamic_slice_in_dim(out_part, (1 - tile) * half, half, axis=1), "tile", SWAP
    )
    grad_out = out_half[0] + send(out_half[1], shifted(count, 0, 1))
    grads[0], grad_out = lax.optimization_barrier((grads[0], grad_out))
    keep, passed = in_of(tile, [cells[c] for c in order], [grads[c] for c in order])
    mine = keep + lax.ppermute(passed, "tile", SWAP)
    grad_in = lax.dynamic_index_in_dim(mine, index, 0, keepdims=False)
    for s in range(1, shards):
        to_z, to_y = (z + s) % count, y ^ (s // count)
        part = lax.dynamic_index_in_dim(mine, 2 * to_z + to_y, 0, keepdims=False)
        grad_in = grad_in + send(part, shifted(count, s % count, s // count))
    return grad_in, grad_out


def full_gradients(cells, targets, factor_in, factor_out, target_weight, land_total):
    shards = lax.axis_size("tgt")
    own_cells = lax.all_to_all(cells, "tgt", split_axis=0, concat_axis=1, tiled=True)
    whole_in = lax.all_gather(factor_in, "tgt", axis=0, tiled=True)
    own_latent = dot(own_cells, whole_in).astype(BF16)
    latent = lax.all_gather(own_latent, "tgt", axis=0, tiled=True)
    residual = (
        (dot(latent, factor_out) - targets.astype(F32)) * (1.0 / land_total) * target_weight[None, :]
    ).astype(BF16)
    out_partial = dot(latent, residual, ((0,), (0,)))
    grad_out = lax.psum_scatter(out_partial, "tile", scatter_dimension=0, tiled=True)
    terms = dot(residual, factor_out, ((1,), (1,))).astype(BF16)
    parts = lax.all_to_all(
        terms.reshape(shards, -1, terms.shape[1]), "tgt", split_axis=0, concat_axis=0, tiled=True
    )
    latent_grad = jnp.sum(parts.astype(F32), axis=0).astype(BF16)
    in_partial = dot(own_cells, latent_grad, ((0,), (0,)))
    in_half = lax.psum_scatter(in_partial, "tile", scatter_dimension=1, tiled=True)
    grad_in = lax.psum_scatter(in_half, "tgt", scatter_dimension=0, tiled=True)
    return grad_in, grad_out


def local(embeddings, land_mask, factor_in, factor_out, targets, target_weight):
    cells = embeddings.shape[0]
    shards, groups = lax.axis_size("tgt"), lax.axis_size("groups")
    grain = SUB * shards * CHUNKS
    cap = -(-cells * 33 // (64 * grain)) * grain
    extra = cap // 2

    y = lax.axis_index("tgt") % 2
    pair_in = jnp.stack([factor_in, send(factor_in, shifted(shards // 2, 0, 1))])
    weights = (target_weight, send(target_weight, shifted(shards // 2, 0, 1)))
    mask_blocks = land_mask.reshape(-1, BLOCK)
    in_block = jnp.sum(mask_blocks, axis=1)
    land = jnp.sum(land_mask).reshape(1)
    at = jnp.arange(in_block.shape[0], dtype=jnp.int32)
    firsts = jnp.maximum(cap - land, 0) + jnp.sum(
        jnp.where(at[None, :] < at[:, None], in_block[None, :], 0), axis=1
    )
    other = lax.ppermute(land, "tile", SWAP)
    firsts, mask_blocks, other, pair_in = lax.optimization_barrier((firsts, mask_blocks, other, pair_in))
    counts = [jnp.concatenate([land, other])]
    counts += [
        lax.ppermute(counts[0], "groups", [(a, (a + g) % groups) for a in range(groups)]) for g in range(1, groups)
    ]
    line_in = [pair_in] + [send(pair_in, shifted(shards // 2, s, 0)) for s in range(1, shards // 2)]
    factors = (factor_out, send(factor_out, shifted(shards // 2, 0, 1)))
    kept = compact(firsts, extra + (1 - y) * (extra // 2), mask_blocks, embeddings, targets, cap, extra, shards)
    kept, counts, line_in, factors = lax.optimization_barrier((kept, counts, line_in, factors))
    counts = jnp.stack(counts)
    low, high = jnp.min(counts, axis=1), jnp.max(counts, axis=1)
    fits = jnp.all((low + jnp.maximum(high - cap, 0) <= cap) & (high - cap <= extra))
    land_total = (land + other)[0].astype(F32)
    received = jnp.maximum(other - cap, 0)

    def few():
        return compacted_gradients(
            *kept, received, jnp.stack(line_in, axis=1), factors, weights, land_total
        )

    def full():
        is_land = land_mask[:, None] > 0
        return full_gradients(
            jnp.where(is_land, embeddings, 0), jnp.where(is_land, targets, 0),
            factor_in, factor_out, target_weight, land_total,
        )

    return lax.cond(fits, few, full)


def solution(mesh):
    return jax.shard_map(
        local,
        mesh=mesh,
        in_specs=(
            P(("groups", "tile"), "tgt"),
            P(("groups", "tile")),
            P("tgt", None),
            P(None, "tgt"),
            P(("groups", "tile"), "tgt"),
            P("tgt"),
        ),
        out_specs=(P(("groups", "tgt"), "tile"), P(("groups", "tile"), "tgt")),
        check_vma=False,
    )
```

time: 733 us -> 225 us (0.31)
  waiting for transfers between devices: 654 us -> 92.5 us
  matrix products: 50.8 us -> 0 us
  starting transfers between devices: 0.43 us -> 50.9 us
  Pallas kernels: 0 us -> 39.7 us
  other arithmetic: 6.19 us -> 20.5 us
    reduce_scatter x4 -> x0, waiting for transfers between devices: 449 us -> none  [the longest x1 225 us: local(): lax.psum_scatter(latent_terms, 'tgt', scatter_dimension=0, tiled=True)]
    all_gather x2 -> x0, waiting for transfers between devices: 205 us -> none  [the longest x1 105 us: local(): latent_grad = lax.all_gather(grad_rows, 'tgt', axis=0, tiled=True)]
    ppermute x0 -> x34, waiting for transfers between devices: none -> 54.8 us  [the longest x28 53 us: send(): return lax.ppermute(x, 'tgt', moves)]
    dot_general x5 -> x0, matrix products: 50.8 us -> none  [the longest x1 13.5 us: local(): jnp.einsum('pk,rk->pr', residual, factor_out, preferred_element_type=jnp....]
    ppermute x0 -> x34, starting transfers between devices: none -> 42 us  [the longest x28 39.5 us: send(): return lax.ppermute(x, 'tgt', moves)]
    pallas_call x0 -> x6, Pallas kernels: none -> 39.7 us  [the longest x2 20.1 us: residual_of(): pl.pallas_call(functools.partial(residual_kernel, count, mixed), grid_spe...]
    all_to_all x0 -> x2, waiting for transfers between devices: none -> 37.7 us  [owners_cells(): return lax.all_to_all(x, 'tgt', split_axis=0, concat_axis=0, tiled=True)]
    all_to_all x0 -> x2, starting transfers between devices: none -> 8.87 us  [owners_cells(): return lax.all_to_all(x, 'tgt', split_axis=0, concat_axis=0, tiled=True)]
  transfers between devices with their start and end apart: 6 -> 36, of which waited for: 5 -> 15; matrix products, arithmetic and copies ran while one was open for 2% -> 7% of each run, Pallas kernels for 0% -> 17%
where the time goes in v2:
time: 225 us
  waiting for transfers between devices  92.5 us (41%)
  starting transfers between devices  50.9 us (23%)
  Pallas kernels  39.7 us (18%)
  other arithmetic  20.5 us (9%)
  between operations  16.7 us (7%)
  local copies, waits for them, and re-layouts  3.37 us (1%)
    ppermute x28, waiting for transfers between devices, send(): return lax.ppermute(x, 'tgt', moves)  53 us
    ppermute x28, starting transfers between devices, send(): return lax.ppermute(x, 'tgt', moves)  39.5 us
    all_to_all x2, waiting for transfers between devices, owners_cells(): return lax.all_to_all(x, 'tgt', split_axis=0, concat_axis=0, tiled=True)  37.7 us
    pallas_call x2, Pallas kernels, residual_of(): pl.pallas_call(functools.partial(residual_kernel, count, mixed), grid_spe...  20.1 us
    pallas_call x1, Pallas kernels, compact(): pl.pallas_call(functools.partial(compact_kernel, group, cap, extra, rows,...  16.5 us
    all_to_all x2, starting transfers between devices, owners_cells(): return lax.all_to_all(x, 'tgt', split_axis=0, concat_axis=0, tiled=True)  8.87 us
    select_n x2, other arithmetic, merged(): return jnp.where(row < received[0], other, own)  6.72 us
  transfers between devices with their start and end apart: 36, of which 15 were waited for; matrix products, arithmetic and copies ran while one was open for 7% of the time, Pallas kernels for 17%

profile of v2, /device:TPU:0, one launch (start us, length us, event | category | flops | bytes accessed | tf_op | source)
XLA Modules:
  0.0 224.7 jit_solution(8244241298208571310)
XLA Ops:
  9.1 2.5 %collective-permute-start.27 = (bf16[128,256]{1,0:T(8,128)(2,1)}, bf16[128,256]{1,0:T(8,128)(2,1)S(1)}, u32[]{:S(2)}, u32[]{:S(2)}) collective-permute-start(bf16[128,256]{1,0:T(8,128)(2,1)} %param.10), channel_id=1, source_target_pairs={{0,2},{2,0},{4,6},{6,4},{8,10},{10,8},{12,14},{14,12},{1,3},{3,1},... | collective-permute-start | bytes 196616 | tf_op jit(solution)/shard_map/ppermute | solution.py:115
  16.1 4.0 %collective-permute-start.31 = (bf16[2,128,256]{2,1,0:T(8,128)(2,1)}, bf16[2,128,256]{2,1,0:T(8,128)(2,1)}, u32[]{:S(2)}, u32[]{:S(2)}) collective-permute-start(bf16[2,128,256]{2,1,0:T(8,128)(2,1)} %pad_maximum_fusion.1), channel_id=1, source_target_pairs={{0,12},{2,14},{4,0},{6,2},{8,4},{10,6},{12,8},{14,10},{1,13},{3,15... | collective-permute-start | bytes 393224 | tf_op jit(solution)/shard_map/ppermute | solution.py:115
  24.0 16.5 %compact.1 = (bf16[8,432,128]{2,1,0:T(8,128)(2,1)}, bf16[3456,128]{1,0:T(8,128)(2,1)}, bf16[3456,128]{1,0:T(8,128)(2,1)}, bf16[6912,512]{1,0:T(8,128)(2,1)}, bf1...) custom-call(s32[52]{0:T(128)S(1)} %broadcast_add_fusion.2.first_ref, s32[1]{0:T(128)} %bitcast.33.pair_ref, ...), custom_call_target="tpu_custom_call" | custom-call | flops 4634705920 | bytes 31129600 | tf_op jit(solution)/shard_map/compact/pallas_call | solution.py:86
  45.5 172.4 %conditional.1 = (f32[128,128]{1,0:T(8,128)}, f32[128,512]{1,0:T(8,128)}) conditional(s32[]{:T(128)} %convert_element_type.57, (s32[13312]{0:T(1024)S(1)}, bf16[13312,128]{1,0:T(8,128)(2,1)S(1)}, bf16[128,256]{1,0:T(8,128)(2,1)}, bf16[256,512]{1,0:T(8,128)(2,1)}, bf16[13312,512]{1,0:T(8,128)(2,1)}, /*index=5*/f32[]{:T(128)}, ...), branch_computations={%region_6.11_spmd, %region_11.12_spmd} | conditional | flops 12263240704 | bytes 233379200 | solution.py:407
  46.0 5.2 %all-to-all-start = ((bf16[8,432,128]{2,1,0:T(8,128)(2,1)}), bf16[8,432,128]{2,1,0:T(8,128)(2,1)S(1)}, u32[]{:S(2)}, u32[]{:S(2)}) async-start(bf16[8,432,128]{2,1,0:T(8,128)(2,1)} %get-tuple-element.57), calls=%async_computation | async-start | bytes 1769472 | tf_op jit(solution)/shard_map/cond/branch_1_fun/all_to_all | solution.py:291
  55.2 2.8 %broadcast_select_fusion.1 = bf16[3456,128]{1,0:T(8,128)(2,1)S(1)} fusion(bf16[3456,128]{1,0:T(8,128)(2,1)S(1)} %collective-permute-done, bf16[3456,128]{1,0:T(8,128)(2,1)} %get-tuple-element.60, pred[3456]{0:T(1024)(128)(4,1)S(1)} %iota_compare_fusion), kind=kLoop, calls=%fused_computation.10 | loop fusion | flops 442368 | bytes 2657664 | tf_op jit(solution)/shard_map/cond/branch_1_fun/jit(_where)/select_n | solution.py:284
  59.0 14.7 %all-to-all-done.cells_ref.refs_0_ = bf16[8,432,128]{2,1,0:T(8,128)(2,1)S(1)} async-done(((bf16[8,432,128]{2,1,0:T(8,128)(2,1)}), bf16[8,432,128]{2,1,0:T(8,128)(2,1)S(1)}, u32[]{:S(2)}, u32[]{:S(2)}) %all-to-all-start) | async-done | bytes 884768 | tf_op jit(solution)/shard_map/cond/branch_1_fun/all_to_all | solution.py:291
  73.8 3.6 %all-to-all-start.1 = ((bf16[8,432,128]{2,1,0:T(8,128)(2,1)}), bf16[8,432,128]{2,1,0:T(8,128)(2,1)S(1)}, u32[]{:S(2)}, u32[]{:S(2)}) async-start(bf16[8,432,128]{2,1,0:T(8,128)(2,1)} %bitcast.76), calls=%async_computation.1 | async-start | bytes 1769472 | tf_op jit(solution)/shard_map/cond/branch_1_fun/all_to_all | solution.py:291
  78.6 3.9 %dynamic-slice_select_fusion = bf16[1728,512]{1,0:T(8,128)(2,1)} fusion(bf16[6912,512]{1,0:T(8,128)(2,1)} %get-tuple-element.78.refs_4_, s32[]{:T(128)S(6)} %select_n.85, bf16[3456,512]{1,0:T(8,128)(2,1)} %collective-permute-done.1.refs_6_, s32[]{:T(128)S(6)} %select_n.84, pred[1728]{0:T(1024)(128)(4,1)S(1)} %add_compare_fusion), kind=kLoop, calls=%fused_computation.5 | loop fusion | flops 884736 | bytes 5310152 | tf_op jit(solution)/shard_map/cond/branch_1_fun/jit(_where)/select_n | solution.py:284
  84.5 3.3 %collective-permute-start.4 = (bf16[432,256]{1,0:T(8,128)(2,1)S(1)}, bf16[432,256]{1,0:T(8,128)(2,1)S(1)}, u32[]{:S(2)}, u32[]{:S(2)}) collective-permute-start(bf16[432,256]{1,0:T(8,128)(2,1)S(1)} %latent.2.refs_0_), channel_id=1, source_target_pairs={{0,12},{2,14},{4,0},{6,2},{8,4},{10,6},{12,8},{14,10},{1,13},{3,15... | collective-permute-start | bytes 663560 | tf_op jit(solution)/shard_map/cond/branch_1_fun/ppermute | solution.py:115
  88.9 23.0 %all-to-all-done.1.cells_ref.refs_1_ = bf16[8,432,128]{2,1,0:T(8,128)(2,1)S(1)} async-done(((bf16[8,432,128]{2,1,0:T(8,128)(2,1)}), bf16[8,432,128]{2,1,0:T(8,128)(2,1)S(1)}, u32[]{:S(2)}, u32[]{:S(2)}) %all-to-all-start.1) | async-done | bytes 884768 | tf_op jit(solution)/shard_map/cond/branch_1_fun/all_to_all | solution.py:291
  111.9 6.9 %collective-permute-done.3.refs_2_ = bf16[432,256]{1,0:T(8,128)(2,1)S(1)} collective-permute-done((bf16[432,256]{1,0:T(8,128)(2,1)S(1)}, bf16[432,256]{1,0:T(8,128)(2,1)S(1)}, u32[]{:S(2)}, u32[]{:S(2)}) %collective-permute-start.3) | collective-permute-done | bytes 221216 | tf_op jit(solution)/shard_map/cond/branch_1_fun/ppermute | solution.py:115
  124.0 9.9 %residual.2 = (bf16[432,256]{1,0:T(8,128)(2,1)}, bf16[432,256]{1,0:T(8,128)(2,1)}, bf16[432,256]{1,0:T(8,128)(2,1)}, bf16[432,256]{1,0:T(8,128)(2,1)}, f32[256,512]{1,0:T(8,128)}, /*index=5*/f32[256,512]{1,0:T(8,128)}) custom-call(s32[4]{0:T(128)} %broadcast_add_fusion.own_ref, s32[4]{0:T(128)} %copy-done.2, s32[1]{0:T(128)} %max.7.part_ref, ...), custom_call_target="tpu_custom_call" | custom-call | flops 226492416 | bytes 1327104 | tf_op jit(solution)/shard_map/cond/branch_1_fun/residual/pallas_call | solution.py:201
  134.0 7.0 %collective-permute-done.7.refs_2_ = bf16[432,256]{1,0:T(8,128)(2,1)S(1)} collective-permute-done((bf16[432,256]{1,0:T(8,128)(2,1)S(1)}, bf16[432,256]{1,0:T(8,128)(2,1)S(1)}, u32[]{:S(2)}, u32[]{:S(2)}) %collective-permute-start.7) | collective-permute-done | bytes 221216 | tf_op jit(solution)/shard_map/cond/branch_1_fun/ppermute | solution.py:115
  140.9 7.8 %collective-permute-done.9.refs_5_ = bf16[1728,512]{1,0:T(8,128)(2,1)} collective-permute-done((bf16[1728,512]{1,0:T(8,128)(2,1)}, bf16[1728,512]{1,0:T(8,128)(2,1)}, u32[]{:S(2)}, u32[]{:S(2)}) %collective-permute-start.9) | collective-permute-done | bytes 1769504 | tf_op jit(solution)/shard_map/cond/branch_1_fun/ppermute | solution.py:115
  148.8 3.3 %collective-permute-start.10 = (bf16[432,256]{1,0:T(8,128)(2,1)}, bf16[432,256]{1,0:T(8,128)(2,1)S(1)}, u32[]{:S(2)}, u32[]{:S(2)}) collective-permute-start(bf16[432,256]{1,0:T(8,128)(2,1)} %get-tuple-element.99), channel_id=1, source_target_pairs={{0,12},{2,14},{4,0},{6,2},{8,4},{10,6},{12,8},{14,10},{1,13},{3,15... | collective-permute-start | bytes 663560 | tf_op jit(solution)/shard_map/cond/branch_1_fun/ppermute | solution.py:115
  153.7 10.2 %residual.3 = (bf16[432,256]{1,0:T(8,128)(2,1)}, bf16[432,256]{1,0:T(8,128)(2,1)}, bf16[432,256]{1,0:T(8,128)(2,1)}, bf16[432,256]{1,0:T(8,128)(2,1)}, f32[256,512]{1,0:T(8,128)}, /*index=5*/f32[256,512]{1,0:T(8,128)}) custom-call(s32[4]{0:T(128)} %broadcast_add_fusion.1.own_ref, s32[4]{0:T(128)} %copy-done.2, s32[1]{0:T(128)} %max.7.part_ref, ...), custom_call_target="tpu_custom_call" | custom-call | flops 226492416 | bytes 1327104 | tf_op jit(solution)/shard_map/cond/branch_1_fun/residual/pallas_call | solution.py:201
  163.9 7.3 %collective-permute-done.11 = bf16[432,256]{1,0:T(8,128)(2,1)} collective-permute-done((bf16[432,256]{1,0:T(8,128)(2,1)}, bf16[432,256]{1,0:T(8,128)(2,1)}, u32[]{:S(2)}, u32[]{:S(2)}) %collective-permute-start.11) | collective-permute-done | bytes 221216 | tf_op jit(solution)/shard_map/cond/branch_1_fun/ppermute | solution.py:115
  174.7 2.6 %collective-permute-start.14 = (bf16[432,256]{1,0:T(8,128)(2,1)}, bf16[432,256]{1,0:T(8,128)(2,1)S(1)}, u32[]{:S(2)}, u32[]{:S(2)}) collective-permute-start(bf16[432,256]{1,0:T(8,128)(2,1)} %get-tuple-element.105), channel_id=1, source_target_pairs={{0,8},{2,10},{4,12},{6,14},{8,0},{10,2},{12,4},{14,6},{1,9},{3,11}... | collective-permute-start | bytes 663560 | tf_op jit(solution)/shard_map/cond/branch_1_fun/ppermute | solution.py:115
  182.7 15.1 %collective-permute-done.14 = bf16[432,256]{1,0:T(8,128)(2,1)S(1)} collective-permute-done((bf16[432,256]{1,0:T(8,128)(2,1)}, bf16[432,256]{1,0:T(8,128)(2,1)S(1)}, u32[]{:S(2)}, u32[]{:S(2)}) %collective-permute-start.14) | collective-permute-done | bytes 221216 | tf_op jit(solution)/shard_map/cond/branch_1_fun/ppermute | solution.py:115
  201.6 3.6 %collective-permute-start.25 = (f32[128,128]{1,0:T(8,128)S(1)}, f32[128,128]{1,0:T(8,128)S(1)}, u32[]{:S(2)}, u32[]{:S(2)}) collective-permute-start(f32[128,128]{1,0:T(8,128)S(1)} %get-tuple-element.170), channel_id=1, source_target_pairs={{0,14},{2,12},{4,2},{6,0},{8,6},{10,4},{12,10},{14,8},{1,15},{3,13... | collective-permute-start | bytes 196616 | tf_op jit(solution)/shard_map/cond/branch_1_fun/ppermute | solution.py:115
  208.4 2.2 collective-permute-start.21
  210.6 2.2 collective-permute-start.20
  214.4 2.8 %collective-permute-done.20 = f32[128,128]{1,0:T(8,128)S(1)} collective-permute-done((f32[128,128]{1,0:T(8,128)S(1)}, f32[128,128]{1,0:T(8,128)S(1)}, u32[]{:S(2)}, u32[]{:S(2)}) %collective-permute-start.20) | collective-permute-done | bytes 65568 | tf_op jit(solution)/shard_map/cond/branch_1_fun/ppermute | solution.py:115
  (118 shorter events, 46.4 us)
Async XLA Ops:
  11.6 32.1 %collective-permute-start.32 = (bf16[256,512]{1,0:T(8,128)(2,1)}, bf16[256,512]{1,0:T(8,128)(2,1)}, u32[]{:S(2)}, u32[]{:S(2)}) collective-permute-start(bf16[256,512]{1,0:T(8,128)(2,1)} %param.11), channel_id=1, source_target_pairs={{0,2},{2,0},{4,6},{6,4},{8,10},{10,8},{12,14},{14,12},{1,3},{3,1},... | collective-permute-start | bytes 786440 | tf_op jit(solution)/shard_map/ppermute | solution.py:115
  16.1 27.6 %collective-permute-start.31 = (bf16[2,128,256]{2,1,0:T(8,128)(2,1)}, bf16[2,128,256]{2,1,0:T(8,128)(2,1)}, u32[]{:S(2)}, u32[]{:S(2)}) collective-permute-start(bf16[2,128,256]{2,1,0:T(8,128)(2,1)} %pad_maximum_fusion.1), channel_id=1, source_target_pairs={{0,12},{2,14},{4,0},{6,2},{8,4},{10,6},{12,8},{14,10},{1,13},{3,15... | collective-permute-start | bytes 393224 | tf_op jit(solution)/shard_map/ppermute | solution.py:115
  20.1 23.5 %collective-permute-start.30 = (bf16[2,128,256]{2,1,0:T(8,128)(2,1)}, bf16[2,128,256]{2,1,0:T(8,128)(2,1)}, u32[]{:S(2)}, u32[]{:S(2)}) collective-permute-start(bf16[2,128,256]{2,1,0:T(8,128)(2,1)} %pad_maximum_fusion.1), channel_id=1, source_target_pairs={{0,8},{2,10},{4,12},{6,14},{8,0},{10,2},{12,4},{14,6},{1,9},{3,11}... | collective-permute-start | bytes 393224 | tf_op jit(solution)/shard_map/ppermute | solution.py:115
  20.1 23.5 %collective-permute-start.29 = (bf16[2,128,256]{2,1,0:T(8,128)(2,1)}, bf16[2,128,256]{2,1,0:T(8,128)(2,1)}, u32[]{:S(2)}, u32[]{:S(2)}) collective-permute-start(bf16[2,128,256]{2,1,0:T(8,128)(2,1)} %pad_maximum_fusion.1), channel_id=1, source_target_pairs={{0,4},{2,6},{4,8},{6,10},{8,12},{10,14},{12,0},{14,2},{1,5},{3,7},... | collective-permute-start | bytes 393224 | tf_op jit(solution)/shard_map/ppermute | solution.py:115
  22.5 19.3 %collective-permute-start.28 = (s32[2]{0:T(128)S(1)}, s32[2]{0:T(128)S(1)}, u32[]{:S(2)}, u32[]{:S(2)}) collective-permute-start(s32[2]{0:T(128)S(1)} %pad_add_fusion.1), channel_id=1, source_target_pairs={{0,16},{16,0},{1,17},{17,1},{2,18},{18,2},{3,19},{19,3},{4,20},{20... | collective-permute-start | bytes 32 | tf_op jit(solution)/shard_map/ppermute | solution.py:383
  45.5 33.1 %collective-permute-start.1 = (bf16[3456,512]{1,0:T(8,128)(2,1)}, bf16[3456,512]{1,0:T(8,128)(2,1)}, u32[]{:S(2)}, u32[]{:S(2)}) collective-permute-start(bf16[3456,512]{1,0:T(8,128)(2,1)} %get-tuple-element.66), channel_id=1, source_target_pairs={{0,1},{1,0},{2,3},{3,2},{4,5},{5,4},{6,7},{7,6},{8,9},{9,8},{10,11... | collective-permute-start | bytes 10616840 | tf_op jit(solution)/shard_map/cond/branch_1_fun/ppermute | solution.py:279
  45.5 9.7 %collective-permute-start = (bf16[3456,128]{1,0:T(8,128)(2,1)}, bf16[3456,128]{1,0:T(8,128)(2,1)S(1)}, u32[]{:S(2)}, u32[]{:S(2)}) collective-permute-start(bf16[3456,128]{1,0:T(8,128)(2,1)} %get-tuple-element.59), channel_id=1, source_target_pairs={{0,1},{1,0},{2,3},{3,2},{4,5},{5,4},{6,7},{7,6},{8,9},{9,8},{10,11... | collective-permute-start | bytes 2654216 | tf_op jit(solution)/shard_map/cond/branch_1_fun/ppermute | solution.py:278
  46.0 27.7 %all-to-all-start = ((bf16[8,432,128]{2,1,0:T(8,128)(2,1)}), bf16[8,432,128]{2,1,0:T(8,128)(2,1)S(1)}, u32[]{:S(2)}, u32[]{:S(2)}) async-start(bf16[8,432,128]{2,1,0:T(8,128)(2,1)} %get-tuple-element.57), calls=%async_computation | async-start | bytes 1769472 | tf_op jit(solution)/shard_map/cond/branch_1_fun/all_to_all | solution.py:291
  51.3 72.8 %collective-permute-start.5 = (bf16[1728,512]{1,0:T(8,128)(2,1)}, bf16[1728,512]{1,0:T(8,128)(2,1)}, u32[]{:S(2)}, u32[]{:S(2)}) collective-permute-start(bf16[1728,512]{1,0:T(8,128)(2,1)} %get-tuple-element.79), channel_id=1, source_target_pairs={{0,2},{2,0},{4,6},{6,4},{8,10},{10,8},{12,14},{14,12},{1,3},{3,1},... | collective-permute-start | bytes 5308424 | tf_op jit(solution)/shard_map/cond/branch_1_fun/ppermute | solution.py:115
  73.8 38.2 %all-to-all-start.1 = ((bf16[8,432,128]{2,1,0:T(8,128)(2,1)}), bf16[8,432,128]{2,1,0:T(8,128)(2,1)S(1)}, u32[]{:S(2)}, u32[]{:S(2)}) async-start(bf16[8,432,128]{2,1,0:T(8,128)(2,1)} %bitcast.76), calls=%async_computation.1 | async-start | bytes 1769472 | tf_op jit(solution)/shard_map/cond/branch_1_fun/all_to_all | solution.py:291
  82.5 66.3 %collective-permute-start.9 = (bf16[1728,512]{1,0:T(8,128)(2,1)}, bf16[1728,512]{1,0:T(8,128)(2,1)}, u32[]{:S(2)}, u32[]{:S(2)}) collective-permute-start(bf16[1728,512]{1,0:T(8,128)(2,1)} %dynamic-slice_select_fusion), channel_id=1, source_target_pairs={{0,2},{2,0},{4,6},{6,4},{8,10},{10,8},{12,14},{14,12},{1,3},{3,1},... | collective-permute-start | bytes 5308424 | tf_op jit(solution)/shard_map/cond/branch_1_fun/ppermute | solution.py:115
  84.5 27.4 %collective-permute-start.4 = (bf16[432,256]{1,0:T(8,128)(2,1)S(1)}, bf16[432,256]{1,0:T(8,128)(2,1)S(1)}, u32[]{:S(2)}, u32[]{:S(2)}) collective-permute-start(bf16[432,256]{1,0:T(8,128)(2,1)S(1)} %latent.2.refs_0_), channel_id=1, source_target_pairs={{0,12},{2,14},{4,0},{6,2},{8,4},{10,6},{12,8},{14,10},{1,13},{3,15... | collective-permute-start | bytes 663560 | tf_op jit(solution)/shard_map/cond/branch_1_fun/ppermute | solution.py:115
  87.8 31.0 %collective-permute-start.3 = (bf16[432,256]{1,0:T(8,128)(2,1)S(1)}, bf16[432,256]{1,0:T(8,128)(2,1)S(1)}, u32[]{:S(2)}, u32[]{:S(2)}) collective-permute-start(bf16[432,256]{1,0:T(8,128)(2,1)S(1)} %latent.2.refs_0_), channel_id=1, source_target_pairs={{0,8},{2,10},{4,12},{6,14},{8,0},{10,2},{12,4},{14,6},{1,9},{3,11}... | collective-permute-start | bytes 663560 | tf_op jit(solution)/shard_map/cond/branch_1_fun/ppermute | solution.py:115
  87.8 31.7 %collective-permute-start.2 = (bf16[432,256]{1,0:T(8,128)(2,1)S(1)}, bf16[432,256]{1,0:T(8,128)(2,1)S(1)}, u32[]{:S(2)}, u32[]{:S(2)}) collective-permute-start(bf16[432,256]{1,0:T(8,128)(2,1)S(1)} %latent.2.refs_0_), channel_id=1, source_target_pairs={{0,4},{2,6},{4,8},{6,10},{8,12},{10,14},{12,0},{14,2},{1,5},{3,7},... | collective-permute-start | bytes 663560 | tf_op jit(solution)/shard_map/cond/branch_1_fun/ppermute | solution.py:115
  121.4 12.6 %collective-permute-start.8 = (bf16[432,256]{1,0:T(8,128)(2,1)S(1)}, bf16[432,256]{1,0:T(8,128)(2,1)S(1)}, u32[]{:S(2)}, u32[]{:S(2)}) collective-permute-start(bf16[432,256]{1,0:T(8,128)(2,1)S(1)} %latent.3.refs_0_), channel_id=1, source_target_pairs={{0,12},{2,14},{4,0},{6,2},{8,4},{10,6},{12,8},{14,10},{1,13},{3,15... | collective-permute-start | bytes 663560 | tf_op jit(solution)/shard_map/cond/branch_1_fun/ppermute | solution.py:115
  121.4 19.5 %collective-permute-start.7 = (bf16[432,256]{1,0:T(8,128)(2,1)S(1)}, bf16[432,256]{1,0:T(8,128)(2,1)S(1)}, u32[]{:S(2)}, u32[]{:S(2)}) collective-permute-start(bf16[432,256]{1,0:T(8,128)(2,1)S(1)} %latent.3.refs_0_), channel_id=1, source_target_pairs={{0,8},{2,10},{4,12},{6,14},{8,0},{10,2},{12,4},{14,6},{1,9},{3,11}... | collective-permute-start | bytes 663560 | tf_op jit(solution)/shard_map/cond/branch_1_fun/ppermute | solution.py:115
  121.5 19.4 %collective-permute-start.6 = (bf16[432,256]{1,0:T(8,128)(2,1)S(1)}, bf16[432,256]{1,0:T(8,128)(2,1)S(1)}, u32[]{:S(2)}, u32[]{:S(2)}) collective-permute-start(bf16[432,256]{1,0:T(8,128)(2,1)S(1)} %latent.3.refs_0_), channel_id=1, source_target_pairs={{0,4},{2,6},{4,8},{6,10},{8,12},{10,14},{12,0},{14,2},{1,5},{3,7},... | collective-permute-start | bytes 663560 | tf_op jit(solution)/shard_map/cond/branch_1_fun/ppermute | solution.py:115
  148.8 15.2 %collective-permute-start.10 = (bf16[432,256]{1,0:T(8,128)(2,1)}, bf16[432,256]{1,0:T(8,128)(2,1)S(1)}, u32[]{:S(2)}, u32[]{:S(2)}) collective-permute-start(bf16[432,256]{1,0:T(8,128)(2,1)} %get-tuple-element.99), channel_id=1, source_target_pairs={{0,12},{2,14},{4,0},{6,2},{8,4},{10,6},{12,8},{14,10},{1,13},{3,15... | collective-permute-start | bytes 663560 | tf_op jit(solution)/shard_map/cond/branch_1_fun/ppermute | solution.py:115
  152.0 19.2 %collective-permute-start.11 = (bf16[432,256]{1,0:T(8,128)(2,1)}, bf16[432,256]{1,0:T(8,128)(2,1)}, u32[]{:S(2)}, u32[]{:S(2)}) collective-permute-start(bf16[432,256]{1,0:T(8,128)(2,1)} %get-tuple-element.100), channel_id=1, source_target_pairs={{0,8},{2,10},{4,12},{6,14},{8,0},{10,2},{12,4},{14,6},{1,9},{3,11}... | collective-permute-start | bytes 663560 | tf_op jit(solution)/shard_map/cond/branch_1_fun/ppermute | solution.py:115
  152.0 19.2 %collective-permute-start.12 = (bf16[432,256]{1,0:T(8,128)(2,1)}, bf16[432,256]{1,0:T(8,128)(2,1)}, u32[]{:S(2)}, u32[]{:S(2)}) collective-permute-start(bf16[432,256]{1,0:T(8,128)(2,1)} %get-tuple-element.101), channel_id=1, source_target_pairs={{0,4},{2,6},{4,8},{6,10},{8,12},{10,14},{12,0},{14,2},{1,5},{3,7},... | collective-permute-start | bytes 663560 | tf_op jit(solution)/shard_map/cond/branch_1_fun/ppermute | solution.py:115
  174.7 23.1 %collective-permute-start.14 = (bf16[432,256]{1,0:T(8,128)(2,1)}, bf16[432,256]{1,0:T(8,128)(2,1)S(1)}, u32[]{:S(2)}, u32[]{:S(2)}) collective-permute-start(bf16[432,256]{1,0:T(8,128)(2,1)} %get-tuple-element.105), channel_id=1, source_target_pairs={{0,8},{2,10},{4,12},{6,14},{8,0},{10,2},{12,4},{14,6},{1,9},{3,11}... | collective-permute-start | bytes 663560 | tf_op jit(solution)/shard_map/cond/branch_1_fun/ppermute | solution.py:115
  177.3 20.5 %collective-permute-start.15 = (bf16[432,256]{1,0:T(8,128)(2,1)}, bf16[432,256]{1,0:T(8,128)(2,1)S(1)}, u32[]{:S(2)}, u32[]{:S(2)}) collective-permute-start(bf16[432,256]{1,0:T(8,128)(2,1)} %get-tuple-element.106), channel_id=1, source_target_pairs={{0,4},{2,6},{4,8},{6,10},{8,12},{10,14},{12,0},{14,2},{1,5},{3,7},... | collective-permute-start | bytes 663560 | tf_op jit(solution)/shard_map/cond/branch_1_fun/ppermute | solution.py:115
  180.5 17.5 %collective-permute-start.17 = (f32[128,512]{1,0:T(8,128)S(1)}, f32[128,512]{1,0:T(8,128)S(1)}, u32[]{:S(2)}, u32[]{:S(2)}) collective-permute-start(f32[128,512]{1,0:T(8,128)S(1)} %slice_bitcast_fusion), channel_id=1, source_target_pairs={{0,2},{2,0},{4,6},{6,4},{8,10},{10,8},{12,14},{14,12},{1,3},{3,1},... | collective-permute-start | bytes 786440 | tf_op jit(solution)/shard_map/cond/branch_1_fun/ppermute | solution.py:115
  201.6 8.9 %collective-permute-start.25 = (f32[128,128]{1,0:T(8,128)S(1)}, f32[128,128]{1,0:T(8,128)S(1)}, u32[]{:S(2)}, u32[]{:S(2)}) collective-permute-start(f32[128,128]{1,0:T(8,128)S(1)} %get-tuple-element.170), channel_id=1, source_target_pairs={{0,14},{2,12},{4,2},{6,0},{8,6},{10,4},{12,10},{14,8},{1,15},{3,13... | collective-permute-start | bytes 196616 | tf_op jit(solution)/shard_map/cond/branch_1_fun/ppermute | solution.py:115
  (29 other events, 495.0 us)

commit v3 on v2

--- a/solution.py
+++ b/solution.py
@@ -20,13 +20,24 @@
     return lax.dot_general(a, b, (dims, ((), ())), preferred_element_type=F32)
 
 
-def compact_kernel(group, cap, extra, rows, shards, first_ref, pair_ref, mask_ref, cells_ref, targets_ref, *refs):
-    (late_ref, early_ref, over_ref, main_ref, pair_out_ref, far_ref, cells_all, targets_all, sems) = refs
+def compact_kernel(
+    group, cap, extra, rows, shards, known, first_ref, pair_ref, mask_ref, cells_ref, targets_ref, *refs
+):
+    counts, refs = [ref[0] for ref in refs[:known]], refs[known:]
+    (facts_ref, late_ref, early_ref, over_ref, main_ref, pair_out_ref, far_ref, cells_all, targets_all, sems) = refs
     step = pl.program_id(0)
     arrays = ((cells_ref, cells_all), (targets_ref, targets_all))
 
     @pl.when(step == 0)
     def _():
+        fits = jnp.int32(1)
+        for one, two in zip(counts[::2], counts[1::2]):
+            low, high = jnp.minimum(one, two), jnp.maximum(one, two)
+            fits = jnp.where((low + jnp.maximum(high - cap, 0) <= cap) & (high - cap <= extra), fits, 0)
+        facts_ref[0] = fits
+        facts_ref[1] = jnp.maximum(counts[1] - cap, 0)
+        facts_ref[2] = counts[0] + counts[1]
+
         def clear(i, carry):
             for _, out_ref in arrays:
                 out_ref[pl.ds(pl.multiple_of(i * BLOCK, BLOCK), BLOCK), :] = jnp.zeros(
@@ -76,7 +87,7 @@
             copy.wait()
 
 
-def compact(firsts, pair_at, mask_blocks, cells, targets, cap, extra, shards):
+def compact(firsts, pair_at, mask_blocks, cells, targets, counts, cap, extra, shards):
     rows = -(-(cap + extra + 2 * BLOCK) // BLOCK) * BLOCK
     blocks = mask_blocks.shape[0]
     group = max(g for g in range(1, GROUP + 1) if blocks % g == 0)
@@ -84,20 +95,23 @@
     shapes = [(shards, extra // shards, width), (extra, width), (extra, width)]
     shapes += [(cap, columns), (extra // 2, columns), (extra, columns)]
     return pl.pallas_call(
-        functools.partial(compact_kernel, group, cap, extra, rows, shards),
+        functools.partial(compact_kernel, group, cap, extra, rows, shards, len(counts)),
         grid_spec=pltpu.PrefetchScalarGridSpec(
             num_scalar_prefetch=2,
             grid=(blocks // group,),
             in_specs=[pl.BlockSpec((1, group, BLOCK), lambda i, f, p: (i, 0, 0))]
-            + [pl.BlockSpec((group * BLOCK, w), lambda i, f, p: (i, 0)) for w in (width, columns)],
-            out_specs=[pl.BlockSpec(memory_space=pl.ANY)] * len(shapes),
+            + [pl.BlockSpec((group * BLOCK, w), lambda i, f, p: (i, 0)) for w in (width, columns)]
+            + [pl.BlockSpec(memory_space=pltpu.SMEM)] * len(counts),
+            out_specs=[pl.BlockSpec(memory_space=pltpu.SMEM)]
+            + [pl.BlockSpec(memory_space=pl.ANY)] * len(shapes),
             scratch_shapes=[
                 pltpu.VMEM((rows, width), BF16),
                 pltpu.VMEM((rows, columns), BF16),
                 pltpu.SemaphoreType.DMA((shards + 5,)),
             ],
         ),
-        out_shape=[jax.ShapeDtypeStruct(shape, BF16) for shape in shapes],
+        out_shape=[jax.ShapeDtypeStruct((3,), jnp.int32)]
+        + [jax.ShapeDtypeStruct(shape, BF16) for shape in shapes],
         compiler_params=pltpu.CompilerParams(vmem_limit_bytes=40 * MIB),
         cost_estimate=pl.CostEstimate(
             flops=2 * (BLOCK + SUB) * blocks * BLOCK * (width + columns),
@@ -105,7 +119,7 @@
             transcendentals=0,
         ),
         name="compact",
-    )(firsts, pair_at.reshape(1), mask_blocks.reshape(-1, group, BLOCK), cells, targets)
+    )(firsts, pair_at.reshape(1), mask_blocks.reshape(-1, group, BLOCK), cells, targets, *counts)
 
 
 SWAP = [(0, 1), (1, 0)]
@@ -153,8 +167,9 @@
     latents, refs = refs[:count], refs[count:]
     targets_ref, far_targets_ref, refs = refs[0], refs[1], refs[2:]
     if mixed:
-        other_ref, refs = refs[0], refs[1:]
-    terms, (out_ref, far_out_ref, held) = refs[:count], refs[count:]
+        other_ref, first_ref, first_far_ref, refs = *refs[:3], refs[3:]
+    terms, (out_ref, far_out_ref, held, *sums) = refs[:count], refs[count:]
+    total_ref, far_total_ref = sums if mixed else (out_ref, far_out_ref)
     rows = targets_ref.shape[0]
 
     for s in range(count):
@@ -165,8 +180,8 @@
 
     @pl.when(slot == 0)
     def _():
-        out_ref[...] = jnp.zeros_like(out_ref)
-        far_out_ref[...] = jnp.zeros_like(far_out_ref)
+        total_ref[...] = first_ref[...] if mixed else jnp.zeros_like(total_ref)
+        far_total_ref[...] = first_far_ref[...] if mixed else jnp.zeros_like(far_total_ref)
 
     latent = held[...]
     targets = targets_ref[...].astype(F32)
@@ -186,16 +201,26 @@
         def _():
             terms[s][...] = total
 
-    out_ref[...] += dot(latent, residual, ((0,), (0,)))
-    far_out_ref[...] += dot(latent, far_residual, ((0,), (0,)))
-
-
-def residual_of(own_at, pair_at, received, scale, weights, factors, latents, own, pair, other):
+    total_ref[...] += dot(latent, residual, ((0,), (0,)))
+    far_total_ref[...] += dot(latent, far_residual, ((0,), (0,)))
+    if mixed:
+
+        @pl.when(slot == count - 1)
+        def _():
+            half = total_ref.shape[0] // 2
+            for out, at in ((out_ref, part_ref[1] * half), (far_out_ref, (1 - part_ref[1]) * half)):
+                at = pl.multiple_of(at, half)
+                out[0] = total_ref[pl.ds(at, half), :]
+                out[1] = far_total_ref[pl.ds(at, half), :]
+
+
+def residual_of(own_at, pair_at, part, scale, weights, factors, latents, own, pair, other=()):
     count = len(latents)
     rows, rank = latents[0].shape
     width = own.shape[1]
-    mixed = other is not None
-    whole = lambda shape: pl.BlockSpec(shape, lambda i, o, p, r: (0, 0))
+    mixed = len(other) > 0
+    whole = lambda shape: pl.BlockSpec(shape, lambda i, o, p, r: (0,) * len(shape))
+    out = (2, rank // 2, width) if mixed else (rank, width)
     by_own = pl.BlockSpec((rows, width), lambda i, o, p, r: (o[i], 0))
     by_pair = pl.BlockSpec((rows, width), lambda i, o, p, r: (p[i], 0))
     result = pl.pallas_call(
@@ -208,12 +233,12 @@
             + [whole((rank, width))] * 2
             + [whole((rows, rank))] * count
             + [by_own, by_pair]
-            + [by_own] * mixed,
-            out_specs=[whole((rows, rank))] * count + [whole((rank, width))] * 2,
-            scratch_shapes=[pltpu.VMEM((rows, rank), BF16)],
+            + ([by_own] + [whole((rank, width))] * 2) * mixed,
+            out_specs=[whole((rows, rank))] * count + [whole(out)] * 2,
+            scratch_shapes=[pltpu.VMEM((rows, rank), BF16)] + [pltpu.VMEM((rank, width), F32)] * (2 * mixed),
         ),
         out_shape=[jax.ShapeDtypeStruct((rows, rank), BF16)] * count
-        + [jax.ShapeDtypeStruct((rank, width), F32)] * 2,
+        + [jax.ShapeDtypeStruct(out, F32)] * 2,
         compiler_params=pltpu.CompilerParams(vmem_limit_bytes=56 * MIB),
         cost_estimate=pl.CostEstimate(
             flops=count * rows * rank * width,
@@ -222,8 +247,8 @@
         ),
         name="residual",
     )(
-        own_at, pair_at, received, scale.reshape(1, 1), *[w.reshape(1, -1) for w in weights], *factors,
-        *latents, own, pair, *([other] * mixed),
+        own_at, pair_at, part, scale.reshape(1, 1), *[w.reshape(1, -1) for w in weights], *factors,
+        *latents, own, pair, *other,
     )
     return result[:count], result[count], result[count + 1]
 
@@ -303,10 +328,10 @@
     cells[0], latents[1] = lax.optimization_barrier((cells[0], latents[1]))
     latents[0] = along_line(latent_of(y, slot_z, cells[0], whole_in))
 
-    def residual(chunk):
+    def residual(chunk, *other):
         return residual_of(
-            slot_z + (chunk * 2 + y) * count, slot_z, received, scale, weights, factors,
-            latents[chunk], own_targets, pairs[chunk], other_targets if chunk == 0 else None,
+            slot_z + (chunk * 2 + y) * count, slot_z, jnp.concatenate([received, tile.reshape(1)]),
+            scale, weights, factors, latents[chunk], own_targets, pairs[chunk], other,
         )
 
     def summed(terms):
@@ -315,16 +340,15 @@
             total = total + send(terms[s], shifted(count, -s, 0)).astype(F32)
         return total.astype(BF16)
 
-    late_parts, latents[0], pairs[0] = lax.optimization_barrier((residual(1), latents[0], pairs[0]))
-    grads = {1: summed(late_parts[0])}
-    early_parts, grads[1] = lax.optimization_barrier((residual(0), grads[1]))
+    late_parts, latents[0] = lax.optimization_barrier((residual(1), latents[0]))
+    terms = list(late_parts[0])
+    terms[count // 2], pairs[0] = lax.optimization_barrier((terms[count // 2], pairs[0]))
+    grads = {1: summed(terms)}
+    early_parts, grads[1] = lax.optimization_barrier(
+        (residual(0, other_targets, *late_parts[1:]), grads[1])
+    )
     grads[0] = summed(early_parts[0])
-    own_part, far_part = late_parts[1] + early_parts[1], late_parts[2] + early_parts[2]
-    out_part = jnp.stack([own_part, far_part])
-    half = out_part.shape[1] // 2
-    out_half = lax.dynamic_slice_in_dim(out_part, tile * half, half, axis=1) + lax.ppermute(
-        lax.dynamic_slice_in_dim(out_part, (1 - tile) * half, half, axis=1), "tile", SWAP
-    )
+    out_half = early_parts[1] + lax.ppermute(early_parts[2], "tile", SWAP)
     grad_out = out_half[0] + send(out_half[1], shifted(count, 0, 1))
     grads[0], grad_out = lax.optimization_barrier((grads[0], grad_out))
     keep, passed = in_of(tile, [cells[c] for c in order], [grads[c] for c in order])
@@ -376,35 +400,34 @@
     firsts = jnp.maximum(cap - land, 0) + jnp.sum(
         jnp.where(at[None, :] < at[:, None], in_block[None, :], 0), axis=1
     )
-    other = lax.ppermute(land, "tile", SWAP)
-    firsts, mask_blocks, other, pair_in = lax.optimization_barrier((firsts, mask_blocks, other, pair_in))
-    counts = [jnp.concatenate([land, other])]
-    counts += [
-        lax.ppermute(counts[0], "groups", [(a, (a + g) % groups) for a in range(groups)]) for g in range(1, groups)
-    ]
+    counts = []
+    for g in range(groups):
+        for t in (0, 1):
+            moves = [(2 * a + b, (a + g) % groups * 2 + (b ^ t)) for a in range(groups) for b in (0, 1)]
+            counts.append(lax.ppermute(land, ("groups", "tile"), moves) if g + t else land)
+    firsts, mask_blocks, counts, pair_in, weights = lax.optimization_barrier(
+        (firsts, mask_blocks, counts, pair_in, weights)
+    )
     line_in = [pair_in] + [send(pair_in, shifted(shards // 2, s, 0)) for s in range(1, shards // 2)]
     factors = (factor_out, send(factor_out, shifted(shards // 2, 0, 1)))
-    kept = compact(firsts, extra + (1 - y) * (extra // 2), mask_blocks, embeddings, targets, cap, extra, shards)
-    kept, counts, line_in, factors = lax.optimization_barrier((kept, counts, line_in, factors))
-    counts = jnp.stack(counts)
-    low, high = jnp.min(counts, axis=1), jnp.max(counts, axis=1)
-    fits = jnp.all((low + jnp.maximum(high - cap, 0) <= cap) & (high - cap <= extra))
-    land_total = (land + other)[0].astype(F32)
-    received = jnp.maximum(other - cap, 0)
+    facts, *kept = compact(
+        firsts, extra + (1 - y) * (extra // 2), mask_blocks, embeddings, targets, counts, cap, extra, shards
+    )
+    facts, kept, line_in, factors = lax.optimization_barrier((facts, kept, line_in, factors))
 
     def few():
         return compacted_gradients(
-            *kept, received, jnp.stack(line_in, axis=1), factors, weights, land_total
+            *kept, facts[1:2], jnp.stack(line_in, axis=1), factors, weights, facts[2].astype(F32)
         )
 
     def full():
         is_land = land_mask[:, None] > 0
         return full_gradients(
             jnp.where(is_land, embeddings, 0), jnp.where(is_land, targets, 0),
-            factor_in, factor_out, target_weight, land_total,
+            factor_in, factor_out, target_weight, facts[2].astype(F32),
         )
 
-    return lax.cond(fits, few, full)
+    return lax.cond(facts[0] > 0, few, full)
 
 
 def solution(mesh):

time: 225 us -> 215 us (0.956)
  waiting for transfers between devices: 92.5 us -> 82.8 us
  Pallas kernels: 39.7 us -> 43.8 us
    ppermute x28, waiting for transfers between devices: 53 us -> 44.9 us  [send(): return lax.ppermute(x, 'tgt', moves)]
    pallas_call x1, Pallas kernels: 16.5 us -> 19.7 us  [compact(): pl.pallas_call(functools.partial(compact_kernel, group, cap, extra, rows,...]
    ppermute x28, starting transfers between devices: 39.5 us -> 36.6 us  [send(): return lax.ppermute(x, 'tgt', moves)]
  transfers between devices with their start and end apart: 36 -> 37, of which waited for: 15 -> 15; matrix products, arithmetic and copies ran while one was open for 7% -> 8% of each run, Pallas kernels for 17% -> 20%
where the time goes in v3:
time: 215 us; the launch traced here: 214 us
  waiting for transfers between devices  82.8 us (39%)
  starting transfers between devices  49 us (23%)
  Pallas kernels  43.8 us (20%)
  other arithmetic  18.9 us (9%)
  between operations  14.9 us (7%)
  local copies, waits for them, and re-layouts  3.55 us (2%)
    ppermute x28, waiting for transfers between devices, send(): return lax.ppermute(x, 'tgt', moves)  44.9 us
    ppermute x28, starting transfers between devices, send(): return lax.ppermute(x, 'tgt', moves)  36.6 us
    all_to_all x2, waiting for transfers between devices, owners_cells(): return lax.all_to_all(x, 'tgt', split_axis=0, concat_axis=0, tiled=True)  36.1 us
    pallas_call x2, Pallas kernels, residual_of(): pl.pallas_call(functools.partial(residual_kernel, count, mixed), grid_spe...  21 us
    pallas_call x1, Pallas kernels, compact(): pl.pallas_call(functools.partial(compact_kernel, group, cap, extra, rows,...  19.7 us
    all_to_all x2, starting transfers between devices, owners_cells(): return lax.all_to_all(x, 'tgt', split_axis=0, concat_axis=0, tiled=True)  8.63 us
    select_n x2, other arithmetic, merged(): return jnp.where(row < received[0], other, own)  6.71 us
  transfers between devices with their start and end apart: 37, of which 15 were waited for; matrix products, arithmetic and copies ran while one was open for 8% of the time, Pallas kernels for 20%

profile of v3, /device:TPU:0, one launch (start us, length us, event | category | flops | bytes accessed | tf_op | source)
XLA Modules:
  0.0 214.1 jit_solution(8254678166492793776)
XLA Ops:
  8.6 2.4 %collective-permute-start.28 = (s32[1]{0:T(128)}, s32[1]{0:T(128)}, u32[]{:S(2)}, u32[]{:S(2)}) collective-permute-start(s32[1]{0:T(128)} %bitcast.28.refs_0_), channel_id=1, source_target_pairs={{0,17},{1,16},{16,1},{17,0},{2,19},{3,18},{18,3},{19,2},{4,21},{5,... | collective-permute-start | bytes 20 | tf_op jit(solution)/shard_map/ppermute | solution.py:407
  15.4 2.5 %collective-permute-done.29 = bf16[128,256]{1,0:T(8,128)(2,1)S(1)} collective-permute-done((bf16[128,256]{1,0:T(8,128)(2,1)}, bf16[128,256]{1,0:T(8,128)(2,1)S(1)}, u32[]{:S(2)}, u32[]{:S(2)}) %collective-permute-start.29) | collective-permute-done | bytes 65568 | tf_op jit(solution)/shard_map/ppermute | solution.py:129
  19.1 3.9 %collective-permute-start.33 = (bf16[2,128,256]{2,1,0:T(8,128)(2,1)S(1)}, bf16[2,128,256]{2,1,0:T(8,128)(2,1)S(1)}, u32[]{:S(2)}, u32[]{:S(2)}) collective-permute-start(bf16[2,128,256]{2,1,0:T(8,128)(2,1)S(1)} %pad_maximum_fusion.1), channel_id=1, source_target_pairs={{0,12},{2,14},{4,0},{6,2},{8,4},{10,6},{12,8},{14,10},{1,13},{3,15... | collective-permute-start | bytes 393224 | tf_op jit(solution)/shard_map/ppermute | solution.py:129
  24.1 19.7 %compact.1 = (s32[3]{0:T(128)S(1)}, bf16[8,432,128]{2,1,0:T(8,128)(2,1)}, bf16[3456,128]{1,0:T(8,128)(2,1)}, bf16[3456,128]{1,0:T(8,128)(2,1)}, bf16[6912,512]{1...) custom-call(s32[52]{0:T(128)S(1)} %broadcast_add_fusion.2.first_ref, s32[1]{0:T(128)} %bitcast.32.pair_ref, ...), custom_call_target="tpu_custom_call" | custom-call | flops 4634705920 | bytes 31129600 | tf_op jit(solution)/shard_map/compact/pallas_call | solution.py:97
  43.8 163.4 %conditional.1 = (f32[128,128]{1,0:T(8,128)}, f32[128,512]{1,0:T(8,128)}) conditional(s32[]{:T(128)} %bitcast.33, (s32[13312]{0:T(1024)S(1)}, bf16[13312,128]{1,0:T(8,128)(2,1)S(1)}, bf16[128,256]{1,0:T(8,128)(2,1)}, bf16[256,512]{1,0:T(8,128)(2,1)}, bf16[13312,512]{1,0:T(8,128)(2,1)}, /*index=5*/s32[3]{0:T(128)S(1)}, f32[512]{0:T(512)S(1)}) %tuple.50, ...), branch_computations={%region_3.8_spmd, %region_8.9_spmd} | conditional | flops 12263240704 | bytes 233272640 | solution.py:430
  44.9 5.0 %all-to-all-start = ((bf16[8,432,128]{2,1,0:T(8,128)(2,1)}), bf16[8,432,128]{2,1,0:T(8,128)(2,1)S(1)}, u32[]{:S(2)}, u32[]{:S(2)}) async-start(bf16[8,432,128]{2,1,0:T(8,128)(2,1)} %get-tuple-element.51), calls=%async_computation | async-start | bytes 1769472 | tf_op jit(solution)/shard_map/cond/branch_1_fun/all_to_all | solution.py:316
  55.0 2.8 %broadcast_select_fusion.1 = bf16[3456,128]{1,0:T(8,128)(2,1)S(1)} fusion(bf16[3456,128]{1,0:T(8,128)(2,1)S(1)} %collective-permute-done, bf16[3456,128]{1,0:T(8,128)(2,1)} %get-tuple-element.54, pred[3456]{0:T(1024)(128)(4,1)S(1)} %iota_compare_fusion), kind=kLoop, calls=%fused_computation.6 | loop fusion | flops 442368 | bytes 2657664 | tf_op jit(solution)/shard_map/cond/branch_1_fun/jit(_where)/select_n | solution.py:309
  58.9 13.5 %all-to-all-done.cells_ref.refs_0_ = bf16[8,432,128]{2,1,0:T(8,128)(2,1)S(1)} async-done(((bf16[8,432,128]{2,1,0:T(8,128)(2,1)}), bf16[8,432,128]{2,1,0:T(8,128)(2,1)S(1)}, u32[]{:S(2)}, u32[]{:S(2)}) %all-to-all-start) | async-done | bytes 884768 | tf_op jit(solution)/shard_map/cond/branch_1_fun/all_to_all | solution.py:316
  72.3 3.6 %all-to-all-start.1 = ((bf16[8,432,128]{2,1,0:T(8,128)(2,1)}), bf16[8,432,128]{2,1,0:T(8,128)(2,1)S(1)}, u32[]{:S(2)}, u32[]{:S(2)}) async-start(bf16[8,432,128]{2,1,0:T(8,128)(2,1)} %bitcast.72), calls=%async_computation.1 | async-start | bytes 1769472 | tf_op jit(solution)/shard_map/cond/branch_1_fun/all_to_all | solution.py:316
  77.1 3.9 %dynamic-slice_select_fusion = bf16[1728,512]{1,0:T(8,128)(2,1)} fusion(bf16[6912,512]{1,0:T(8,128)(2,1)} %get-tuple-element.71.refs_4_, s32[]{:T(128)S(6)} %select_n.81, bf16[3456,512]{1,0:T(8,128)(2,1)} %collective-permute-done.1.refs_6_, s32[]{:T(128)S(6)} %select_n.80, pred[1728]{0:T(1024)(128)(4,1)S(1)} %add_compare_fusion), kind=kLoop, calls=%fused_computation.5 | loop fusion | flops 884736 | bytes 5310152 | tf_op jit(solution)/shard_map/cond/branch_1_fun/jit(_where)/select_n | solution.py:309
  83.0 3.3 %collective-permute-start.4 = (bf16[432,256]{1,0:T(8,128)(2,1)S(1)}, bf16[432,256]{1,0:T(8,128)(2,1)S(1)}, u32[]{:S(2)}, u32[]{:S(2)}) collective-permute-start(bf16[432,256]{1,0:T(8,128)(2,1)S(1)} %latent.2.refs_0_), channel_id=1, source_target_pairs={{0,12},{2,14},{4,0},{6,2},{8,4},{10,6},{12,8},{14,10},{1,13},{3,15... | collective-permute-start | bytes 663560 | tf_op jit(solution)/shard_map/cond/branch_1_fun/ppermute | solution.py:129
  88.0 22.6 %all-to-all-done.1.cells_ref.refs_1_ = bf16[8,432,128]{2,1,0:T(8,128)(2,1)S(1)} async-done(((bf16[8,432,128]{2,1,0:T(8,128)(2,1)}), bf16[8,432,128]{2,1,0:T(8,128)(2,1)S(1)}, u32[]{:S(2)}, u32[]{:S(2)}) %all-to-all-start.1) | async-done | bytes 884768 | tf_op jit(solution)/shard_map/cond/branch_1_fun/all_to_all | solution.py:316
  110.6 6.8 %collective-permute-done.3.refs_2_ = bf16[432,256]{1,0:T(8,128)(2,1)} collective-permute-done((bf16[432,256]{1,0:T(8,128)(2,1)S(1)}, bf16[432,256]{1,0:T(8,128)(2,1)}, u32[]{:S(2)}, u32[]{:S(2)}) %collective-permute-start.3) | collective-permute-done | bytes 221216 | tf_op jit(solution)/shard_map/cond/branch_1_fun/ppermute | solution.py:129
  122.8 9.8 %residual.2 = (bf16[432,256]{1,0:T(8,128)(2,1)}, bf16[432,256]{1,0:T(8,128)(2,1)}, bf16[432,256]{1,0:T(8,128)(2,1)}, bf16[432,256]{1,0:T(8,128)(2,1)}, f32[256,512]{1,0:T(8,128)}, /*index=5*/f32[256,512]{1,0:T(8,128)}) custom-call(s32[4]{0:T(128)} %broadcast_add_fusion.own_ref, s32[4]{0:T(128)} %copy-done.2, s32[2]{0:T(128)} %pad_add_fusion.part_ref, ...), custom_call_target="tpu_custom_call" | custom-call | flops 226492416 | bytes 1327104 | tf_op jit(solution)/shard_map/cond/branch_1_fun/residual/pallas_call | solution.py:226
  132.6 6.1 %collective-permute-done.7.refs_2_ = bf16[432,256]{1,0:T(8,128)(2,1)S(1)} collective-permute-done((bf16[432,256]{1,0:T(8,128)(2,1)S(1)}, bf16[432,256]{1,0:T(8,128)(2,1)S(1)}, u32[]{:S(2)}, u32[]{:S(2)}) %collective-permute-start.7) | collective-permute-done | bytes 221216 | tf_op jit(solution)/shard_map/cond/branch_1_fun/ppermute | solution.py:129
  139.5 2.0 collective-permute-start.12
  141.5 5.8 %collective-permute-done.9.refs_5_ = bf16[1728,512]{1,0:T(8,128)(2,1)} collective-permute-done((bf16[1728,512]{1,0:T(8,128)(2,1)}, bf16[1728,512]{1,0:T(8,128)(2,1)}, u32[]{:S(2)}, u32[]{:S(2)}) %collective-permute-start.9) | collective-permute-done | bytes 1769504 | tf_op jit(solution)/shard_map/cond/branch_1_fun/ppermute | solution.py:129
  147.3 2.4 %collective-permute-start.11 = (bf16[432,256]{1,0:T(8,128)(2,1)}, bf16[432,256]{1,0:T(8,128)(2,1)}, u32[]{:S(2)}, u32[]{:S(2)}) collective-permute-start(bf16[432,256]{1,0:T(8,128)(2,1)} %get-tuple-element.96), channel_id=1, source_target_pairs={{0,8},{2,10},{4,12},{6,14},{8,0},{10,2},{12,4},{14,6},{1,9},{3,11}... | collective-permute-start | bytes 663560 | tf_op jit(solution)/shard_map/cond/branch_1_fun/ppermute | solution.py:129
  150.2 11.2 %residual.3 = (bf16[432,256]{1,0:T(8,128)(2,1)}, bf16[432,256]{1,0:T(8,128)(2,1)}, bf16[432,256]{1,0:T(8,128)(2,1)}, bf16[432,256]{1,0:T(8,128)(2,1)}, f32[2,128,512]{2,1,0:T(8,128)}, /*index=5*/f32[2,128,512]{2,1,0:T(8,128)}) custom-call(s32[4]{0:T(128)} %broadcast_add_fusion.1.own_ref, s32[4]{0:T(128)} %copy-done.2, s32[2]{0:T(128)} %pad_add_fusion.part_ref, ...), custom_call_target="tpu_custom_call" | custom-call | flops 226492416 | bytes 1327104 | tf_op jit(solution)/shard_map/cond/branch_1_fun/residual/pallas_call | solution.py:226
  168.6 3.2 %collective-permute-done.13 = bf16[432,256]{1,0:T(8,128)(2,1)S(1)} collective-permute-done((bf16[432,256]{1,0:T(8,128)(2,1)}, bf16[432,256]{1,0:T(8,128)(2,1)S(1)}, u32[]{:S(2)}, u32[]{:S(2)}) %collective-permute-start.13) | collective-permute-done | bytes 221216 | tf_op jit(solution)/shard_map/cond/branch_1_fun/ppermute | solution.py:129
  171.8 14.2 %collective-permute-done.14 = bf16[432,256]{1,0:T(8,128)(2,1)S(1)} collective-permute-done((bf16[432,256]{1,0:T(8,128)(2,1)}, bf16[432,256]{1,0:T(8,128)(2,1)S(1)}, u32[]{:S(2)}, u32[]{:S(2)}) %collective-permute-start.14) | collective-permute-done | bytes 221216 | tf_op jit(solution)/shard_map/cond/branch_1_fun/ppermute | solution.py:129
  190.7 3.5 %collective-permute-start.25 = (f32[128,128]{1,0:T(8,128)S(1)}, f32[128,128]{1,0:T(8,128)S(1)}, u32[]{:S(2)}, u32[]{:S(2)}) collective-permute-start(f32[128,128]{1,0:T(8,128)S(1)} %get-tuple-element.172), channel_id=1, source_target_pairs={{0,14},{2,12},{4,2},{6,0},{8,6},{10,4},{12,10},{14,8},{1,15},{3,13... | collective-permute-start | bytes 196616 | tf_op jit(solution)/shard_map/cond/branch_1_fun/ppermute | solution.py:129
  197.4 3.0 %collective-permute-start.21 = (f32[128,128]{1,0:T(8,128)S(1)}, f32[128,128]{1,0:T(8,128)S(1)}, u32[]{:S(2)}, u32[]{:S(2)}) collective-permute-start(f32[128,128]{1,0:T(8,128)S(1)} %get-tuple-element.176), channel_id=1, source_target_pairs={{0,12},{2,14},{4,0},{6,2},{8,4},{10,6},{12,8},{14,10},{1,13},{3,15... | collective-permute-start | bytes 196616 | tf_op jit(solution)/shard_map/cond/branch_1_fun/ppermute | solution.py:129
  203.8 2.8 %collective-permute-done.20 = f32[128,128]{1,0:T(8,128)S(1)} collective-permute-done((f32[128,128]{1,0:T(8,128)S(1)}, f32[128,128]{1,0:T(8,128)S(1)}, u32[]{:S(2)}, u32[]{:S(2)}) %collective-permute-start.20) | collective-permute-done | bytes 65568 | tf_op jit(solution)/shard_map/cond/branch_1_fun/ppermute | solution.py:129
  (117 shorter events, 44.1 us)
Async XLA Ops:
  8.6 10.4 %collective-permute-start.28 = (s32[1]{0:T(128)}, s32[1]{0:T(128)}, u32[]{:S(2)}, u32[]{:S(2)}) collective-permute-start(s32[1]{0:T(128)} %bitcast.28.refs_0_), channel_id=1, source_target_pairs={{0,17},{1,16},{16,1},{17,0},{2,19},{3,18},{18,3},{19,2},{4,21},{5,... | collective-permute-start | bytes 20 | tf_op jit(solution)/shard_map/ppermute | solution.py:407
  17.9 25.8 %collective-permute-start.34 = (bf16[256,512]{1,0:T(8,128)(2,1)}, bf16[256,512]{1,0:T(8,128)(2,1)S(1)}, u32[]{:S(2)}, u32[]{:S(2)}) collective-permute-start(bf16[256,512]{1,0:T(8,128)(2,1)} %param.11), channel_id=1, source_target_pairs={{0,2},{2,0},{4,6},{6,4},{8,10},{10,8},{12,14},{14,12},{1,3},{3,1},... | collective-permute-start | bytes 786440 | tf_op jit(solution)/shard_map/ppermute | solution.py:129
  19.1 24.7 %collective-permute-start.33 = (bf16[2,128,256]{2,1,0:T(8,128)(2,1)S(1)}, bf16[2,128,256]{2,1,0:T(8,128)(2,1)S(1)}, u32[]{:S(2)}, u32[]{:S(2)}) collective-permute-start(bf16[2,128,256]{2,1,0:T(8,128)(2,1)S(1)} %pad_maximum_fusion.1), channel_id=1, source_target_pairs={{0,12},{2,14},{4,0},{6,2},{8,4},{10,6},{12,8},{14,10},{1,13},{3,15... | collective-permute-start | bytes 393224 | tf_op jit(solution)/shard_map/ppermute | solution.py:129
  23.0 20.8 %collective-permute-start.32 = (bf16[2,128,256]{2,1,0:T(8,128)(2,1)S(1)}, bf16[2,128,256]{2,1,0:T(8,128)(2,1)S(1)}, u32[]{:S(2)}, u32[]{:S(2)}) collective-permute-start(bf16[2,128,256]{2,1,0:T(8,128)(2,1)S(1)} %pad_maximum_fusion.1), channel_id=1, source_target_pairs={{0,8},{2,10},{4,12},{6,14},{8,0},{10,2},{12,4},{14,6},{1,9},{3,11}... | collective-permute-start | bytes 393224 | tf_op jit(solution)/shard_map/ppermute | solution.py:129
  23.0 20.8 %collective-permute-start.31 = (bf16[2,128,256]{2,1,0:T(8,128)(2,1)S(1)}, bf16[2,128,256]{2,1,0:T(8,128)(2,1)S(1)}, u32[]{:S(2)}, u32[]{:S(2)}) collective-permute-start(bf16[2,128,256]{2,1,0:T(8,128)(2,1)S(1)} %pad_maximum_fusion.1), channel_id=1, source_target_pairs={{0,4},{2,6},{4,8},{6,10},{8,12},{10,14},{12,0},{14,2},{1,5},{3,7},... | collective-permute-start | bytes 393224 | tf_op jit(solution)/shard_map/ppermute | solution.py:129
  44.1 33.0 %collective-permute-start.1 = (bf16[3456,512]{1,0:T(8,128)(2,1)}, bf16[3456,512]{1,0:T(8,128)(2,1)}, u32[]{:S(2)}, u32[]{:S(2)}) collective-permute-start(bf16[3456,512]{1,0:T(8,128)(2,1)} %get-tuple-element.60), channel_id=1, source_target_pairs={{0,1},{1,0},{2,3},{3,2},{4,5},{5,4},{6,7},{7,6},{8,9},{9,8},{10,11... | collective-permute-start | bytes 10616840 | tf_op jit(solution)/shard_map/cond/branch_1_fun/ppermute | solution.py:304
  44.2 10.8 %collective-permute-start = (bf16[3456,128]{1,0:T(8,128)(2,1)}, bf16[3456,128]{1,0:T(8,128)(2,1)S(1)}, u32[]{:S(2)}, u32[]{:S(2)}) collective-permute-start(bf16[3456,128]{1,0:T(8,128)(2,1)} %get-tuple-element.53), channel_id=1, source_target_pairs={{0,1},{1,0},{2,3},{3,2},{4,5},{5,4},{6,7},{7,6},{8,9},{9,8},{10,11... | collective-permute-start | bytes 2654216 | tf_op jit(solution)/shard_map/cond/branch_1_fun/ppermute | solution.py:303
  44.9 27.4 %all-to-all-start = ((bf16[8,432,128]{2,1,0:T(8,128)(2,1)}), bf16[8,432,128]{2,1,0:T(8,128)(2,1)S(1)}, u32[]{:S(2)}, u32[]{:S(2)}) async-start(bf16[8,432,128]{2,1,0:T(8,128)(2,1)} %get-tuple-element.51), calls=%async_computation | async-start | bytes 1769472 | tf_op jit(solution)/shard_map/cond/branch_1_fun/all_to_all | solution.py:316
  49.9 72.8 %collective-permute-start.5 = (bf16[1728,512]{1,0:T(8,128)(2,1)}, bf16[1728,512]{1,0:T(8,128)(2,1)}, u32[]{:S(2)}, u32[]{:S(2)}) collective-permute-start(bf16[1728,512]{1,0:T(8,128)(2,1)} %get-tuple-element.72), channel_id=1, source_target_pairs={{0,2},{2,0},{4,6},{6,4},{8,10},{10,8},{12,14},{14,12},{1,3},{3,1},... | collective-permute-start | bytes 5308424 | tf_op jit(solution)/shard_map/cond/branch_1_fun/ppermute | solution.py:129
  72.3 38.3 %all-to-all-start.1 = ((bf16[8,432,128]{2,1,0:T(8,128)(2,1)}), bf16[8,432,128]{2,1,0:T(8,128)(2,1)S(1)}, u32[]{:S(2)}, u32[]{:S(2)}) async-start(bf16[8,432,128]{2,1,0:T(8,128)(2,1)} %bitcast.72), calls=%async_computation.1 | async-start | bytes 1769472 | tf_op jit(solution)/shard_map/cond/branch_1_fun/all_to_all | solution.py:316
  81.0 66.3 %collective-permute-start.9 = (bf16[1728,512]{1,0:T(8,128)(2,1)}, bf16[1728,512]{1,0:T(8,128)(2,1)}, u32[]{:S(2)}, u32[]{:S(2)}) collective-permute-start(bf16[1728,512]{1,0:T(8,128)(2,1)} %dynamic-slice_select_fusion), channel_id=1, source_target_pairs={{0,2},{2,0},{4,6},{6,4},{8,10},{10,8},{12,14},{14,12},{1,3},{3,1},... | collective-permute-start | bytes 5308424 | tf_op jit(solution)/shard_map/cond/branch_1_fun/ppermute | solution.py:129
  83.0 27.6 %collective-permute-start.4 = (bf16[432,256]{1,0:T(8,128)(2,1)S(1)}, bf16[432,256]{1,0:T(8,128)(2,1)S(1)}, u32[]{:S(2)}, u32[]{:S(2)}) collective-permute-start(bf16[432,256]{1,0:T(8,128)(2,1)S(1)} %latent.2.refs_0_), channel_id=1, source_target_pairs={{0,12},{2,14},{4,0},{6,2},{8,4},{10,6},{12,8},{14,10},{1,13},{3,15... | collective-permute-start | bytes 663560 | tf_op jit(solution)/shard_map/cond/branch_1_fun/ppermute | solution.py:129
  86.3 31.1 %collective-permute-start.3 = (bf16[432,256]{1,0:T(8,128)(2,1)S(1)}, bf16[432,256]{1,0:T(8,128)(2,1)}, u32[]{:S(2)}, u32[]{:S(2)}) collective-permute-start(bf16[432,256]{1,0:T(8,128)(2,1)S(1)} %latent.2.refs_0_), channel_id=1, source_target_pairs={{0,8},{2,10},{4,12},{6,14},{8,0},{10,2},{12,4},{14,6},{1,9},{3,11}... | collective-permute-start | bytes 663560 | tf_op jit(solution)/shard_map/cond/branch_1_fun/ppermute | solution.py:129
  86.3 31.1 %collective-permute-start.2 = (bf16[432,256]{1,0:T(8,128)(2,1)S(1)}, bf16[432,256]{1,0:T(8,128)(2,1)}, u32[]{:S(2)}, u32[]{:S(2)}) collective-permute-start(bf16[432,256]{1,0:T(8,128)(2,1)S(1)} %latent.2.refs_0_), channel_id=1, source_target_pairs={{0,4},{2,6},{4,8},{6,10},{8,12},{10,14},{12,0},{14,2},{1,5},{3,7},... | collective-permute-start | bytes 663560 | tf_op jit(solution)/shard_map/cond/branch_1_fun/ppermute | solution.py:129
  118.6 14.0 %collective-permute-start.8 = (bf16[432,256]{1,0:T(8,128)(2,1)S(1)}, bf16[432,256]{1,0:T(8,128)(2,1)S(1)}, u32[]{:S(2)}, u32[]{:S(2)}) collective-permute-start(bf16[432,256]{1,0:T(8,128)(2,1)S(1)} %latent.3.refs_0_), channel_id=1, source_target_pairs={{0,12},{2,14},{4,0},{6,2},{8,4},{10,6},{12,8},{14,10},{1,13},{3,15... | collective-permute-start | bytes 663560 | tf_op jit(solution)/shard_map/cond/branch_1_fun/ppermute | solution.py:129
  118.7 20.1 %collective-permute-start.7 = (bf16[432,256]{1,0:T(8,128)(2,1)S(1)}, bf16[432,256]{1,0:T(8,128)(2,1)S(1)}, u32[]{:S(2)}, u32[]{:S(2)}) collective-permute-start(bf16[432,256]{1,0:T(8,128)(2,1)S(1)} %latent.3.refs_0_), channel_id=1, source_target_pairs={{0,8},{2,10},{4,12},{6,14},{8,0},{10,2},{12,4},{14,6},{1,9},{3,11}... | collective-permute-start | bytes 663560 | tf_op jit(solution)/shard_map/cond/branch_1_fun/ppermute | solution.py:129
  119.0 19.8 %collective-permute-start.6 = (bf16[432,256]{1,0:T(8,128)(2,1)S(1)}, bf16[432,256]{1,0:T(8,128)(2,1)S(1)}, u32[]{:S(2)}, u32[]{:S(2)}) collective-permute-start(bf16[432,256]{1,0:T(8,128)(2,1)S(1)} %latent.3.refs_0_), channel_id=1, source_target_pairs={{0,4},{2,6},{4,8},{6,10},{8,12},{10,14},{12,0},{14,2},{1,5},{3,7},... | collective-permute-start | bytes 663560 | tf_op jit(solution)/shard_map/cond/branch_1_fun/ppermute | solution.py:129
  139.5 21.9 %collective-permute-start.10 = (bf16[432,256]{1,0:T(8,128)(2,1)}, bf16[432,256]{1,0:T(8,128)(2,1)}, u32[]{:S(2)}, u32[]{:S(2)}) collective-permute-start(bf16[432,256]{1,0:T(8,128)(2,1)} %get-tuple-element.95), channel_id=1, source_target_pairs={{0,12},{2,14},{4,0},{6,2},{8,4},{10,6},{12,8},{14,10},{1,13},{3,15... | collective-permute-start | bytes 663560 | tf_op jit(solution)/shard_map/cond/branch_1_fun/ppermute | solution.py:129
  139.5 21.9 %collective-permute-start.12 = (bf16[432,256]{1,0:T(8,128)(2,1)}, bf16[432,256]{1,0:T(8,128)(2,1)}, u32[]{:S(2)}, u32[]{:S(2)}) collective-permute-start(bf16[432,256]{1,0:T(8,128)(2,1)} %get-tuple-element.97), channel_id=1, source_target_pairs={{0,4},{2,6},{4,8},{6,10},{8,12},{10,14},{12,0},{14,2},{1,5},{3,7},... | collective-permute-start | bytes 663560 | tf_op jit(solution)/shard_map/cond/branch_1_fun/ppermute | solution.py:129
  147.3 15.1 %collective-permute-start.11 = (bf16[432,256]{1,0:T(8,128)(2,1)}, bf16[432,256]{1,0:T(8,128)(2,1)}, u32[]{:S(2)}, u32[]{:S(2)}) collective-permute-start(bf16[432,256]{1,0:T(8,128)(2,1)} %get-tuple-element.96), channel_id=1, source_target_pairs={{0,8},{2,10},{4,12},{6,14},{8,0},{10,2},{12,4},{14,6},{1,9},{3,11}... | collective-permute-start | bytes 663560 | tf_op jit(solution)/shard_map/cond/branch_1_fun/ppermute | solution.py:129
  164.3 21.6 %collective-permute-start.14 = (bf16[432,256]{1,0:T(8,128)(2,1)}, bf16[432,256]{1,0:T(8,128)(2,1)S(1)}, u32[]{:S(2)}, u32[]{:S(2)}) collective-permute-start(bf16[432,256]{1,0:T(8,128)(2,1)} %get-tuple-element.101), channel_id=1, source_target_pairs={{0,8},{2,10},{4,12},{6,14},{8,0},{10,2},{12,4},{14,6},{1,9},{3,11}... | collective-permute-start | bytes 663560 | tf_op jit(solution)/shard_map/cond/branch_1_fun/ppermute | solution.py:129
  165.8 20.2 %collective-permute-start.15 = (bf16[432,256]{1,0:T(8,128)(2,1)}, bf16[432,256]{1,0:T(8,128)(2,1)S(1)}, u32[]{:S(2)}, u32[]{:S(2)}) collective-permute-start(bf16[432,256]{1,0:T(8,128)(2,1)} %get-tuple-element.102), channel_id=1, source_target_pairs={{0,4},{2,6},{4,8},{6,10},{8,12},{10,14},{12,0},{14,2},{1,5},{3,7},... | collective-permute-start | bytes 663560 | tf_op jit(solution)/shard_map/cond/branch_1_fun/ppermute | solution.py:129
  167.0 20.0 %collective-permute-start.17 = (f32[128,512]{1,0:T(8,128)S(1)}, f32[128,512]{1,0:T(8,128)S(1)}, u32[]{:S(2)}, u32[]{:S(2)}) collective-permute-start(f32[128,512]{1,0:T(8,128)S(1)} %slice_bitcast_fusion), channel_id=1, source_target_pairs={{0,2},{2,0},{4,6},{6,4},{8,10},{10,8},{12,14},{14,12},{1,3},{3,1},... | collective-permute-start | bytes 786440 | tf_op jit(solution)/shard_map/cond/branch_1_fun/ppermute | solution.py:129
  190.7 9.7 %collective-permute-start.25 = (f32[128,128]{1,0:T(8,128)S(1)}, f32[128,128]{1,0:T(8,128)S(1)}, u32[]{:S(2)}, u32[]{:S(2)}) collective-permute-start(f32[128,128]{1,0:T(8,128)S(1)} %get-tuple-element.172), channel_id=1, source_target_pairs={{0,14},{2,12},{4,2},{6,0},{8,6},{10,4},{12,10},{14,8},{1,15},{3,13... | collective-permute-start | bytes 196616 | tf_op jit(solution)/shard_map/cond/branch_1_fun/ppermute | solution.py:129
  (30 other events, 470.0 us)

commit v4 on v3

--- a/solution.py
+++ b/solution.py
@@ -21,15 +21,16 @@
 
 
 def compact_kernel(
-    group, cap, extra, rows, shards, known, first_ref, pair_ref, mask_ref, cells_ref, targets_ref, *refs
+    group, cap, extra, rows, shards, known, plan_ref, mask_ref, cells_ref, targets_ref, *refs
 ):
-    counts, refs = [ref[0] for ref in refs[:known]], refs[known:]
-    (facts_ref, late_ref, early_ref, over_ref, main_ref, pair_out_ref, far_ref, cells_all, targets_all, sems) = refs
+    blocks = mask_ref.shape[0]
+    (facts_ref, late_ref, early_ref, over_ref, main_ref, pair_out_ref, far_ref, cells_all, targets_all, place_in, sems) = refs
     step = pl.program_id(0)
     arrays = ((cells_ref, cells_all), (targets_ref, targets_all))
 
     @pl.when(step == 0)
     def _():
+        counts = [plan_ref[blocks + i] for i in range(known)]
         fits = jnp.int32(1)
         for one, two in zip(counts[::2], counts[1::2]):
             low, high = jnp.minimum(one, two), jnp.maximum(one, two)
@@ -45,19 +46,21 @@
                 )
             return carry
 
-        lax.fori_loop(0, first_ref[0] // BLOCK + 1, clear, 0)
-
-    before = lax.broadcasted_iota(jnp.int32, (BLOCK, BLOCK), 0) < lax.broadcasted_iota(
-        jnp.int32, (BLOCK, BLOCK), 1
-    )
-    before = before.astype(F32).astype(BF16)
+        lax.fori_loop(0, plan_ref[0] // BLOCK + 1, clear, 0)
+        before = lax.broadcasted_iota(jnp.int32, (BLOCK, BLOCK), 0) < lax.broadcasted_iota(
+            jnp.int32, (BLOCK, BLOCK), 1
+        )
+        before = before.astype(F32).astype(BF16)
+        mask = mask_ref[...]
+        prefix = dot(mask.astype(F32).astype(BF16), before).astype(jnp.int32)
+        place_in[...] = jnp.where(mask > 0, prefix, -rows)
+
     place = lax.broadcasted_iota(jnp.int32, (BLOCK + SUB, BLOCK), 0)
-    mask = mask_ref[0]
-    prefix = dot(mask.astype(F32).astype(BF16), before).astype(jnp.int32)
     for k in range(group):
-        first = first_ref[step * group + k]
+        first = plan_ref[step * group + k]
         start = jnp.minimum(first // SUB * SUB, rows - BLOCK - SUB)
-        slot = jnp.where(mask[k : k + 1] > 0, prefix[k : k + 1] + (first - start), -1)
+        offset = jnp.minimum(first - start, rows - 1)
+        slot = place_in[pl.ds(step * group + k, 1), :] + offset
         choose = (place == slot).astype(F32).astype(BF16)
         start = pl.multiple_of(start, SUB)
         for x_ref, out_ref in arrays:
@@ -76,7 +79,7 @@
         moves += [
             (cells_all.at[pl.ds(cap, extra)], over_ref),
             (cells_all.at[pl.ds(0, extra)], early_ref),
-            (targets_all.at[pl.ds(pl.multiple_of(pair_ref[0], SUB), extra // 2)], pair_out_ref),
+            (targets_all.at[pl.ds(pl.multiple_of(plan_ref[blocks + known], SUB), extra // 2)], pair_out_ref),
             (targets_all.at[pl.ds(cap, extra)], far_ref),
             (targets_all.at[pl.ds(0, cap)], main_ref),
         ]
@@ -91,22 +94,26 @@
     rows = -(-(cap + extra + 2 * BLOCK) // BLOCK) * BLOCK
     blocks = mask_blocks.shape[0]
     group = max(g for g in range(1, GROUP + 1) if blocks % g == 0)
+    at = jnp.arange(firsts.shape[0], dtype=jnp.int32)
+    plan = jnp.where(at < blocks, firsts, pair_at)
+    for i, known in enumerate(counts):
+        plan = jnp.where(at == blocks + i, known, plan)
     width, columns = cells.shape[1], targets.shape[1]
     shapes = [(shards, extra // shards, width), (extra, width), (extra, width)]
     shapes += [(cap, columns), (extra // 2, columns), (extra, columns)]
     return pl.pallas_call(
         functools.partial(compact_kernel, group, cap, extra, rows, shards, len(counts)),
         grid_spec=pltpu.PrefetchScalarGridSpec(
-            num_scalar_prefetch=2,
+            num_scalar_prefetch=1,
             grid=(blocks // group,),
-            in_specs=[pl.BlockSpec((1, group, BLOCK), lambda i, f, p: (i, 0, 0))]
-            + [pl.BlockSpec((group * BLOCK, w), lambda i, f, p: (i, 0)) for w in (width, columns)]
-            + [pl.BlockSpec(memory_space=pltpu.SMEM)] * len(counts),
+            in_specs=[pl.BlockSpec((blocks, BLOCK), lambda i, p: (0, 0))]
+            + [pl.BlockSpec((group * BLOCK, w), lambda i, p: (i, 0)) for w in (width, columns)],
             out_specs=[pl.BlockSpec(memory_space=pltpu.SMEM)]
             + [pl.BlockSpec(memory_space=pl.ANY)] * len(shapes),
             scratch_shapes=[
                 pltpu.VMEM((rows, width), BF16),
                 pltpu.VMEM((rows, columns), BF16),
+                pltpu.VMEM((blocks, BLOCK), jnp.int32),
                 pltpu.SemaphoreType.DMA((shards + 5,)),
             ],
         ),
@@ -119,7 +126,7 @@
             transcendentals=0,
         ),
         name="compact",
-    )(firsts, pair_at.reshape(1), mask_blocks.reshape(-1, group, BLOCK), cells, targets, *counts)
+    )(plan, mask_blocks, cells, targets)
 
 
 SWAP = [(0, 1), (1, 0)]
@@ -342,7 +349,7 @@
 
     late_parts, latents[0] = lax.optimization_barrier((residual(1), latents[0]))
     terms = list(late_parts[0])
-    terms[count // 2], pairs[0] = lax.optimization_barrier((terms[count // 2], pairs[0]))
+    terms[1], pairs[0] = lax.optimization_barrier((terms[1], pairs[0]))
     grads = {1: summed(terms)}
     early_parts, grads[1] = lax.optimization_barrier(
         (residual(0, other_targets, *late_parts[1:]), grads[1])
@@ -396,9 +403,9 @@
     mask_blocks = land_mask.reshape(-1, BLOCK)
     in_block = jnp.sum(mask_blocks, axis=1)
     land = jnp.sum(land_mask).reshape(1)
-    at = jnp.arange(in_block.shape[0], dtype=jnp.int32)
+    at = jnp.arange(in_block.shape[0] + 2 * groups + 1, dtype=jnp.int32)
     firsts = jnp.maximum(cap - land, 0) + jnp.sum(
-        jnp.where(at[None, :] < at[:, None], in_block[None, :], 0), axis=1
+        jnp.where(at[None, : in_block.shape[0]] < at[:, None], in_block[None, :], 0), axis=1
     )
     counts = []
     for g in range(groups):

time: 215 us -> 213 us (level)
  Pallas kernels: 43.8 us -> 41.1 us
  other arithmetic: 18.9 us -> 21.2 us
    pallas_call x1, Pallas kernels: 19.7 us -> 16.8 us  [compact(): pl.pallas_call(functools.partial(compact_kernel, group, cap, extra, rows,...]
    select_n x0 -> x1, other arithmetic: none -> 2.44 us  [compact(): plan = jnp.where(at == blocks + i, known, plan)]
  transfers between devices with their start and end apart: 37 -> 37, of which waited for: 15 -> 12; matrix products, arithmetic and copies ran while one was open for 8% -> 9% of each run, Pallas kernels for 20% -> 19%
where the time goes in v4:
time: 213 us
  waiting for transfers between devices  82.3 us (39%)
  starting transfers between devices  49.2 us (23%)
  Pallas kernels  41.1 us (19%)
  other arithmetic  21.2 us (10%)
  between operations  14.9 us (7%)
  local copies, waits for them, and re-layouts  2.69 us (1%)
    ppermute x28, waiting for transfers between devices, send(): return lax.ppermute(x, 'tgt', moves)  44.4 us
    ppermute x28, starting transfers between devices, send(): return lax.ppermute(x, 'tgt', moves)  36.7 us
    all_to_all x2, waiting for transfers between devices, owners_cells(): return lax.all_to_all(x, 'tgt', split_axis=0, concat_axis=0, tiled=True)  36.1 us
    pallas_call x2, Pallas kernels, residual_of(): pl.pallas_call(functools.partial(residual_kernel, count, mixed), grid_spe...  21.2 us
    pallas_call x1, Pallas kernels, compact(): pl.pallas_call(functools.partial(compact_kernel, group, cap, extra, rows,...  16.8 us
    all_to_all x2, starting transfers between devices, owners_cells(): return lax.all_to_all(x, 'tgt', split_axis=0, concat_axis=0, tiled=True)  8.66 us
    select_n x2, other arithmetic, merged(): return jnp.where(row < received[0], other, own)  6.68 us
  transfers between devices with their start and end apart: 37, of which 12 were waited for; matrix products, arithmetic and copies ran while one was open for 9% of the time, Pallas kernels for 19%

profile of v4, /device:TPU:0, one launch (start us, length us, event | category | flops | bytes accessed | tf_op | source)
XLA Modules:
  0.0 212.6 jit_solution(186330424442885224)
XLA Ops:
  8.6 2.4 %collective-permute-start.28 = (s32[1]{0:T(128)}, s32[1]{0:T(128)}, u32[]{:S(2)}, u32[]{:S(2)}) collective-permute-start(s32[1]{0:T(128)} %bitcast.28), channel_id=1, source_target_pairs={{0,17},{1,16},{16,1},{17,0},{2,19},{3,18},{18,3},{19,2},{4,21},{5,... | collective-permute-start | bytes 20 | tf_op jit(solution)/shard_map/ppermute | solution.py:414
  15.4 2.5 %collective-permute-done.29 = bf16[128,256]{1,0:T(8,128)(2,1)S(1)} collective-permute-done((bf16[128,256]{1,0:T(8,128)(2,1)}, bf16[128,256]{1,0:T(8,128)(2,1)S(1)}, u32[]{:S(2)}, u32[]{:S(2)}) %collective-permute-start.29) | collective-permute-done | bytes 65568 | tf_op jit(solution)/shard_map/ppermute | solution.py:136
  19.1 3.9 %collective-permute-start.33 = (bf16[2,128,256]{2,1,0:T(8,128)(2,1)S(1)}, bf16[2,128,256]{2,1,0:T(8,128)(2,1)S(1)}, u32[]{:S(2)}, u32[]{:S(2)}) collective-permute-start(bf16[2,128,256]{2,1,0:T(8,128)(2,1)S(1)} %pad_maximum_fusion.1), channel_id=1, source_target_pairs={{0,12},{2,14},{4,0},{6,2},{8,4},{10,6},{12,8},{14,10},{1,13},{3,15... | collective-permute-start | bytes 393224 | tf_op jit(solution)/shard_map/ppermute | solution.py:136
  24.0 2.4 %compare_select_fusion.6.plan_ref = s32[57]{0:T(128)S(1)} fusion(s32[57]{0:T(128)S(1)} %broadcast_add_fusion.2, s32[]{:T(128)S(6)} %add.205, s32[]{:T(128)} %bitcast.35, s32[]{:T(128)} %bitcast.34, s32[]{:T(128)} %bitcast.33, s32[]{:T(128)} %bitcast.32), kind=kLoop, calls=%fused_computation.43 | loop fusion | flops 570 | bytes 476 | tf_op jit(solution)/shard_map/jit(_where)/select_n | solution.py:100
  26.5 16.8 %compact.1 = (s32[3]{0:T(128)S(1)}, bf16[8,432,128]{2,1,0:T(8,128)(2,1)}, bf16[3456,128]{1,0:T(8,128)(2,1)}, bf16[3456,128]{1,0:T(8,128)(2,1)}, bf16[6912,512]{1...) custom-call(s32[57]{0:T(128)S(1)} %compare_select_fusion.6.plan_ref, ...), custom_call_target="tpu_custom_call" | custom-call | flops 4634705920 | bytes 31129600 | tf_op jit(solution)/shard_map/compact/pallas_call | solution.py:104
  43.4 162.3 %conditional.1 = (f32[128,128]{1,0:T(8,128)}, f32[128,512]{1,0:T(8,128)}) conditional(s32[]{:T(128)} %bitcast.36, (s32[13312]{0:T(1024)S(1)}, bf16[13312,128]{1,0:T(8,128)(2,1)S(1)}, bf16[128,256]{1,0:T(8,128)(2,1)}, bf16[256,512]{1,0:T(8,128)(2,1)}, bf16[13312,512]{1,0:T(8,128)(2,1)}, /*index=5*/s32[3]{0:T(128)S(1)}, f32[512]{0:T(512)S(1)}) %tuple.50, ...), branch_computations={%region_3.8_spmd, %region_8.9_spmd} | conditional | flops 12263240704 | bytes 233272640 | solution.py:437
  44.4 5.0 %all-to-all-start = ((bf16[8,432,128]{2,1,0:T(8,128)(2,1)}), bf16[8,432,128]{2,1,0:T(8,128)(2,1)S(1)}, u32[]{:S(2)}, u32[]{:S(2)}) async-start(bf16[8,432,128]{2,1,0:T(8,128)(2,1)} %get-tuple-element.51), calls=%async_computation | async-start | bytes 1769472 | tf_op jit(solution)/shard_map/cond/branch_1_fun/all_to_all | solution.py:323
  54.5 2.8 %broadcast_select_fusion.1 = bf16[3456,128]{1,0:T(8,128)(2,1)S(1)} fusion(bf16[3456,128]{1,0:T(8,128)(2,1)S(1)} %collective-permute-done, bf16[3456,128]{1,0:T(8,128)(2,1)} %get-tuple-element.54, pred[3456]{0:T(1024)(128)(4,1)S(1)} %iota_compare_fusion), kind=kLoop, calls=%fused_computation.6 | loop fusion | flops 442368 | bytes 2657664 | tf_op jit(solution)/shard_map/cond/branch_1_fun/jit(_where)/select_n | solution.py:316
  58.3 13.6 %all-to-all-done.cells_ref.refs_0_ = bf16[8,432,128]{2,1,0:T(8,128)(2,1)S(1)} async-done(((bf16[8,432,128]{2,1,0:T(8,128)(2,1)}), bf16[8,432,128]{2,1,0:T(8,128)(2,1)S(1)}, u32[]{:S(2)}, u32[]{:S(2)}) %all-to-all-start) | async-done | bytes 884768 | tf_op jit(solution)/shard_map/cond/branch_1_fun/all_to_all | solution.py:323
  71.8 3.6 %all-to-all-start.1 = ((bf16[8,432,128]{2,1,0:T(8,128)(2,1)}), bf16[8,432,128]{2,1,0:T(8,128)(2,1)S(1)}, u32[]{:S(2)}, u32[]{:S(2)}) async-start(bf16[8,432,128]{2,1,0:T(8,128)(2,1)} %bitcast.76), calls=%async_computation.1 | async-start | bytes 1769472 | tf_op jit(solution)/shard_map/cond/branch_1_fun/all_to_all | solution.py:323
  76.6 3.9 %dynamic-slice_select_fusion = bf16[1728,512]{1,0:T(8,128)(2,1)} fusion(bf16[6912,512]{1,0:T(8,128)(2,1)} %get-tuple-element.71.refs_4_, s32[]{:T(128)S(6)} %select_n.93, bf16[3456,512]{1,0:T(8,128)(2,1)} %collective-permute-done.1.refs_6_, s32[]{:T(128)S(6)} %select_n.92, pred[1728]{0:T(1024)(128)(4,1)S(1)} %add_compare_fusion), kind=kLoop, calls=%fused_computation.5 | loop fusion | flops 884736 | bytes 5310152 | tf_op jit(solution)/shard_map/cond/branch_1_fun/jit(_where)/select_n | solution.py:316
  82.5 3.3 %collective-permute-start.4 = (bf16[432,256]{1,0:T(8,128)(2,1)S(1)}, bf16[432,256]{1,0:T(8,128)(2,1)S(1)}, u32[]{:S(2)}, u32[]{:S(2)}) collective-permute-start(bf16[432,256]{1,0:T(8,128)(2,1)S(1)} %latent.2.refs_0_), channel_id=1, source_target_pairs={{0,12},{2,14},{4,0},{6,2},{8,4},{10,6},{12,8},{14,10},{1,13},{3,15... | collective-permute-start | bytes 663560 | tf_op jit(solution)/shard_map/cond/branch_1_fun/ppermute | solution.py:136
  87.5 22.6 %all-to-all-done.1.cells_ref.refs_1_ = bf16[8,432,128]{2,1,0:T(8,128)(2,1)S(1)} async-done(((bf16[8,432,128]{2,1,0:T(8,128)(2,1)}), bf16[8,432,128]{2,1,0:T(8,128)(2,1)S(1)}, u32[]{:S(2)}, u32[]{:S(2)}) %all-to-all-start.1) | async-done | bytes 884768 | tf_op jit(solution)/shard_map/cond/branch_1_fun/all_to_all | solution.py:323
  110.1 6.7 %collective-permute-done.3.refs_2_ = bf16[432,256]{1,0:T(8,128)(2,1)S(1)} collective-permute-done((bf16[432,256]{1,0:T(8,128)(2,1)S(1)}, bf16[432,256]{1,0:T(8,128)(2,1)S(1)}, u32[]{:S(2)}, u32[]{:S(2)}) %collective-permute-start.3) | collective-permute-done | bytes 221216 | tf_op jit(solution)/shard_map/cond/branch_1_fun/ppermute | solution.py:136
  122.3 9.9 %residual.2 = (bf16[432,256]{1,0:T(8,128)(2,1)}, bf16[432,256]{1,0:T(8,128)(2,1)}, bf16[432,256]{1,0:T(8,128)(2,1)}, bf16[432,256]{1,0:T(8,128)(2,1)}, f32[256,512]{1,0:T(8,128)}, /*index=5*/f32[256,512]{1,0:T(8,128)}) custom-call(s32[4]{0:T(128)} %broadcast_add_fusion.own_ref, s32[4]{0:T(128)} %copy-done.2, s32[2]{0:T(128)} %pad_add_fusion.part_ref, ...), custom_call_target="tpu_custom_call" | custom-call | flops 226492416 | bytes 1327104 | tf_op jit(solution)/shard_map/cond/branch_1_fun/residual/pallas_call | solution.py:233
  132.2 6.0 %collective-permute-done.7.refs_2_ = bf16[432,256]{1,0:T(8,128)(2,1)S(1)} collective-permute-done((bf16[432,256]{1,0:T(8,128)(2,1)S(1)}, bf16[432,256]{1,0:T(8,128)(2,1)S(1)}, u32[]{:S(2)}, u32[]{:S(2)}) %collective-permute-start.7) | collective-permute-done | bytes 221216 | tf_op jit(solution)/shard_map/cond/branch_1_fun/ppermute | solution.py:136
  139.7 7.1 %collective-permute-done.9.refs_5_ = bf16[1728,512]{1,0:T(8,128)(2,1)} collective-permute-done((bf16[1728,512]{1,0:T(8,128)(2,1)}, bf16[1728,512]{1,0:T(8,128)(2,1)}, u32[]{:S(2)}, u32[]{:S(2)}) %collective-permute-start.9) | collective-permute-done | bytes 1769504 | tf_op jit(solution)/shard_map/cond/branch_1_fun/ppermute | solution.py:136
  146.8 3.3 %collective-permute-start.10 = (bf16[432,256]{1,0:T(8,128)(2,1)}, bf16[432,256]{1,0:T(8,128)(2,1)}, u32[]{:S(2)}, u32[]{:S(2)}) collective-permute-start(bf16[432,256]{1,0:T(8,128)(2,1)} %get-tuple-element.95), channel_id=1, source_target_pairs={{0,12},{2,14},{4,0},{6,2},{8,4},{10,6},{12,8},{14,10},{1,13},{3,15... | collective-permute-start | bytes 663560 | tf_op jit(solution)/shard_map/cond/branch_1_fun/ppermute | solution.py:136
  150.6 11.3 %residual.3 = (bf16[432,256]{1,0:T(8,128)(2,1)}, bf16[432,256]{1,0:T(8,128)(2,1)}, bf16[432,256]{1,0:T(8,128)(2,1)}, bf16[432,256]{1,0:T(8,128)(2,1)}, f32[2,128,512]{2,1,0:T(8,128)}, /*index=5*/f32[2,128,512]{2,1,0:T(8,128)}) custom-call(s32[4]{0:T(128)} %broadcast_add_fusion.1.own_ref, s32[4]{0:T(128)} %copy-done.2, s32[2]{0:T(128)} %pad_add_fusion.part_ref, ...), custom_call_target="tpu_custom_call" | custom-call | flops 226492416 | bytes 1327104 | tf_op jit(solution)/shard_map/cond/branch_1_fun/residual/pallas_call | solution.py:233
  166.8 5.4 %collective-permute-done.13 = bf16[432,256]{1,0:T(8,128)(2,1)S(1)} collective-permute-done((bf16[432,256]{1,0:T(8,128)(2,1)}, bf16[432,256]{1,0:T(8,128)(2,1)S(1)}, u32[]{:S(2)}, u32[]{:S(2)}) %collective-permute-start.13) | collective-permute-done | bytes 221216 | tf_op jit(solution)/shard_map/cond/branch_1_fun/ppermute | solution.py:136
  172.2 11.4 %collective-permute-done.14 = bf16[432,256]{1,0:T(8,128)(2,1)S(1)} collective-permute-done((bf16[432,256]{1,0:T(8,128)(2,1)}, bf16[432,256]{1,0:T(8,128)(2,1)S(1)}, u32[]{:S(2)}, u32[]{:S(2)}) %collective-permute-start.14) | collective-permute-done | bytes 221216 | tf_op jit(solution)/shard_map/cond/branch_1_fun/ppermute | solution.py:136
  189.9 3.3 %collective-permute-start.25 = (f32[128,128]{1,0:T(8,128)S(1)}, f32[128,128]{1,0:T(8,128)S(1)}, u32[]{:S(2)}, u32[]{:S(2)}) collective-permute-start(f32[128,128]{1,0:T(8,128)S(1)} %get-tuple-element.172), channel_id=1, source_target_pairs={{0,14},{2,12},{4,2},{6,0},{8,6},{10,4},{12,10},{14,8},{1,15},{3,13... | collective-permute-start | bytes 196616 | tf_op jit(solution)/shard_map/cond/branch_1_fun/ppermute | solution.py:136
  196.1 3.8 %collective-permute-start.21 = (f32[128,128]{1,0:T(8,128)S(1)}, f32[128,128]{1,0:T(8,128)S(1)}, u32[]{:S(2)}, u32[]{:S(2)}) collective-permute-start(f32[128,128]{1,0:T(8,128)S(1)} %get-tuple-element.176), channel_id=1, source_target_pairs={{0,12},{2,14},{4,0},{6,2},{8,4},{10,6},{12,8},{14,10},{1,13},{3,15... | collective-permute-start | bytes 196616 | tf_op jit(solution)/shard_map/cond/branch_1_fun/ppermute | solution.py:136
  202.3 2.8 %collective-permute-done.20 = f32[128,128]{1,0:T(8,128)S(1)} collective-permute-done((f32[128,128]{1,0:T(8,128)S(1)}, f32[128,128]{1,0:T(8,128)S(1)}, u32[]{:S(2)}, u32[]{:S(2)}) %collective-permute-start.20) | collective-permute-done | bytes 65568 | tf_op jit(solution)/shard_map/cond/branch_1_fun/ppermute | solution.py:136
  (116 shorter events, 42.7 us)
Async XLA Ops:
  8.6 10.4 %collective-permute-start.28 = (s32[1]{0:T(128)}, s32[1]{0:T(128)}, u32[]{:S(2)}, u32[]{:S(2)}) collective-permute-start(s32[1]{0:T(128)} %bitcast.28), channel_id=1, source_target_pairs={{0,17},{1,16},{16,1},{17,0},{2,19},{3,18},{18,3},{19,2},{4,21},{5,... | collective-permute-start | bytes 20 | tf_op jit(solution)/shard_map/ppermute | solution.py:414
  17.9 25.4 %collective-permute-start.34 = (bf16[256,512]{1,0:T(8,128)(2,1)}, bf16[256,512]{1,0:T(8,128)(2,1)}, u32[]{:S(2)}, u32[]{:S(2)}) collective-permute-start(bf16[256,512]{1,0:T(8,128)(2,1)} %param.11), channel_id=1, source_target_pairs={{0,2},{2,0},{4,6},{6,4},{8,10},{10,8},{12,14},{14,12},{1,3},{3,1},... | collective-permute-start | bytes 786440 | tf_op jit(solution)/shard_map/ppermute | solution.py:136
  19.1 24.2 %collective-permute-start.33 = (bf16[2,128,256]{2,1,0:T(8,128)(2,1)S(1)}, bf16[2,128,256]{2,1,0:T(8,128)(2,1)S(1)}, u32[]{:S(2)}, u32[]{:S(2)}) collective-permute-start(bf16[2,128,256]{2,1,0:T(8,128)(2,1)S(1)} %pad_maximum_fusion.1), channel_id=1, source_target_pairs={{0,12},{2,14},{4,0},{6,2},{8,4},{10,6},{12,8},{14,10},{1,13},{3,15... | collective-permute-start | bytes 393224 | tf_op jit(solution)/shard_map/ppermute | solution.py:136
  23.0 20.3 %collective-permute-start.32 = (bf16[2,128,256]{2,1,0:T(8,128)(2,1)S(1)}, bf16[2,128,256]{2,1,0:T(8,128)(2,1)S(1)}, u32[]{:S(2)}, u32[]{:S(2)}) collective-permute-start(bf16[2,128,256]{2,1,0:T(8,128)(2,1)S(1)} %pad_maximum_fusion.1), channel_id=1, source_target_pairs={{0,8},{2,10},{4,12},{6,14},{8,0},{10,2},{12,4},{14,6},{1,9},{3,11}... | collective-permute-start | bytes 393224 | tf_op jit(solution)/shard_map/ppermute | solution.py:136
  23.0 20.3 %collective-permute-start.31 = (bf16[2,128,256]{2,1,0:T(8,128)(2,1)S(1)}, bf16[2,128,256]{2,1,0:T(8,128)(2,1)S(1)}, u32[]{:S(2)}, u32[]{:S(2)}) collective-permute-start(bf16[2,128,256]{2,1,0:T(8,128)(2,1)S(1)} %pad_maximum_fusion.1), channel_id=1, source_target_pairs={{0,4},{2,6},{4,8},{6,10},{8,12},{10,14},{12,0},{14,2},{1,5},{3,7},... | collective-permute-start | bytes 393224 | tf_op jit(solution)/shard_map/ppermute | solution.py:136
  43.7 33.0 %collective-permute-start.1 = (bf16[3456,512]{1,0:T(8,128)(2,1)}, bf16[3456,512]{1,0:T(8,128)(2,1)}, u32[]{:S(2)}, u32[]{:S(2)}) collective-permute-start(bf16[3456,512]{1,0:T(8,128)(2,1)} %get-tuple-element.60), channel_id=1, source_target_pairs={{0,1},{1,0},{2,3},{3,2},{4,5},{5,4},{6,7},{7,6},{8,9},{9,8},{10,11... | collective-permute-start | bytes 10616840 | tf_op jit(solution)/shard_map/cond/branch_1_fun/ppermute | solution.py:311
  43.7 10.7 %collective-permute-start = (bf16[3456,128]{1,0:T(8,128)(2,1)}, bf16[3456,128]{1,0:T(8,128)(2,1)S(1)}, u32[]{:S(2)}, u32[]{:S(2)}) collective-permute-start(bf16[3456,128]{1,0:T(8,128)(2,1)} %get-tuple-element.53), channel_id=1, source_target_pairs={{0,1},{1,0},{2,3},{3,2},{4,5},{5,4},{6,7},{7,6},{8,9},{9,8},{10,11... | collective-permute-start | bytes 2654216 | tf_op jit(solution)/shard_map/cond/branch_1_fun/ppermute | solution.py:310
  44.4 27.5 %all-to-all-start = ((bf16[8,432,128]{2,1,0:T(8,128)(2,1)}), bf16[8,432,128]{2,1,0:T(8,128)(2,1)S(1)}, u32[]{:S(2)}, u32[]{:S(2)}) async-start(bf16[8,432,128]{2,1,0:T(8,128)(2,1)} %get-tuple-element.51), calls=%async_computation | async-start | bytes 1769472 | tf_op jit(solution)/shard_map/cond/branch_1_fun/all_to_all | solution.py:323
  49.4 72.9 %collective-permute-start.5 = (bf16[1728,512]{1,0:T(8,128)(2,1)}, bf16[1728,512]{1,0:T(8,128)(2,1)}, u32[]{:S(2)}, u32[]{:S(2)}) collective-permute-start(bf16[1728,512]{1,0:T(8,128)(2,1)} %get-tuple-element.72), channel_id=1, source_target_pairs={{0,2},{2,0},{4,6},{6,4},{8,10},{10,8},{12,14},{14,12},{1,3},{3,1},... | collective-permute-start | bytes 5308424 | tf_op jit(solution)/shard_map/cond/branch_1_fun/ppermute | solution.py:136
  71.8 38.3 %all-to-all-start.1 = ((bf16[8,432,128]{2,1,0:T(8,128)(2,1)}), bf16[8,432,128]{2,1,0:T(8,128)(2,1)S(1)}, u32[]{:S(2)}, u32[]{:S(2)}) async-start(bf16[8,432,128]{2,1,0:T(8,128)(2,1)} %bitcast.76), calls=%async_computation.1 | async-start | bytes 1769472 | tf_op jit(solution)/shard_map/cond/branch_1_fun/all_to_all | solution.py:323
  80.5 66.3 %collective-permute-start.9 = (bf16[1728,512]{1,0:T(8,128)(2,1)}, bf16[1728,512]{1,0:T(8,128)(2,1)}, u32[]{:S(2)}, u32[]{:S(2)}) collective-permute-start(bf16[1728,512]{1,0:T(8,128)(2,1)} %dynamic-slice_select_fusion), channel_id=1, source_target_pairs={{0,2},{2,0},{4,6},{6,4},{8,10},{10,8},{12,14},{14,12},{1,3},{3,1},... | collective-permute-start | bytes 5308424 | tf_op jit(solution)/shard_map/cond/branch_1_fun/ppermute | solution.py:136
  82.5 27.6 %collective-permute-start.4 = (bf16[432,256]{1,0:T(8,128)(2,1)S(1)}, bf16[432,256]{1,0:T(8,128)(2,1)S(1)}, u32[]{:S(2)}, u32[]{:S(2)}) collective-permute-start(bf16[432,256]{1,0:T(8,128)(2,1)S(1)} %latent.2.refs_0_), channel_id=1, source_target_pairs={{0,12},{2,14},{4,0},{6,2},{8,4},{10,6},{12,8},{14,10},{1,13},{3,15... | collective-permute-start | bytes 663560 | tf_op jit(solution)/shard_map/cond/branch_1_fun/ppermute | solution.py:136
  85.8 31.0 %collective-permute-start.3 = (bf16[432,256]{1,0:T(8,128)(2,1)S(1)}, bf16[432,256]{1,0:T(8,128)(2,1)S(1)}, u32[]{:S(2)}, u32[]{:S(2)}) collective-permute-start(bf16[432,256]{1,0:T(8,128)(2,1)S(1)} %latent.2.refs_0_), channel_id=1, source_target_pairs={{0,8},{2,10},{4,12},{6,14},{8,0},{10,2},{12,4},{14,6},{1,9},{3,11}... | collective-permute-start | bytes 663560 | tf_op jit(solution)/shard_map/cond/branch_1_fun/ppermute | solution.py:136
  85.8 31.0 %collective-permute-start.2 = (bf16[432,256]{1,0:T(8,128)(2,1)S(1)}, bf16[432,256]{1,0:T(8,128)(2,1)}, u32[]{:S(2)}, u32[]{:S(2)}) collective-permute-start(bf16[432,256]{1,0:T(8,128)(2,1)S(1)} %latent.2.refs_0_), channel_id=1, source_target_pairs={{0,4},{2,6},{4,8},{6,10},{8,12},{10,14},{12,0},{14,2},{1,5},{3,7},... | collective-permute-start | bytes 663560 | tf_op jit(solution)/shard_map/cond/branch_1_fun/ppermute | solution.py:136
  118.0 14.2 %collective-permute-start.8 = (bf16[432,256]{1,0:T(8,128)(2,1)S(1)}, bf16[432,256]{1,0:T(8,128)(2,1)S(1)}, u32[]{:S(2)}, u32[]{:S(2)}) collective-permute-start(bf16[432,256]{1,0:T(8,128)(2,1)S(1)} %latent.3.refs_0_), channel_id=1, source_target_pairs={{0,12},{2,14},{4,0},{6,2},{8,4},{10,6},{12,8},{14,10},{1,13},{3,15... | collective-permute-start | bytes 663560 | tf_op jit(solution)/shard_map/cond/branch_1_fun/ppermute | solution.py:136
  118.1 20.2 %collective-permute-start.7 = (bf16[432,256]{1,0:T(8,128)(2,1)S(1)}, bf16[432,256]{1,0:T(8,128)(2,1)S(1)}, u32[]{:S(2)}, u32[]{:S(2)}) collective-permute-start(bf16[432,256]{1,0:T(8,128)(2,1)S(1)} %latent.3.refs_0_), channel_id=1, source_target_pairs={{0,8},{2,10},{4,12},{6,14},{8,0},{10,2},{12,4},{14,6},{1,9},{3,11}... | collective-permute-start | bytes 663560 | tf_op jit(solution)/shard_map/cond/branch_1_fun/ppermute | solution.py:136
  118.5 19.7 %collective-permute-start.6 = (bf16[432,256]{1,0:T(8,128)(2,1)S(1)}, bf16[432,256]{1,0:T(8,128)(2,1)S(1)}, u32[]{:S(2)}, u32[]{:S(2)}) collective-permute-start(bf16[432,256]{1,0:T(8,128)(2,1)S(1)} %latent.3.refs_0_), channel_id=1, source_target_pairs={{0,4},{2,6},{4,8},{6,10},{8,12},{10,14},{12,0},{14,2},{1,5},{3,7},... | collective-permute-start | bytes 663560 | tf_op jit(solution)/shard_map/cond/branch_1_fun/ppermute | solution.py:136
  138.3 23.6 %collective-permute-start.11 = (bf16[432,256]{1,0:T(8,128)(2,1)}, bf16[432,256]{1,0:T(8,128)(2,1)S(1)}, u32[]{:S(2)}, u32[]{:S(2)}) collective-permute-start(bf16[432,256]{1,0:T(8,128)(2,1)} %get-tuple-element.96), channel_id=1, source_target_pairs={{0,8},{2,10},{4,12},{6,14},{8,0},{10,2},{12,4},{14,6},{1,9},{3,11}... | collective-permute-start | bytes 663560 | tf_op jit(solution)/shard_map/cond/branch_1_fun/ppermute | solution.py:136
  139.7 22.2 %collective-permute-start.12 = (bf16[432,256]{1,0:T(8,128)(2,1)}, bf16[432,256]{1,0:T(8,128)(2,1)}, u32[]{:S(2)}, u32[]{:S(2)}) collective-permute-start(bf16[432,256]{1,0:T(8,128)(2,1)} %get-tuple-element.97), channel_id=1, source_target_pairs={{0,4},{2,6},{4,8},{6,10},{8,12},{10,14},{12,0},{14,2},{1,5},{3,7},... | collective-permute-start | bytes 663560 | tf_op jit(solution)/shard_map/cond/branch_1_fun/ppermute | solution.py:136
  146.8 15.1 %collective-permute-start.10 = (bf16[432,256]{1,0:T(8,128)(2,1)}, bf16[432,256]{1,0:T(8,128)(2,1)}, u32[]{:S(2)}, u32[]{:S(2)}) collective-permute-start(bf16[432,256]{1,0:T(8,128)(2,1)} %get-tuple-element.95), channel_id=1, source_target_pairs={{0,12},{2,14},{4,0},{6,2},{8,4},{10,6},{12,8},{14,10},{1,13},{3,15... | collective-permute-start | bytes 663560 | tf_op jit(solution)/shard_map/cond/branch_1_fun/ppermute | solution.py:136
  163.8 19.8 %collective-permute-start.14 = (bf16[432,256]{1,0:T(8,128)(2,1)}, bf16[432,256]{1,0:T(8,128)(2,1)S(1)}, u32[]{:S(2)}, u32[]{:S(2)}) collective-permute-start(bf16[432,256]{1,0:T(8,128)(2,1)} %get-tuple-element.101), channel_id=1, source_target_pairs={{0,8},{2,10},{4,12},{6,14},{8,0},{10,2},{12,4},{14,6},{1,9},{3,11}... | collective-permute-start | bytes 663560 | tf_op jit(solution)/shard_map/cond/branch_1_fun/ppermute | solution.py:136
  163.8 19.8 %collective-permute-start.15 = (bf16[432,256]{1,0:T(8,128)(2,1)}, bf16[432,256]{1,0:T(8,128)(2,1)S(1)}, u32[]{:S(2)}, u32[]{:S(2)}) collective-permute-start(bf16[432,256]{1,0:T(8,128)(2,1)} %get-tuple-element.102), channel_id=1, source_target_pairs={{0,4},{2,6},{4,8},{6,10},{8,12},{10,14},{12,0},{14,2},{1,5},{3,7},... | collective-permute-start | bytes 663560 | tf_op jit(solution)/shard_map/cond/branch_1_fun/ppermute | solution.py:136
  166.4 18.3 %collective-permute-start.17 = (f32[128,512]{1,0:T(8,128)S(1)}, f32[128,512]{1,0:T(8,128)S(1)}, u32[]{:S(2)}, u32[]{:S(2)}) collective-permute-start(f32[128,512]{1,0:T(8,128)S(1)} %slice_bitcast_fusion), channel_id=1, source_target_pairs={{0,2},{2,0},{4,6},{6,4},{8,10},{10,8},{12,14},{14,12},{1,3},{3,1},... | collective-permute-start | bytes 786440 | tf_op jit(solution)/shard_map/cond/branch_1_fun/ppermute | solution.py:136
  189.9 10.0 %collective-permute-start.25 = (f32[128,128]{1,0:T(8,128)S(1)}, f32[128,128]{1,0:T(8,128)S(1)}, u32[]{:S(2)}, u32[]{:S(2)}) collective-permute-start(f32[128,128]{1,0:T(8,128)S(1)} %get-tuple-element.172), channel_id=1, source_target_pairs={{0,14},{2,12},{4,2},{6,0},{8,6},{10,4},{12,10},{14,8},{1,15},{3,13... | collective-permute-start | bytes 196616 | tf_op jit(solution)/shard_map/cond/branch_1_fun/ppermute | solution.py:136
  (29 other events, 414.7 us)

commit v5 on v4

--- a/solution.py
+++ b/solution.py
@@ -341,20 +341,23 @@
             scale, weights, factors, latents[chunk], own_targets, pairs[chunk], other,
         )
 
-    def summed(terms):
-        total = terms[0].astype(F32)
-        for s in range(1, count):
-            total = total + send(terms[s], shifted(count, -s, 0)).astype(F32)
+    def exchanged(terms):
+        return [terms[0]] + [send(terms[s], shifted(count, -s, 0)) for s in range(1, count)]
+
+    def summed(parts):
+        total = parts[0].astype(F32)
+        for part in parts[1:]:
+            total = total + part.astype(F32)
         return total.astype(BF16)
 
     late_parts, latents[0] = lax.optimization_barrier((residual(1), latents[0]))
     terms = list(late_parts[0])
     terms[1], pairs[0] = lax.optimization_barrier((terms[1], pairs[0]))
-    grads = {1: summed(terms)}
-    early_parts, grads[1] = lax.optimization_barrier(
-        (residual(0, other_targets, *late_parts[1:]), grads[1])
-    )
-    grads[0] = summed(early_parts[0])
+    late_terms = exchanged(terms)
+    early_parts, late_terms = lax.optimization_barrier(
+        (residual(0, other_targets, *late_parts[1:]), late_terms)
+    )
+    grads = {0: summed(exchanged(early_parts[0])), 1: summed(late_terms)}
     out_half = early_parts[1] + lax.ppermute(early_parts[2], "tile", SWAP)
     grad_out = out_half[0] + send(out_half[1], shifted(count, 0, 1))
     grads[0], grad_out = lax.optimization_barrier((grads[0], grad_out))

time: 213 us -> 212 us (level)
  transfers between devices with their start and end apart: 37 -> 37, of which waited for: 12 -> 12; matrix products, arithmetic and copies ran while one was open for 9% -> 10% of each run, Pallas kernels for 19% -> 19%
where the time goes in v5:
time: 212 us
  waiting for transfers between devices  81.1 us (38%)
  starting transfers between devices  49.2 us (23%)
  Pallas kernels  41.1 us (19%)
  other arithmetic  21.3 us (10%)
  between operations  14.9 us (7%)
  local copies, waits for them, and re-layouts  2.74 us (1%)
    ppermute x28, waiting for transfers between devices, send(): return lax.ppermute(x, 'tgt', moves)  43.3 us
    ppermute x28, starting transfers between devices, send(): return lax.ppermute(x, 'tgt', moves)  36.8 us
    all_to_all x2, waiting for transfers between devices, owners_cells(): return lax.all_to_all(x, 'tgt', split_axis=0, concat_axis=0, tiled=True)  36.1 us
    pallas_call x2, Pallas kernels, residual_of(): pl.pallas_call(functools.partial(residual_kernel, count, mixed), grid_spe...  21.2 us
    pallas_call x1, Pallas kernels, compact(): pl.pallas_call(functools.partial(compact_kernel, group, cap, extra, rows,...  16.8 us
    all_to_all x2, starting transfers between devices, owners_cells(): return lax.all_to_all(x, 'tgt', split_axis=0, concat_axis=0, tiled=True)  8.67 us
    select_n x2, other arithmetic, merged(): return jnp.where(row < received[0], other, own)  6.68 us
  transfers between devices with their start and end apart: 37, of which 12 were waited for; matrix products, arithmetic and copies ran while one was open for 10% of the time, Pallas kernels for 19%

profile of v5, /device:TPU:0, one launch (start us, length us, event | category | flops | bytes accessed | tf_op | source)
XLA Modules:
  0.0 211.6 jit_solution(8166675581699107492)
XLA Ops:
  8.6 2.4 %collective-permute-start.28 = (s32[1]{0:T(128)}, s32[1]{0:T(128)}, u32[]{:S(2)}, u32[]{:S(2)}) collective-permute-start(s32[1]{0:T(128)} %bitcast.28), channel_id=1, source_target_pairs={{0,17},{1,16},{16,1},{17,0},{2,19},{3,18},{18,3},{19,2},{4,21},{5,... | collective-permute-start | bytes 20 | tf_op jit(solution)/shard_map/ppermute | solution.py:417
  15.4 2.5 %collective-permute-done.29 = bf16[128,256]{1,0:T(8,128)(2,1)S(1)} collective-permute-done((bf16[128,256]{1,0:T(8,128)(2,1)}, bf16[128,256]{1,0:T(8,128)(2,1)S(1)}, u32[]{:S(2)}, u32[]{:S(2)}) %collective-permute-start.29) | collective-permute-done | bytes 65568 | tf_op jit(solution)/shard_map/ppermute | solution.py:136
  19.1 3.9 %collective-permute-start.33 = (bf16[2,128,256]{2,1,0:T(8,128)(2,1)S(1)}, bf16[2,128,256]{2,1,0:T(8,128)(2,1)S(1)}, u32[]{:S(2)}, u32[]{:S(2)}) collective-permute-start(bf16[2,128,256]{2,1,0:T(8,128)(2,1)S(1)} %pad_maximum_fusion.1), channel_id=1, source_target_pairs={{0,12},{2,14},{4,0},{6,2},{8,4},{10,6},{12,8},{14,10},{1,13},{3,15... | collective-permute-start | bytes 393224 | tf_op jit(solution)/shard_map/ppermute | solution.py:136
  24.0 2.6 %compare_select_fusion.6.plan_ref = s32[57]{0:T(128)S(1)} fusion(s32[57]{0:T(128)S(1)} %broadcast_add_fusion.2, s32[]{:T(128)S(6)} %add.205, s32[]{:T(128)} %bitcast.35, s32[]{:T(128)} %bitcast.34, s32[]{:T(128)} %bitcast.33, s32[]{:T(128)} %bitcast.32), kind=kLoop, calls=%fused_computation.43 | loop fusion | flops 570 | bytes 476 | tf_op jit(solution)/shard_map/jit(_where)/select_n | solution.py:100
  26.6 16.8 %compact.1 = (s32[3]{0:T(128)S(1)}, bf16[8,432,128]{2,1,0:T(8,128)(2,1)}, bf16[3456,128]{1,0:T(8,128)(2,1)}, bf16[3456,128]{1,0:T(8,128)(2,1)}, bf16[6912,512]{1...) custom-call(s32[57]{0:T(128)S(1)} %compare_select_fusion.6.plan_ref, ...), custom_call_target="tpu_custom_call" | custom-call | flops 4634705920 | bytes 31129600 | tf_op jit(solution)/shard_map/compact/pallas_call | solution.py:104
  43.5 161.2 %conditional.1 = (f32[128,128]{1,0:T(8,128)}, f32[128,512]{1,0:T(8,128)}) conditional(s32[]{:T(128)} %bitcast.36, (s32[13312]{0:T(1024)S(1)}, bf16[13312,128]{1,0:T(8,128)(2,1)S(1)}, bf16[128,256]{1,0:T(8,128)(2,1)}, bf16[256,512]{1,0:T(8,128)(2,1)}, bf16[13312,512]{1,0:T(8,128)(2,1)}, /*index=5*/s32[3]{0:T(128)S(1)}, f32[512]{0:T(512)S(1)}) %tuple.50, ...), branch_computations={%region_3.8_spmd, %region_8.9_spmd} | conditional | flops 12263240704 | bytes 233272640 | solution.py:440
  44.5 5.0 %all-to-all-start = ((bf16[8,432,128]{2,1,0:T(8,128)(2,1)}), bf16[8,432,128]{2,1,0:T(8,128)(2,1)S(1)}, u32[]{:S(2)}, u32[]{:S(2)}) async-start(bf16[8,432,128]{2,1,0:T(8,128)(2,1)} %get-tuple-element.51), calls=%async_computation | async-start | bytes 1769472 | tf_op jit(solution)/shard_map/cond/branch_1_fun/all_to_all | solution.py:323
  54.6 2.8 %broadcast_select_fusion.1 = bf16[3456,128]{1,0:T(8,128)(2,1)S(1)} fusion(bf16[3456,128]{1,0:T(8,128)(2,1)S(1)} %collective-permute-done, bf16[3456,128]{1,0:T(8,128)(2,1)} %get-tuple-element.54, pred[3456]{0:T(1024)(128)(4,1)S(1)} %iota_compare_fusion), kind=kLoop, calls=%fused_computation.6 | loop fusion | flops 442368 | bytes 2657664 | tf_op jit(solution)/shard_map/cond/branch_1_fun/jit(_where)/select_n | solution.py:316
  58.4 13.5 %all-to-all-done.cells_ref.refs_0_ = bf16[8,432,128]{2,1,0:T(8,128)(2,1)S(1)} async-done(((bf16[8,432,128]{2,1,0:T(8,128)(2,1)}), bf16[8,432,128]{2,1,0:T(8,128)(2,1)S(1)}, u32[]{:S(2)}, u32[]{:S(2)}) %all-to-all-start) | async-done | bytes 884768 | tf_op jit(solution)/shard_map/cond/branch_1_fun/all_to_all | solution.py:323
  71.9 3.6 %all-to-all-start.1 = ((bf16[8,432,128]{2,1,0:T(8,128)(2,1)}), bf16[8,432,128]{2,1,0:T(8,128)(2,1)S(1)}, u32[]{:S(2)}, u32[]{:S(2)}) async-start(bf16[8,432,128]{2,1,0:T(8,128)(2,1)} %bitcast.76), calls=%async_computation.1 | async-start | bytes 1769472 | tf_op jit(solution)/shard_map/cond/branch_1_fun/all_to_all | solution.py:323
  76.7 3.9 %dynamic-slice_select_fusion = bf16[1728,512]{1,0:T(8,128)(2,1)} fusion(bf16[6912,512]{1,0:T(8,128)(2,1)} %get-tuple-element.71.refs_4_, s32[]{:T(128)S(6)} %select_n.93, bf16[3456,512]{1,0:T(8,128)(2,1)} %collective-permute-done.1.refs_6_, s32[]{:T(128)S(6)} %select_n.92, pred[1728]{0:T(1024)(128)(4,1)S(1)} %add_compare_fusion), kind=kLoop, calls=%fused_computation.5 | loop fusion | flops 884736 | bytes 5310152 | tf_op jit(solution)/shard_map/cond/branch_1_fun/jit(_where)/select_n | solution.py:316
  82.6 3.3 %collective-permute-start.4 = (bf16[432,256]{1,0:T(8,128)(2,1)S(1)}, bf16[432,256]{1,0:T(8,128)(2,1)S(1)}, u32[]{:S(2)}, u32[]{:S(2)}) collective-permute-start(bf16[432,256]{1,0:T(8,128)(2,1)S(1)} %latent.2.refs_0_), channel_id=1, source_target_pairs={{0,12},{2,14},{4,0},{6,2},{8,4},{10,6},{12,8},{14,10},{1,13},{3,15... | collective-permute-start | bytes 663560 | tf_op jit(solution)/shard_map/cond/branch_1_fun/ppermute | solution.py:136
  87.7 22.5 %all-to-all-done.1.cells_ref.refs_1_ = bf16[8,432,128]{2,1,0:T(8,128)(2,1)S(1)} async-done(((bf16[8,432,128]{2,1,0:T(8,128)(2,1)}), bf16[8,432,128]{2,1,0:T(8,128)(2,1)S(1)}, u32[]{:S(2)}, u32[]{:S(2)}) %all-to-all-start.1) | async-done | bytes 884768 | tf_op jit(solution)/shard_map/cond/branch_1_fun/all_to_all | solution.py:323
  110.2 6.7 %collective-permute-done.3.refs_2_ = bf16[432,256]{1,0:T(8,128)(2,1)S(1)} collective-permute-done((bf16[432,256]{1,0:T(8,128)(2,1)S(1)}, bf16[432,256]{1,0:T(8,128)(2,1)S(1)}, u32[]{:S(2)}, u32[]{:S(2)}) %collective-permute-start.3) | collective-permute-done | bytes 221216 | tf_op jit(solution)/shard_map/cond/branch_1_fun/ppermute | solution.py:136
  122.4 9.9 %residual.2 = (bf16[432,256]{1,0:T(8,128)(2,1)}, bf16[432,256]{1,0:T(8,128)(2,1)}, bf16[432,256]{1,0:T(8,128)(2,1)}, bf16[432,256]{1,0:T(8,128)(2,1)}, f32[256,512]{1,0:T(8,128)}, /*index=5*/f32[256,512]{1,0:T(8,128)}) custom-call(s32[4]{0:T(128)} %broadcast_add_fusion.own_ref, s32[4]{0:T(128)} %copy-done.2, s32[2]{0:T(128)} %pad_add_fusion.part_ref, ...), custom_call_target="tpu_custom_call" | custom-call | flops 226492416 | bytes 1327104 | tf_op jit(solution)/shard_map/cond/branch_1_fun/residual/pallas_call | solution.py:233
  132.4 6.0 %collective-permute-done.7.refs_2_ = bf16[432,256]{1,0:T(8,128)(2,1)S(1)} collective-permute-done((bf16[432,256]{1,0:T(8,128)(2,1)S(1)}, bf16[432,256]{1,0:T(8,128)(2,1)S(1)}, u32[]{:S(2)}, u32[]{:S(2)}) %collective-permute-start.7) | collective-permute-done | bytes 221216 | tf_op jit(solution)/shard_map/cond/branch_1_fun/ppermute | solution.py:136
  139.8 7.1 %collective-permute-done.9.refs_5_ = bf16[1728,512]{1,0:T(8,128)(2,1)} collective-permute-done((bf16[1728,512]{1,0:T(8,128)(2,1)}, bf16[1728,512]{1,0:T(8,128)(2,1)}, u32[]{:S(2)}, u32[]{:S(2)}) %collective-permute-start.9) | collective-permute-done | bytes 1769504 | tf_op jit(solution)/shard_map/cond/branch_1_fun/ppermute | solution.py:136
  146.9 3.3 %collective-permute-start.10 = (bf16[432,256]{1,0:T(8,128)(2,1)}, bf16[432,256]{1,0:T(8,128)(2,1)}, u32[]{:S(2)}, u32[]{:S(2)}) collective-permute-start(bf16[432,256]{1,0:T(8,128)(2,1)} %get-tuple-element.95), channel_id=1, source_target_pairs={{0,12},{2,14},{4,0},{6,2},{8,4},{10,6},{12,8},{14,10},{1,13},{3,15... | collective-permute-start | bytes 663560 | tf_op jit(solution)/shard_map/cond/branch_1_fun/ppermute | solution.py:136
  150.8 11.3 %residual.3 = (bf16[432,256]{1,0:T(8,128)(2,1)}, bf16[432,256]{1,0:T(8,128)(2,1)}, bf16[432,256]{1,0:T(8,128)(2,1)}, bf16[432,256]{1,0:T(8,128)(2,1)}, f32[2,128,512]{2,1,0:T(8,128)}, /*index=5*/f32[2,128,512]{2,1,0:T(8,128)}) custom-call(s32[4]{0:T(128)} %broadcast_add_fusion.1.own_ref, s32[4]{0:T(128)} %copy-done.2, s32[2]{0:T(128)} %pad_add_fusion.part_ref, ...), custom_call_target="tpu_custom_call" | custom-call | flops 226492416 | bytes 1327104 | tf_op jit(solution)/shard_map/cond/branch_1_fun/residual/pallas_call | solution.py:233
  166.9 4.3 %collective-permute-done.13 = bf16[432,256]{1,0:T(8,128)(2,1)S(1)} collective-permute-done((bf16[432,256]{1,0:T(8,128)(2,1)}, bf16[432,256]{1,0:T(8,128)(2,1)S(1)}, u32[]{:S(2)}, u32[]{:S(2)}) %collective-permute-start.13) | collective-permute-done | bytes 221216 | tf_op jit(solution)/shard_map/cond/branch_1_fun/ppermute | solution.py:136
  171.2 11.4 %collective-permute-done.14 = bf16[432,256]{1,0:T(8,128)(2,1)S(1)} collective-permute-done((bf16[432,256]{1,0:T(8,128)(2,1)}, bf16[432,256]{1,0:T(8,128)(2,1)S(1)}, u32[]{:S(2)}, u32[]{:S(2)}) %collective-permute-start.14) | collective-permute-done | bytes 221216 | tf_op jit(solution)/shard_map/cond/branch_1_fun/ppermute | solution.py:136
  188.9 3.2 %collective-permute-start.25 = (f32[128,128]{1,0:T(8,128)S(1)}, f32[128,128]{1,0:T(8,128)S(1)}, u32[]{:S(2)}, u32[]{:S(2)}) collective-permute-start(f32[128,128]{1,0:T(8,128)S(1)} %get-tuple-element.175), channel_id=1, source_target_pairs={{0,14},{2,12},{4,2},{6,0},{8,6},{10,4},{12,10},{14,8},{1,15},{3,13... | collective-permute-start | bytes 196616 | tf_op jit(solution)/shard_map/cond/branch_1_fun/ppermute | solution.py:136
  195.1 3.8 %collective-permute-start.21 = (f32[128,128]{1,0:T(8,128)S(1)}, f32[128,128]{1,0:T(8,128)S(1)}, u32[]{:S(2)}, u32[]{:S(2)}) collective-permute-start(f32[128,128]{1,0:T(8,128)S(1)} %get-tuple-element.179), channel_id=1, source_target_pairs={{0,12},{2,14},{4,0},{6,2},{8,4},{10,6},{12,8},{14,10},{1,13},{3,15... | collective-permute-start | bytes 196616 | tf_op jit(solution)/shard_map/cond/branch_1_fun/ppermute | solution.py:136
  201.2 2.9 %collective-permute-done.20 = f32[128,128]{1,0:T(8,128)S(1)} collective-permute-done((f32[128,128]{1,0:T(8,128)S(1)}, f32[128,128]{1,0:T(8,128)S(1)}, u32[]{:S(2)}, u32[]{:S(2)}) %collective-permute-start.20) | collective-permute-done | bytes 65568 | tf_op jit(solution)/shard_map/cond/branch_1_fun/ppermute | solution.py:136
  (118 shorter events, 42.7 us)
Async XLA Ops:
  8.6 10.4 %collective-permute-start.28 = (s32[1]{0:T(128)}, s32[1]{0:T(128)}, u32[]{:S(2)}, u32[]{:S(2)}) collective-permute-start(s32[1]{0:T(128)} %bitcast.28), channel_id=1, source_target_pairs={{0,17},{1,16},{16,1},{17,0},{2,19},{3,18},{18,3},{19,2},{4,21},{5,... | collective-permute-start | bytes 20 | tf_op jit(solution)/shard_map/ppermute | solution.py:417
  17.9 25.5 %collective-permute-start.34 = (bf16[256,512]{1,0:T(8,128)(2,1)}, bf16[256,512]{1,0:T(8,128)(2,1)}, u32[]{:S(2)}, u32[]{:S(2)}) collective-permute-start(bf16[256,512]{1,0:T(8,128)(2,1)} %param.11), channel_id=1, source_target_pairs={{0,2},{2,0},{4,6},{6,4},{8,10},{10,8},{12,14},{14,12},{1,3},{3,1},... | collective-permute-start | bytes 786440 | tf_op jit(solution)/shard_map/ppermute | solution.py:136
  19.1 24.3 %collective-permute-start.33 = (bf16[2,128,256]{2,1,0:T(8,128)(2,1)S(1)}, bf16[2,128,256]{2,1,0:T(8,128)(2,1)S(1)}, u32[]{:S(2)}, u32[]{:S(2)}) collective-permute-start(bf16[2,128,256]{2,1,0:T(8,128)(2,1)S(1)} %pad_maximum_fusion.1), channel_id=1, source_target_pairs={{0,12},{2,14},{4,0},{6,2},{8,4},{10,6},{12,8},{14,10},{1,13},{3,15... | collective-permute-start | bytes 393224 | tf_op jit(solution)/shard_map/ppermute | solution.py:136
  23.0 20.4 %collective-permute-start.32 = (bf16[2,128,256]{2,1,0:T(8,128)(2,1)S(1)}, bf16[2,128,256]{2,1,0:T(8,128)(2,1)S(1)}, u32[]{:S(2)}, u32[]{:S(2)}) collective-permute-start(bf16[2,128,256]{2,1,0:T(8,128)(2,1)S(1)} %pad_maximum_fusion.1), channel_id=1, source_target_pairs={{0,8},{2,10},{4,12},{6,14},{8,0},{10,2},{12,4},{14,6},{1,9},{3,11}... | collective-permute-start | bytes 393224 | tf_op jit(solution)/shard_map/ppermute | solution.py:136
  23.0 20.4 %collective-permute-start.31 = (bf16[2,128,256]{2,1,0:T(8,128)(2,1)S(1)}, bf16[2,128,256]{2,1,0:T(8,128)(2,1)S(1)}, u32[]{:S(2)}, u32[]{:S(2)}) collective-permute-start(bf16[2,128,256]{2,1,0:T(8,128)(2,1)S(1)} %pad_maximum_fusion.1), channel_id=1, source_target_pairs={{0,4},{2,6},{4,8},{6,10},{8,12},{10,14},{12,0},{14,2},{1,5},{3,7},... | collective-permute-start | bytes 393224 | tf_op jit(solution)/shard_map/ppermute | solution.py:136
  43.8 32.9 %collective-permute-start.1 = (bf16[3456,512]{1,0:T(8,128)(2,1)}, bf16[3456,512]{1,0:T(8,128)(2,1)}, u32[]{:S(2)}, u32[]{:S(2)}) collective-permute-start(bf16[3456,512]{1,0:T(8,128)(2,1)} %get-tuple-element.60), channel_id=1, source_target_pairs={{0,1},{1,0},{2,3},{3,2},{4,5},{5,4},{6,7},{7,6},{8,9},{9,8},{10,11... | collective-permute-start | bytes 10616840 | tf_op jit(solution)/shard_map/cond/branch_1_fun/ppermute | solution.py:311
  43.9 10.7 %collective-permute-start = (bf16[3456,128]{1,0:T(8,128)(2,1)}, bf16[3456,128]{1,0:T(8,128)(2,1)S(1)}, u32[]{:S(2)}, u32[]{:S(2)}) collective-permute-start(bf16[3456,128]{1,0:T(8,128)(2,1)} %get-tuple-element.53), channel_id=1, source_target_pairs={{0,1},{1,0},{2,3},{3,2},{4,5},{5,4},{6,7},{7,6},{8,9},{9,8},{10,11... | collective-permute-start | bytes 2654216 | tf_op jit(solution)/shard_map/cond/branch_1_fun/ppermute | solution.py:310
  44.5 27.5 %all-to-all-start = ((bf16[8,432,128]{2,1,0:T(8,128)(2,1)}), bf16[8,432,128]{2,1,0:T(8,128)(2,1)S(1)}, u32[]{:S(2)}, u32[]{:S(2)}) async-start(bf16[8,432,128]{2,1,0:T(8,128)(2,1)} %get-tuple-element.51), calls=%async_computation | async-start | bytes 1769472 | tf_op jit(solution)/shard_map/cond/branch_1_fun/all_to_all | solution.py:323
  49.5 72.9 %collective-permute-start.5 = (bf16[1728,512]{1,0:T(8,128)(2,1)}, bf16[1728,512]{1,0:T(8,128)(2,1)}, u32[]{:S(2)}, u32[]{:S(2)}) collective-permute-start(bf16[1728,512]{1,0:T(8,128)(2,1)} %get-tuple-element.72), channel_id=1, source_target_pairs={{0,2},{2,0},{4,6},{6,4},{8,10},{10,8},{12,14},{14,12},{1,3},{3,1},... | collective-permute-start | bytes 5308424 | tf_op jit(solution)/shard_map/cond/branch_1_fun/ppermute | solution.py:136
  71.9 38.3 %all-to-all-start.1 = ((bf16[8,432,128]{2,1,0:T(8,128)(2,1)}), bf16[8,432,128]{2,1,0:T(8,128)(2,1)S(1)}, u32[]{:S(2)}, u32[]{:S(2)}) async-start(bf16[8,432,128]{2,1,0:T(8,128)(2,1)} %bitcast.76), calls=%async_computation.1 | async-start | bytes 1769472 | tf_op jit(solution)/shard_map/cond/branch_1_fun/all_to_all | solution.py:323
  80.6 66.3 %collective-permute-start.9 = (bf16[1728,512]{1,0:T(8,128)(2,1)}, bf16[1728,512]{1,0:T(8,128)(2,1)}, u32[]{:S(2)}, u32[]{:S(2)}) collective-permute-start(bf16[1728,512]{1,0:T(8,128)(2,1)} %dynamic-slice_select_fusion), channel_id=1, source_target_pairs={{0,2},{2,0},{4,6},{6,4},{8,10},{10,8},{12,14},{14,12},{1,3},{3,1},... | collective-permute-start | bytes 5308424 | tf_op jit(solution)/shard_map/cond/branch_1_fun/ppermute | solution.py:136
  82.6 27.6 %collective-permute-start.4 = (bf16[432,256]{1,0:T(8,128)(2,1)S(1)}, bf16[432,256]{1,0:T(8,128)(2,1)S(1)}, u32[]{:S(2)}, u32[]{:S(2)}) collective-permute-start(bf16[432,256]{1,0:T(8,128)(2,1)S(1)} %latent.2.refs_0_), channel_id=1, source_target_pairs={{0,12},{2,14},{4,0},{6,2},{8,4},{10,6},{12,8},{14,10},{1,13},{3,15... | collective-permute-start | bytes 663560 | tf_op jit(solution)/shard_map/cond/branch_1_fun/ppermute | solution.py:136
  85.9 31.0 %collective-permute-start.3 = (bf16[432,256]{1,0:T(8,128)(2,1)S(1)}, bf16[432,256]{1,0:T(8,128)(2,1)S(1)}, u32[]{:S(2)}, u32[]{:S(2)}) collective-permute-start(bf16[432,256]{1,0:T(8,128)(2,1)S(1)} %latent.2.refs_0_), channel_id=1, source_target_pairs={{0,8},{2,10},{4,12},{6,14},{8,0},{10,2},{12,4},{14,6},{1,9},{3,11}... | collective-permute-start | bytes 663560 | tf_op jit(solution)/shard_map/cond/branch_1_fun/ppermute | solution.py:136
  85.9 31.0 %collective-permute-start.2 = (bf16[432,256]{1,0:T(8,128)(2,1)S(1)}, bf16[432,256]{1,0:T(8,128)(2,1)}, u32[]{:S(2)}, u32[]{:S(2)}) collective-permute-start(bf16[432,256]{1,0:T(8,128)(2,1)S(1)} %latent.2.refs_0_), channel_id=1, source_target_pairs={{0,4},{2,6},{4,8},{6,10},{8,12},{10,14},{12,0},{14,2},{1,5},{3,7},... | collective-permute-start | bytes 663560 | tf_op jit(solution)/shard_map/cond/branch_1_fun/ppermute | solution.py:136
  118.1 14.2 %collective-permute-start.8 = (bf16[432,256]{1,0:T(8,128)(2,1)S(1)}, bf16[432,256]{1,0:T(8,128)(2,1)S(1)}, u32[]{:S(2)}, u32[]{:S(2)}) collective-permute-start(bf16[432,256]{1,0:T(8,128)(2,1)S(1)} %latent.3.refs_0_), channel_id=1, source_target_pairs={{0,12},{2,14},{4,0},{6,2},{8,4},{10,6},{12,8},{14,10},{1,13},{3,15... | collective-permute-start | bytes 663560 | tf_op jit(solution)/shard_map/cond/branch_1_fun/ppermute | solution.py:136
  118.2 20.2 %collective-permute-start.7 = (bf16[432,256]{1,0:T(8,128)(2,1)S(1)}, bf16[432,256]{1,0:T(8,128)(2,1)S(1)}, u32[]{:S(2)}, u32[]{:S(2)}) collective-permute-start(bf16[432,256]{1,0:T(8,128)(2,1)S(1)} %latent.3.refs_0_), channel_id=1, source_target_pairs={{0,8},{2,10},{4,12},{6,14},{8,0},{10,2},{12,4},{14,6},{1,9},{3,11}... | collective-permute-start | bytes 663560 | tf_op jit(solution)/shard_map/cond/branch_1_fun/ppermute | solution.py:136
  118.7 19.7 %collective-permute-start.6 = (bf16[432,256]{1,0:T(8,128)(2,1)S(1)}, bf16[432,256]{1,0:T(8,128)(2,1)S(1)}, u32[]{:S(2)}, u32[]{:S(2)}) collective-permute-start(bf16[432,256]{1,0:T(8,128)(2,1)S(1)} %latent.3.refs_0_), channel_id=1, source_target_pairs={{0,4},{2,6},{4,8},{6,10},{8,12},{10,14},{12,0},{14,2},{1,5},{3,7},... | collective-permute-start | bytes 663560 | tf_op jit(solution)/shard_map/cond/branch_1_fun/ppermute | solution.py:136
  138.4 23.6 %collective-permute-start.11 = (bf16[432,256]{1,0:T(8,128)(2,1)}, bf16[432,256]{1,0:T(8,128)(2,1)S(1)}, u32[]{:S(2)}, u32[]{:S(2)}) collective-permute-start(bf16[432,256]{1,0:T(8,128)(2,1)} %get-tuple-element.96), channel_id=1, source_target_pairs={{0,8},{2,10},{4,12},{6,14},{8,0},{10,2},{12,4},{14,6},{1,9},{3,11}... | collective-permute-start | bytes 663560 | tf_op jit(solution)/shard_map/cond/branch_1_fun/ppermute | solution.py:136
  139.8 22.2 %collective-permute-start.12 = (bf16[432,256]{1,0:T(8,128)(2,1)}, bf16[432,256]{1,0:T(8,128)(2,1)S(1)}, u32[]{:S(2)}, u32[]{:S(2)}) collective-permute-start(bf16[432,256]{1,0:T(8,128)(2,1)} %get-tuple-element.97), channel_id=1, source_target_pairs={{0,4},{2,6},{4,8},{6,10},{8,12},{10,14},{12,0},{14,2},{1,5},{3,7},... | collective-permute-start | bytes 663560 | tf_op jit(solution)/shard_map/cond/branch_1_fun/ppermute | solution.py:136
  146.9 15.1 %collective-permute-start.10 = (bf16[432,256]{1,0:T(8,128)(2,1)}, bf16[432,256]{1,0:T(8,128)(2,1)}, u32[]{:S(2)}, u32[]{:S(2)}) collective-permute-start(bf16[432,256]{1,0:T(8,128)(2,1)} %get-tuple-element.95), channel_id=1, source_target_pairs={{0,12},{2,14},{4,0},{6,2},{8,4},{10,6},{12,8},{14,10},{1,13},{3,15... | collective-permute-start | bytes 663560 | tf_op jit(solution)/shard_map/cond/branch_1_fun/ppermute | solution.py:136
  162.8 19.8 %collective-permute-start.14 = (bf16[432,256]{1,0:T(8,128)(2,1)}, bf16[432,256]{1,0:T(8,128)(2,1)S(1)}, u32[]{:S(2)}, u32[]{:S(2)}) collective-permute-start(bf16[432,256]{1,0:T(8,128)(2,1)} %get-tuple-element.104), channel_id=1, source_target_pairs={{0,8},{2,10},{4,12},{6,14},{8,0},{10,2},{12,4},{14,6},{1,9},{3,11}... | collective-permute-start | bytes 663560 | tf_op jit(solution)/shard_map/cond/branch_1_fun/ppermute | solution.py:136
  162.8 19.8 %collective-permute-start.15 = (bf16[432,256]{1,0:T(8,128)(2,1)}, bf16[432,256]{1,0:T(8,128)(2,1)S(1)}, u32[]{:S(2)}, u32[]{:S(2)}) collective-permute-start(bf16[432,256]{1,0:T(8,128)(2,1)} %get-tuple-element.105), channel_id=1, source_target_pairs={{0,4},{2,6},{4,8},{6,10},{8,12},{10,14},{12,0},{14,2},{1,5},{3,7},... | collective-permute-start | bytes 663560 | tf_op jit(solution)/shard_map/cond/branch_1_fun/ppermute | solution.py:136
  165.4 18.3 %collective-permute-start.17 = (f32[128,512]{1,0:T(8,128)S(1)}, f32[128,512]{1,0:T(8,128)S(1)}, u32[]{:S(2)}, u32[]{:S(2)}) collective-permute-start(f32[128,512]{1,0:T(8,128)S(1)} %slice_bitcast_fusion), channel_id=1, source_target_pairs={{0,2},{2,0},{4,6},{6,4},{8,10},{10,8},{12,14},{14,12},{1,3},{3,1},... | collective-permute-start | bytes 786440 | tf_op jit(solution)/shard_map/cond/branch_1_fun/ppermute | solution.py:136
  188.9 10.0 %collective-permute-start.25 = (f32[128,128]{1,0:T(8,128)S(1)}, f32[128,128]{1,0:T(8,128)S(1)}, u32[]{:S(2)}, u32[]{:S(2)}) collective-permute-start(f32[128,128]{1,0:T(8,128)S(1)} %get-tuple-element.175), channel_id=1, source_target_pairs={{0,14},{2,12},{4,2},{6,0},{8,6},{10,4},{12,10},{14,8},{1,15},{3,13... | collective-permute-start | bytes 196616 | tf_op jit(solution)/shard_map/cond/branch_1_fun/ppermute | solution.py:136
  (30 other events, 420.3 us)
